TPU v7x, 32 devices: a whole 2x2x4 slice. The times are simulated.
32 devices in a mesh: dp: 4 (over y, x), expert: 8 (over z, core).
Axes of the slice: x: 2, y: 2, z: 4, core: 2. Of those that a mesh axis runs over, the one named last changes fastest.
Arguments:
- hidden_in: bfloat16 [8192, 2048], P(('dp', 'expert')), may hold values from -6 to 6
- cotangent: bfloat16 [8192, 2048], P(('dp', 'expert')), may hold values from -6 to 6
- attention_gain: bfloat16 [2048], P(('dp', 'expert')), may hold values from 0.25 to 1.75
- query_gain: bfloat16 [2048], P(('dp', 'expert')), may hold values from 0.25 to 1.75
- key_gain: bfloat16 [2048], P(('dp', 'expert')), may hold values from 0.25 to 1.75
- mixture_gain: bfloat16 [2048], P(('dp', 'expert')), may hold values from 0.25 to 1.75
- query_weight: bfloat16 [2048, 2048], P(('dp', 'expert')), may hold values from -0.125 to 0.125
- key_weight: bfloat16 [2048, 2048], P(('dp', 'expert')), may hold values from -0.125 to 0.125
- value_weight: bfloat16 [2048, 2048], P(('dp', 'expert')), may hold values from -0.125 to 0.125
- output_weight: bfloat16 [2048, 2048], P(('dp', 'expert')), may hold values from -0.375 to 0.375
- router_weight: bfloat16 [2048, 16], P(('dp', 'expert')), may hold values from -0.0625 to 0.0625
- gate_weight: bfloat16 [16, 2048, 1024], P('expert', None, 'dp'), may hold values from -0.125 to 0.125
- up_weight: bfloat16 [16, 2048, 1024], P('expert', None, 'dp'), may hold values from -0.125 to 0.125
- down_weight: bfloat16 [16, 1024, 2048], P('expert', 'dp'), may hold values from -4 to 4
- routes: int32 [8192, 8], P(('dp', 'expert')), may hold values from 0 to 15, all different within a row; in each aligned block of 256 rows (0 to 255, 256 to 511, ...) at most 160 rows name the same one
- segments: int32 [32, 256], P(('dp', 'expert')), may hold values from 0 to 3, never falling along the last dimension, each value on 1 to 128 neighbouring positions
Outputs:
- layer_out: bfloat16 [8192, 2048], P(('dp', 'expert'))
- hidden_grad: float32 [8192, 2048], P(('dp', 'expert'))
- attention_gain_grad: float32 [2048], P(('dp', 'expert'))
- query_gain_grad: float32 [2048], P(('dp', 'expert'))
- key_gain_grad: float32 [2048], P(('dp', 'expert'))
- mixture_gain_grad: float32 [2048], P(('dp', 'expert'))
- query_weight_grad: float32 [2048, 2048], P(('dp', 'expert'))
- key_weight_grad: float32 [2048, 2048], P(('dp', 'expert'))
- value_weight_grad: float32 [2048, 2048], P(('dp', 'expert'))
- output_weight_grad: float32 [2048, 2048], P(('dp', 'expert'))
- router_weight_grad: float32 [2048, 16], P(('dp', 'expert'))
- gate_weight_grad: float32 [16, 2048, 1024], P('expert', None, 'dp')
- up_weight_grad: float32 [16, 2048, 1024], P('expert', None, 'dp')
- down_weight_grad: float32 [16, 1024, 2048], P('expert', 'dp')
Inputs may be any that keep to these rules, and one draw needn't show every extreme that they name: `routes`: A token's 8 experts differ. Within the rows of one device no expert is named more than 160 times, and in every draw some expert is named exactly 160 times by the rows of some device. `segments`: along each sequence the segment numbers never fall.
All inputs are finite; a program needn't handle non-finite values.
Results may differ from a plain program's by a relative error of at most 0.019.
Values may be sent and summed in bfloat16 or wider, within the bound.
No kernel may reach another device: no remote copies, remote signals or barrier semaphores. Data moves between devices by JAX's collectives and lax.ppermute only.
A program may use at most 320 MiB of HBM per device.

v0:
```python
import jax
import jax.numpy as jnp
from jax import lax
from jax.sharding import PartitionSpec as P

HD = 128


epsilon = 1e-05
rope_base = 10000.0
masked_score = -1e30


def norm_scale(values):
    return lax.rsqrt(jnp.mean(values * values, axis=-1, keepdims=True) + epsilon)


def norm_back(upstream, unit, scale):
    return scale * (upstream - unit * jnp.mean(upstream * unit, axis=-1, keepdims=True))


def rotary_tables(segments, head_size):
    length = segments.shape[-1]
    order = jnp.arange(length, dtype=jnp.int32)
    starts = jnp.sum((segments[..., None, :] < segments[..., :, None]).astype(jnp.int32), axis=-1)
    position = (order - starts).astype(jnp.float32)
    frequency = rope_base ** (-2.0 * jnp.arange(head_size // 2, dtype=jnp.float32) / head_size)
    angle = position[..., None] * frequency
    return (jnp.cos(angle), jnp.sin(angle))


def rotate(values, cosine, sine):
    half = values.shape[-1] // 2
    first = values[..., :half]
    second = values[..., half:]
    return jnp.concatenate(
        [first * cosine - second * sine, second * cosine + first * sine], axis=-1
    )


def rotate_back(upstream, cosine, sine):
    half = upstream.shape[-1] // 2
    first = upstream[..., :half]
    second = upstream[..., half:]
    return jnp.concatenate(
        [first * cosine + second * sine, second * cosine - first * sine], axis=-1
    )


def block_scores(query_rows, key_heads, allowed_rows, score_scale):
    scores = (
        jnp.einsum("thd,shd->hts", query_rows, key_heads, preferred_element_type=jnp.float32)
        * score_scale
    )
    return jnp.where(allowed_rows[None], scores, masked_score)


def attend_block(query_rows, key_heads, value_heads, allowed_rows, score_scale):
    scores = block_scores(query_rows, key_heads, allowed_rows, score_scale)
    peak = jnp.max(scores, axis=-1, keepdims=True)
    spread = jnp.exp(scores - peak)
    total = jnp.sum(spread, axis=-1, keepdims=True)
    weights = (spread / total).astype(jnp.bfloat16)
    context = jnp.einsum("hts,shd->thd", weights, value_heads, preferred_element_type=jnp.float32)
    return (context, peak + jnp.log(total))


def attend_back(
    query_rows, key_heads, value_heads, allowed_rows, log_total, upstream_rows, score_scale
):
    scores = block_scores(query_rows, key_heads, allowed_rows, score_scale)
    chances = jnp.exp(scores - log_total)
    chance_upstream = jnp.einsum(
        "thd,shd->hts", upstream_rows, value_heads, preferred_element_type=jnp.float32
    )
    value_term = jnp.einsum(
        "hts,thd->shd",
        chances.astype(jnp.bfloat16),
        upstream_rows,
        preferred_element_type=jnp.float32,
    )
    score_upstream = (
        chances * (chance_upstream - jnp.sum(chances * chance_upstream, axis=-1, keepdims=True))
    ).astype(jnp.bfloat16)
    query_term = (
        jnp.einsum("hts,shd->thd", score_upstream, key_heads, preferred_element_type=jnp.float32)
        * score_scale
    )
    key_term = (
        jnp.einsum("hts,thd->shd", score_upstream, query_rows, preferred_element_type=jnp.float32)
        * score_scale
    )
    return (query_term, key_term, value_term)


def swiglu_back(hidden_upstream, gate_pre, up_pre):
    sigmoid = jax.nn.sigmoid(gate_pre)
    up_upstream = (hidden_upstream * gate_pre * sigmoid).astype(jnp.bfloat16)
    gate_upstream = (
        hidden_upstream * up_pre * sigmoid * (1.0 + gate_pre * (1.0 - sigmoid))
    ).astype(jnp.bfloat16)
    return (gate_upstream, up_upstream)


def on_device(
    hidden_in,
    cotangent,
    attention_gain,
    query_gain,
    key_gain,
    mixture_gain,
    query_weight,
    key_weight,
    value_weight,
    output_weight,
    router_weight,
    gate_weight,
    up_weight,
    down_weight,
    routes,
    segments,
):
    gathered = (
        lax.all_gather(attention_gain, ("dp", "expert"), axis=0, tiled=True),
        lax.all_gather(query_gain, ("dp", "expert"), axis=0, tiled=True),
        lax.all_gather(key_gain, ("dp", "expert"), axis=0, tiled=True),
        lax.all_gather(mixture_gain, ("dp", "expert"), axis=0, tiled=True),
        lax.all_gather(query_weight, ("dp", "expert"), axis=0, tiled=True),
        lax.all_gather(key_weight, ("dp", "expert"), axis=0, tiled=True),
        lax.all_gather(value_weight, ("dp", "expert"), axis=0, tiled=True),
        lax.all_gather(output_weight, ("dp", "expert"), axis=0, tiled=True),
        lax.all_gather(router_weight, ("dp", "expert"), axis=0, tiled=True),
    )
    (
        attention_scale_all,
        query_scale_all,
        key_scale_all,
        mixture_scale_all,
        query_all,
        key_all,
        value_all,
        output_all,
        router_all,
    ) = gathered
    attention_gain_full = attention_scale_all.astype(jnp.float32)
    query_gain_full = query_scale_all.astype(jnp.float32)
    key_gain_full = key_scale_all.astype(jnp.float32)
    mixture_gain_full = mixture_scale_all.astype(jnp.float32)
    tokens = hidden_in.shape[0]
    width = hidden_in.shape[1]
    heads = width // HD
    score_scale = HD ** (-0.5)
    top = routes.shape[1]
    exp_dev = gate_weight.shape[0]
    owners = lax.axis_size("expert")
    experts = exp_dev * owners
    cap = max(2, tokens * top * 5 // (experts * 4))
    slots = experts * cap
    residual = hidden_in.astype(jnp.float32)
    scale_one = norm_scale(residual)
    unit_one = residual * scale_one
    normed = (unit_one * attention_gain_full).astype(jnp.bfloat16)
    query_raw = jnp.dot(normed, query_all, preferred_element_type=jnp.float32)
    key_raw = jnp.dot(normed, key_all, preferred_element_type=jnp.float32)
    value_heads = (
        jnp.dot(normed, value_all, preferred_element_type=jnp.float32)
        .astype(jnp.bfloat16)
        .reshape(tokens, heads, HD)
    )
    query_scale = norm_scale(query_raw)
    query_unit = query_raw * query_scale
    key_scale = norm_scale(key_raw)
    key_unit = key_raw * key_scale
    cosine, sine = rotary_tables(segments[0], HD)
    cosine = cosine[:, None, :]
    sine = sine[:, None, :]
    query_heads = rotate(
        (query_unit * query_gain_full).reshape(tokens, heads, HD), cosine, sine
    ).astype(jnp.bfloat16)
    key_heads = rotate((key_unit * key_gain_full).reshape(tokens, heads, HD), cosine, sine).astype(
        jnp.bfloat16
    )
    document = segments[0]
    order = jnp.arange(tokens, dtype=jnp.int32)
    allowed = (document[:, None] == document[None, :]) & (order[:, None] >= order[None, :])
    part, log_total = attend_block(query_heads, key_heads, value_heads, allowed, score_scale)
    context = part.reshape(tokens, width).astype(jnp.bfloat16)
    middle = residual + jnp.dot(context, output_all, preferred_element_type=jnp.float32)
    scale_two = norm_scale(middle)
    unit_two = middle * scale_two
    mixed_in = (unit_two * mixture_gain_full).astype(jnp.bfloat16)
    router_probs = jax.nn.softmax(
        jnp.dot(mixed_in, router_all, preferred_element_type=jnp.float32), axis=-1
    )
    picks = (routes[:, :, None] == jnp.arange(experts, dtype=jnp.int32)[None, None, :]).astype(
        jnp.float32
    )
    gates = jnp.sum(picks * router_probs[:, None, :], axis=-1)
    flat = routes.reshape(-1)
    hits = (flat[:, None] == jnp.arange(experts, dtype=jnp.int32)[None, :]).astype(jnp.int32)
    ranks = jnp.sum((jnp.cumsum(hits, axis=0) - 1) * hits, axis=-1)
    dest = (flat // exp_dev * cap + ranks) * exp_dev + flat % exp_dev
    owner = (
        jnp.full((slots,), -1, jnp.int32).at[dest].set(jnp.arange(flat.shape[0], dtype=jnp.int32))
    )
    filled = owner >= 0
    pick = jnp.where(filled, owner, 0)
    token_of = pick // top
    outgoing = jnp.where(filled[:, None], mixed_in[token_of], jnp.zeros((), jnp.bfloat16)).reshape(
        owners, cap, exp_dev, width
    )
    rows_local = lax.all_to_all(
        outgoing, "expert", split_axis=0, concat_axis=1, tiled=True
    ).reshape(owners * cap, exp_dev, width)
    row_count = rows_local.shape[0]
    gate_full, up_full, down_full = (
        lax.all_gather(gate_weight, "dp", axis=2, tiled=True),
        lax.all_gather(up_weight, "dp", axis=2, tiled=True),
        lax.all_gather(down_weight, "dp", axis=1, tiled=True),
    )
    gate_pre = jnp.einsum("red,edf->ref", rows_local, gate_full, preferred_element_type=jnp.float32)
    up_pre = jnp.einsum("red,edf->ref", rows_local, up_full, preferred_element_type=jnp.float32)
    hidden = (jax.nn.silu(gate_pre) * up_pre).astype(jnp.bfloat16)
    expert_out = jnp.einsum("ref,efd->red", hidden, down_full, preferred_element_type=jnp.float32)
    returning = expert_out.astype(jnp.bfloat16).reshape(owners, cap, exp_dev, width)
    returned = lax.all_to_all(returning, "expert", split_axis=0, concat_axis=0, tiled=True).reshape(
        slots, width
    )
    routed_out = returned[dest].reshape(tokens, top, width)
    mixture = jnp.einsum("tk,tkd->td", gates, routed_out.astype(jnp.float32))
    layer_out = (middle + mixture).astype(jnp.bfloat16)
    upstream = cotangent.astype(jnp.float32)
    gate_upstream = jnp.einsum(
        "tkd,td->tk", routed_out, cotangent, preferred_element_type=jnp.float32
    )
    out_upstream = (
        (gates[:, :, None] * upstream[:, None, :]).astype(jnp.bfloat16).reshape(tokens * top, width)
    )
    outgoing_grad = jnp.where(
        filled[:, None], out_upstream[pick], jnp.zeros((), jnp.bfloat16)
    ).reshape(owners, cap, exp_dev, width)
    cot_local = lax.all_to_all(
        outgoing_grad, "expert", split_axis=0, concat_axis=1, tiled=True
    ).reshape(row_count, exp_dev, width)
    hidden_upstream = jnp.einsum(
        "red,efd->ref", cot_local, down_full, preferred_element_type=jnp.float32
    )
    down_term = jnp.einsum("ref,red->efd", hidden, cot_local, preferred_element_type=jnp.float32)
    gate_back, up_back = swiglu_back(hidden_upstream, gate_pre, up_pre)
    gate_term = jnp.einsum(
        "red,ref->edf", rows_local, gate_back, preferred_element_type=jnp.float32
    )
    up_term = jnp.einsum("red,ref->edf", rows_local, up_back, preferred_element_type=jnp.float32)
    rows_grad = jnp.einsum("ref,edf->red", gate_back, gate_full, preferred_element_type=jnp.float32)
    rows_grad = rows_grad + jnp.einsum(
        "ref,edf->red", up_back, up_full, preferred_element_type=jnp.float32
    )
    gate_grad, up_grad, down_grad = (
        lax.psum_scatter(
            gate_term.astype(jnp.bfloat16), "dp", scatter_dimension=2, tiled=True
        ).astype(jnp.float32),
        lax.psum_scatter(
            up_term.astype(jnp.bfloat16), "dp", scatter_dimension=2, tiled=True
        ).astype(jnp.float32),
        lax.psum_scatter(
            down_term.astype(jnp.bfloat16), "dp", scatter_dimension=1, tiled=True
        ).astype(jnp.float32),
    )
    sending_grad = rows_grad.astype(jnp.bfloat16).reshape(owners, cap, exp_dev, width)
    returned_grad = lax.all_to_all(
        sending_grad, "expert", split_axis=0, concat_axis=0, tiled=True
    ).reshape(slots, width)
    copies_grad = jnp.sum(
        returned_grad[dest].reshape(tokens, top, width), axis=1, dtype=jnp.float32
    )
    prob_upstream = jnp.einsum("tk,tke->te", gate_upstream, picks)
    logit_upstream = (
        router_probs
        * (prob_upstream - jnp.sum(router_probs * prob_upstream, axis=-1, keepdims=True))
    ).astype(jnp.bfloat16)
    mixed_upstream = copies_grad + jnp.einsum(
        "te,de->td", logit_upstream, router_all, preferred_element_type=jnp.float32
    )
    mixture_gain_grad = jnp.sum(mixed_upstream * unit_two, axis=0)
    middle_grad = upstream + norm_back(mixed_upstream * mixture_gain_full, unit_two, scale_two)
    branch_upstream = middle_grad.astype(jnp.bfloat16)
    context_upstream = (
        jnp.einsum("td,cd->tc", branch_upstream, output_all, preferred_element_type=jnp.float32)
        .astype(jnp.bfloat16)
        .reshape(tokens, heads, HD)
    )
    query_term, key_term, value_term = attend_back(
        query_heads, key_heads, value_heads, allowed, log_total, context_upstream, score_scale
    )
    value_upstream = value_term.astype(jnp.bfloat16).reshape(tokens, width)
    query_norm_grad = rotate_back(query_term, cosine, sine).reshape(tokens, width)
    key_norm_grad = rotate_back(key_term, cosine, sine).reshape(tokens, width)
    query_gain_grad = jnp.sum(query_norm_grad * query_unit, axis=0)
    key_gain_grad = jnp.sum(key_norm_grad * key_unit, axis=0)
    query_upstream = norm_back(query_norm_grad * query_gain_full, query_unit, query_scale).astype(
        jnp.bfloat16
    )
    key_upstream = norm_back(key_norm_grad * key_gain_full, key_unit, key_scale).astype(
        jnp.bfloat16
    )
    normed_upstream = jnp.einsum(
        "td,cd->tc", query_upstream, query_all, preferred_element_type=jnp.float32
    )
    normed_upstream = normed_upstream + jnp.einsum(
        "td,cd->tc", key_upstream, key_all, preferred_element_type=jnp.float32
    )
    normed_upstream = normed_upstream + jnp.einsum(
        "td,cd->tc", value_upstream, value_all, preferred_element_type=jnp.float32
    )
    attention_gain_grad = jnp.sum(normed_upstream * unit_one, axis=0)
    hidden_grad = middle_grad + norm_back(
        normed_upstream * attention_gain_full, unit_one, scale_one
    )
    query_grad = jnp.einsum("tc,td->cd", normed, query_upstream, preferred_element_type=jnp.float32)
    key_grad = jnp.einsum("tc,td->cd", normed, key_upstream, preferred_element_type=jnp.float32)
    value_grad = jnp.einsum("tc,td->cd", normed, value_upstream, preferred_element_type=jnp.float32)
    output_grad = jnp.einsum(
        "tc,td->cd", context, branch_upstream, preferred_element_type=jnp.float32
    )
    router_grad = jnp.einsum(
        "td,te->de", mixed_in, logit_upstream, preferred_element_type=jnp.float32
    )
    sums = (
        lax.psum_scatter(query_grad, ("dp", "expert"), scatter_dimension=0, tiled=True),
        lax.psum_scatter(key_grad, ("dp", "expert"), scatter_dimension=0, tiled=True),
        lax.psum_scatter(value_grad, ("dp", "expert"), scatter_dimension=0, tiled=True),
        lax.psum_scatter(output_grad, ("dp", "expert"), scatter_dimension=0, tiled=True),
        lax.psum_scatter(router_grad, ("dp", "expert"), scatter_dimension=0, tiled=True),
        lax.psum_scatter(attention_gain_grad, ("dp", "expert"), scatter_dimension=0, tiled=True),
        lax.psum_scatter(query_gain_grad, ("dp", "expert"), scatter_dimension=0, tiled=True),
        lax.psum_scatter(key_gain_grad, ("dp", "expert"), scatter_dimension=0, tiled=True),
        lax.psum_scatter(mixture_gain_grad, ("dp", "expert"), scatter_dimension=0, tiled=True),
    )
    weight_sums = (sums[0], sums[1], sums[2], sums[3], sums[4])
    gain_parts = (sums[5], sums[6], sums[7], sums[8])
    return (
        layer_out,
        hidden_grad,
        gain_parts[0],
        gain_parts[1],
        gain_parts[2],
        gain_parts[3],
        weight_sums[0],
        weight_sums[1],
        weight_sums[2],
        weight_sums[3],
        weight_sums[4],
        gate_grad,
        up_grad,
        down_grad,
    )


def solution(mesh):
    return jax.shard_map(
        on_device,
        mesh=mesh,
        in_specs=(
            P(("dp", "expert"), None),
            P(("dp", "expert"), None),
            P(("dp", "expert")),
            P(("dp", "expert")),
            P(("dp", "expert")),
            P(("dp", "expert")),
            P(("dp", "expert"), None),
            P(("dp", "expert"), None),
            P(("dp", "expert"), None),
            P(("dp", "expert"), None),
            P(("dp", "expert"), None),
            P("expert", None, "dp"),
            P("expert", None, "dp"),
            P("expert", "dp", None),
            P(("dp", "expert"), None),
            P(("dp", "expert"), None),
        ),
        out_specs=(
            P(("dp", "expert"), None),
            P(("dp", "expert"), None),
            P(("dp", "expert")),
            P(("dp", "expert")),
            P(("dp", "expert")),
            P(("dp", "expert")),
            P(("dp", "expert"), None),
            P(("dp", "expert"), None),
            P(("dp", "expert"), None),
            P(("dp", "expert"), None),
            P(("dp", "expert"), None),
            P("expert", None, "dp"),
            P("expert", None, "dp"),
            P("expert", "dp", None),
        ),
        check_vma=False,
    )
```

profile of v0, /device:TPU:0, one launch (start us, length us, event | category | flops | bytes accessed | tf_op | source)
XLA Modules:
  0.0 2521.6 jit_solution(1490292043529680212)
XLA Ops:
  12.2 42.8 %all-reduce.9 = (bf16[2048]{0:T(1024)(128)(2,1)S(1)}, bf16[2048]{0:T(1024)(128)(2,1)S(1)}, bf16[2048]{0:T(1024)(128)(2,1)S(1)}, bf16[2048]{0:T(1024)(128)(2,1)S(1)}) all-reduce(bf16[2048]{0:T(1024)(128)(2,1)S(1)} %dynamic-update-slice, bf16[2048]{0:T(1024)(128)(2,1)S(1)} %dynamic-update-slice.2, ...), channel_id=1, replica_groups=mesh['dp'=4,'expert'=8] {'dp','expert'}, use_global_device_ids=true, to_apply=%add | all-reduce | flops 8192 | bytes 32768
  71.8 19.9 all-gather.13.cloned.1.call-done
  99.3 71.2 %all-gather.11.cloned.1.call-done = bf16[2048,2048]{1,0:T(8,128)(2,1)} async-done(((bf16[64,2048]{1,0:T(8,128)(2,1)}), bf16[2048,2048]{1,0:T(8,128)(2,1)}) %all-gather.11.cloned.1.call-update) | async-done | bytes 8388624 | tf_op jit(solution)/shard_map/all_gather | solution.py:128
  186.8 62.7 %all-gather.9.cloned.1.call-done = bf16[2048,2048]{1,0:T(8,128)(2,1)} async-done(((bf16[64,2048]{1,0:T(8,128)(2,1)}), bf16[2048,2048]{1,0:T(8,128)(2,1)}) %all-gather.9.cloned.1.call-update) | async-done | bytes 8388624 | tf_op jit(solution)/shard_map/all_gather | solution.py:130
  257.5 70.9 %all-gather.15.cloned.1.call-done = bf16[2048,2048]{1,0:T(8,128)(2,1)} async-done(((bf16[64,2048]{1,0:T(8,128)(2,1)}), bf16[2048,2048]{1,0:T(8,128)(2,1)}) %all-gather.15.cloned.1.call-update) | async-done | bytes 8388624 | tf_op jit(solution)/shard_map/all_gather | solution.py:131
  346.6 17.3 gather.17
  384.4 227.5 %all-to-all-done = bf16[8,160,2,2048]{3,1,2,0:T(8,128)(2,1)} async-done(((bf16[8,160,2,2048]{3,1,2,0:T(8,128)(2,1)}), bf16[8,160,2,2048]{3,1,2,0:T(8,128)(2,1)}, u32[]{:S(2)}, u32[]{:S(2)}) %all-to-all-start) | async-done | bytes 10485792 | tf_op jit(solution)/shard_map/all_to_all | solution.py:212
  622.1 18.6 fusion.78
  640.7 21.3 fusion.6
  662.0 18.1 convolution_convert_fusion
  695.5 258.4 %all-gather = bf16[32,64,16]{1,2,0:T(8,128)(2,1)S(1)} all-gather(bf16[1,64,16]{1,2,0:T(8,128)(2,1)S(1)} %bitcast.213), channel_id=1, replica_groups=mesh['dp'=4,'expert'=8] {'dp','expert'}, dimensions={0}, use_global_device_ids=true | all-gather | bytes 67584 | tf_op jit(solution)/shard_map/all_gather | solution.py:132
  956.2 20.3 copy.139
  976.6 16.0 reshape.422
  992.6 21.7 gather_fusion.1
  1027.8 24.6 gather_fusion.2
  1052.4 17.3 gather.20
  1090.8 238.0 %all-to-all-done.2 = bf16[8,160,2,2048]{3,1,2,0:T(8,128)(2,1)} async-done(((bf16[8,160,2,2048]{3,1,2,0:T(8,128)(2,1)}), bf16[8,160,2,2048]{3,1,2,0:T(8,128)(2,1)}, u32[]{:S(2)}, u32[]{:S(2)}) %all-to-all-start.2) | async-done | bytes 10485792 | tf_op jit(solution)/shard_map/all_to_all | solution.py:242
  1338.8 17.4 convolution_convert_fusion.1
  1356.3 24.4 fusion.5
  1380.8 17.8 convolution_convert_fusion.3
  1398.6 19.4 fusion.79
  1418.0 20.6 add_convert_fusion
  1453.9 17.9 convolution_convert_fusion.2
  1479.9 202.8 %all-to-all-done.3 = bf16[8,160,2,2048]{3,1,2,0:T(8,128)(2,1)} async-done(((bf16[8,160,2,2048]{3,1,2,0:T(8,128)(2,1)}), bf16[8,160,2,2048]{3,1,2,0:T(8,128)(2,1)}, u32[]{:S(2)}, u32[]{:S(2)}) %all-to-all-start.3) | async-done | bytes 10485792 | tf_op jit(solution)/shard_map/all_to_all | solution.py:270
  1682.7 20.2 copy.144
  1702.9 16.0 reshape.426
  1718.9 22.1 gather_fusion.3
  1857.1 39.5 %all-reduce.8 = (f32[2048]{0:T(1024)S(1)}, f32[2048]{0:T(1024)S(1)}, f32[2048]{0:T(1024)S(1)}, f32[2048]{0:T(1024)S(1)}) all-reduce(f32[2048]{0:T(1024)S(1)} %get-tuple-element.20, f32[2048]{0:T(1024)S(1)} %get-tuple-element.18, f32[2048]{0:T(1024)S(1)} %get-tuple-element.16, ...), channel_id=2, replica_groups=mesh['dp'=4,'expert'=8] {'dp','expert'}, use_global_device_ids=true, to_apply=%region_22.23.clone | all-reduce | flops 8192 | bytes 65536
  1902.5 50.9 %reduce-scatter.17.cloned.1.call-done = f32[64,2048]{1,0:T(8,128)} async-done(((f32[2048,2048]{1,0:T(8,128)}), f32[64,2048]{1,0:T(8,128)}) %reduce-scatter.17.cloned.1.call-update) | async-done | bytes 524304 | tf_op jit(solution)/shard_map/reduce_scatter | solution.py:332
  1953.4 187.2 %reduce-scatter.15.cloned.1.call-done = f32[64,2048]{1,0:T(8,128)} async-done(((f32[2048,2048]{1,0:T(8,128)}), f32[64,2048]{1,0:T(8,128)}) %reduce-scatter.15.cloned.1.call-update) | async-done | bytes 524304 | tf_op jit(solution)/shard_map/reduce_scatter | solution.py:331
  2140.6 187.1 %reduce-scatter.13.cloned.1.call-done = f32[64,2048]{1,0:T(8,128)} async-done(((f32[2048,2048]{1,0:T(8,128)}), f32[64,2048]{1,0:T(8,128)}) %reduce-scatter.13.cloned.1.call-update) | async-done | bytes 524304 | tf_op jit(solution)/shard_map/reduce_scatter | solution.py:330
  2327.7 187.1 %reduce-scatter.11.cloned.1.call-done = f32[64,2048]{1,0:T(8,128)} async-done(((f32[2048,2048]{1,0:T(8,128)}), f32[64,2048]{1,0:T(8,128)}) %reduce-scatter.11.cloned.1.call-update) | async-done | bytes 524304 | tf_op jit(solution)/shard_map/reduce_scatter | solution.py:329
  (325 shorter events, 309.1 us)
Async XLA Ops:
  7.2 84.4 %all-gather.13.cloned.1.call-start = ((), (), s32[]{:S(2)}) async-start(), calls=%async_computation.14 | async-start | bytes 8650752 | tf_op jit(solution)/shard_map/all_gather | solution.py:129
  8.0 162.6 %all-gather.11.cloned.1.call-start = ((), (), s32[]{:S(2)}) async-start(), calls=%async_computation.13 | async-start | bytes 8650752 | tf_op jit(solution)/shard_map/all_gather | solution.py:128
  8.7 240.8 %all-gather.9.cloned.1.call-start = ((), (), s32[]{:S(2)}) async-start(), calls=%async_computation.12 | async-start | bytes 8650752 | tf_op jit(solution)/shard_map/all_gather | solution.py:130
  9.5 319.0 %all-gather.15.cloned.1.call-start = ((), (), s32[]{:S(2)}) async-start(), calls=%async_computation.15 | async-start | bytes 8650752 | tf_op jit(solution)/shard_map/all_gather | solution.py:131
  10.0 60.7 %copy-start.3 = (bf16[256,2048]{1,0:T(8,128)(2,1)S(1)}, bf16[256,2048]{1,0:T(8,128)(2,1)}, u32[]{:S(2)}) copy-start(bf16[256,2048]{1,0:T(8,128)(2,1)} %param.16) | copy-start | bytes 3145732
  10.1 612.0 %all-gather.17.cloned.1.call-start = ((), (), s32[]{:S(2)}) async-start(), calls=%async_computation.16 | async-start | bytes 10485760 | tf_op jit(solution)/shard_map/all_gather | solution.py:217
  54.9 194.6 %copy-start.40 = (f32[2048]{0:T(1024)}, f32[2048]{0:T(1024)S(1)}, u32[]{:S(2)}) copy-start(f32[2048]{0:T(1024)S(1)} %convert_element_type.138) | copy-start | bytes 24580
  55.0 121.4 %copy-start.44 = (f32[2048]{0:T(1024)}, f32[2048]{0:T(1024)S(1)}, u32[]{:S(2)}) copy-start(f32[2048]{0:T(1024)S(1)} %convert_element_type.141) | copy-start | bytes 24580
  55.0 279.3 %copy-start.48 = (f32[2048]{0:T(1024)}, f32[2048]{0:T(1024)S(1)}, u32[]{:S(2)}) copy-start(f32[2048]{0:T(1024)S(1)} %convert_element_type.149) | copy-start | bytes 24580
  70.0 293.9 %copy-start.54 = (pred[8,160,2]{1,2,0:T(4,128)(4,1)}, pred[8,160,2]{1,2,0:T(4,128)(4,1)S(1)}, u32[]{:S(2)}) copy-start(pred[8,160,2]{1,2,0:T(4,128)(4,1)S(1)} %copy.135) | copy-start | bytes 7684
  71.1 178.5 %copy-start.58 = (f32[256]{0:T(256)}, f32[256]{0:T(256)S(1)}, u32[]{:S(2)}) copy-start(f32[256]{0:T(256)S(1)} %add_rsqrt_fusion.3) | copy-start | bytes 3076
  71.8 107.7 %copy-start.33 = (f32[256,64]{1,0:T(8,128)}, f32[256,64]{1,0:T(8,128)S(1)}, u32[]{:S(2)}) copy-start(f32[256,64]{1,0:T(8,128)S(1)} %get-tuple-element.54) | copy-start | bytes 196612
  71.8 107.7 %copy-start.35 = (f32[256,64]{1,0:T(8,128)}, f32[256,64]{1,0:T(8,128)S(1)}, u32[]{:S(2)}) copy-start(f32[256,64]{1,0:T(8,128)S(1)} %get-tuple-element.55) | copy-start | bytes 196612
  184.2 71.2 %copy-start.42 = (f32[16,256]{1,0:T(8,128)}, f32[16,256]{1,0:T(8,128)S(1)}, u32[]{:S(2)}) copy-start(f32[16,256]{1,0:T(8,128)S(1)} %get-tuple-element.60) | copy-start | bytes 49156
  186.8 68.7 %copy-start.60 = (f32[16,256]{1,0:T(8,128)}, f32[16,256]{1,0:T(8,128)S(1)}, u32[]{:S(2)}) copy-start(f32[16,256]{1,0:T(8,128)S(1)} %fusion.15) | copy-start | bytes 49156
  257.5 76.7 %copy-start.24 = (bf16[16,128,256]{2,1,0:T(8,128)(2,1)}, bf16[16,128,256]{2,1,0:T(8,128)(2,1)S(1)}, u32[]{:S(2)}) copy-start(bf16[16,128,256]{2,1,0:T(8,128)(2,1)S(1)} %fusion.36) | copy-start | bytes 3145732
  377.9 234.0 %all-to-all-start = ((bf16[8,160,2,2048]{3,1,2,0:T(8,128)(2,1)}), bf16[8,160,2,2048]{3,1,2,0:T(8,128)(2,1)}, u32[]{:S(2)}, u32[]{:S(2)}) async-start(bf16[8,160,2,2048]{3,1,2,0:T(8,128)(2,1)} %copy_select_fusion.1), calls=%async_computation | async-start | bytes 20971520 | tf_op jit(solution)/shard_map/all_to_all | solution.py:212
  383.1 257.6 %all-gather.19.cloned.1.call-start = ((), (), s32[]{:S(2)}) async-start(), calls=%async_computation.17 | async-start | bytes 10485760 | tf_op jit(solution)/shard_map/all_gather | solution.py:218
  383.7 278.3 %all-gather.21.cloned.1.call-start = ((), (), s32[]{:S(2)}) async-start(), calls=%async_computation.18 | async-start | bytes 10485760 | tf_op jit(solution)/shard_map/all_gather | solution.py:219
  690.2 266.0 %all-to-all-start.1 = ((bf16[8,160,2,2048]{3,1,2,0:T(8,128)(2,1)}), bf16[8,160,2,2048]{3,1,2,0:T(8,128)(2,1)}, u32[]{:S(2)}, u32[]{:S(2)}) async-start(bf16[8,160,2,2048]{3,1,2,0:T(8,128)(2,1)} %copy.138), calls=%async_computation.1 | async-start | bytes 20971520 | tf_op jit(solution)/shard_map/all_to_all | solution.py:226
  695.5 260.2 %copy-start.66 = (s32[2048,1]{0,1:T(1,128)S(1)}, s32[2048,1]{0,1:T(1,128)}, u32[]{:S(2)}) copy-start(s32[2048,1]{0,1:T(1,128)} %copy-done.65) | copy-start | bytes 24580
  1083.9 244.9 %all-to-all-start.2 = ((bf16[8,160,2,2048]{3,1,2,0:T(8,128)(2,1)}), bf16[8,160,2,2048]{3,1,2,0:T(8,128)(2,1)}, u32[]{:S(2)}, u32[]{:S(2)}) async-start(bf16[8,160,2,2048]{3,1,2,0:T(8,128)(2,1)} %copy_select_fusion), calls=%async_computation.2 | async-start | bytes 20971520 | tf_op jit(solution)/shard_map/all_to_all | solution.py:242
  1089.1 738.6 %reduce-scatter.25.cloned.1.call-start = ((), (), s32[]{:S(2)}) async-start(), calls=%async_computation.26 | async-start | bytes 1081344
  1089.2 249.7 %copy-start.52 = (bf16[256,16]{0,1:T(8,128)(2,1)}, bf16[256,16]{0,1:T(8,128)(2,1)S(1)}, u32[]{:S(2)}) copy-start(bf16[256,16]{0,1:T(8,128)(2,1)S(1)} %multiply_convert_fusion.4) | copy-start | bytes 24580
  1090.7 738.4 %reduce-scatter.23.cloned.1.call-start = ((), (), s32[]{:S(2)}) async-start(), calls=%async_computation.25 | async-start | bytes 10485760 | tf_op jit(solution)/shard_map/reduce_scatter | solution.py:265
  1356.3 477.0 %reduce-scatter.19.cloned.1.call-start = ((), (), s32[]{:S(2)}) async-start(), calls=%async_computation.23 | async-start | bytes 10485760 | tf_op jit(solution)/shard_map/reduce_scatter | solution.py:259
  1448.7 234.0 %all-to-all-start.3 = ((bf16[8,160,2,2048]{3,1,2,0:T(8,128)(2,1)}), bf16[8,160,2,2048]{3,1,2,0:T(8,128)(2,1)}, u32[]{:S(2)}, u32[]{:S(2)}) async-start(bf16[8,160,2,2048]{3,1,2,0:T(8,128)(2,1)} %copy.143), calls=%async_computation.3 | async-start | bytes 20971520 | tf_op jit(solution)/shard_map/all_to_all | solution.py:270
  1453.9 383.3 %reduce-scatter.21.cloned.1.call-start = ((), (), s32[]{:S(2)}) async-start(), calls=%async_computation.24 | async-start | bytes 10485760 | tf_op jit(solution)/shard_map/reduce_scatter | solution.py:262
  1471.8 481.6 %reduce-scatter.17.cloned.1.call-start = ((), (), s32[]{:S(2)}) async-start(), calls=%async_computation.22 | async-start | bytes 17301504 | tf_op jit(solution)/shard_map/reduce_scatter | solution.py:332
  1767.4 373.3 %reduce-scatter.15.cloned.1.call-start = ((), (), s32[]{:S(2)}) async-start(), calls=%async_computation.21 | async-start | bytes 17301504 | tf_op jit(solution)/shard_map/reduce_scatter | solution.py:331
  1789.2 538.6 %reduce-scatter.13.cloned.1.call-start = ((), (), s32[]{:S(2)}) async-start(), calls=%async_computation.20 | async-start | bytes 17301504 | tf_op jit(solution)/shard_map/reduce_scatter | solution.py:330
  1811.9 702.9 %reduce-scatter.11.cloned.1.call-start = ((), (), s32[]{:S(2)}) async-start(), calls=%async_computation.19 | async-start | bytes 17301504 | tf_op jit(solution)/shard_map/reduce_scatter | solution.py:329
  (70 other events, 439.8 us)
Sparse Core Ops, SparseCore 0:
  11.1 80.5 all-gather.12
  94.6 75.8 all-gather.10
  173.5 75.9 all-gather.8
  252.4 75.9 all-gather.14
  330.1 86.0 all-gather.16
  417.9 87.4 all-gather.18
  507.2 87.6 all-gather.20
  1092.1 143.9 reduce-scatter.24
  1356.4 84.3 reduce-scatter.22
  1443.7 86.3 reduce-scatter.18
  1533.4 86.3 reduce-scatter.20
  1767.5 185.8 reduce-scatter.16
  1956.3 184.3 reduce-scatter.14
  2143.4 184.3 reduce-scatter.12
  2330.5 184.3 reduce-scatter.10
where the time goes:
time: 2530 us; the launch traced here: 2520 us
  waiting for transfers between devices  1510 us (60%)
  blocking collectives  341 us (13%)
  matrix products  287 us (11%)
  local copies, waits for them, and re-layouts  261 us (10%)
  other arithmetic  85.7 us (3%)
    all_gather x1, blocking collectives, on_device(): lax.all_gather(router_weight, ('dp', 'expert'), axis=0, tiled=True)  258 us
    all_to_all x1, waiting for transfers between devices, on_device(): lax.all_to_all(outgoing_grad, 'expert', split_axis=0, concat_axis=1, tile...  238 us
    all_to_all x1, waiting for transfers between devices, on_device(): lax.all_to_all(outgoing, 'expert', split_axis=0, concat_axis=1, tiled=True)  228 us
    all_to_all x1, waiting for transfers between devices, on_device(): lax.all_to_all(sending_grad, 'expert', split_axis=0, concat_axis=0, tiled...  203 us
    reduce_scatter x1, waiting for transfers between devices, on_device(): lax.psum_scatter(value_grad, ('dp', 'expert'), scatter_dimension=0, tiled...  187 us
    reduce_scatter x1, waiting for transfers between devices, on_device(): lax.psum_scatter(key_grad, ('dp', 'expert'), scatter_dimension=0, tiled=T...  187 us
    reduce_scatter x1, waiting for transfers between devices, on_device(): lax.psum_scatter(query_grad, ('dp', 'expert'), scatter_dimension=0, tiled...  187 us
    unnamed x2, blocking collectives  82.3 us
  transfers between devices with their start and end apart: 19, of which 11 were waited for; matrix products, arithmetic and copies ran while one was open for 18% of the time, Pallas kernels for 0%

commit v1 on v0

v1 whole, which is shorter than its diff:
```python
import functools
import math

import jax
import jax.numpy as jnp
from jax import lax
from jax.experimental import pallas as pl
from jax.experimental.pallas import tpu as pltpu
from jax.sharding import PartitionSpec as P

HD = 128


epsilon = 1e-05
rope_base = 10000.0
masked_score = -1e30


def norm_scale(values):
    return lax.rsqrt(jnp.mean(values * values, axis=-1, keepdims=True) + epsilon)


def norm_back(upstream, unit, scale):
    return scale * (upstream - unit * jnp.mean(upstream * unit, axis=-1, keepdims=True))


def rotary_tables(segments, head_size):
    length = segments.shape[-1]
    order = jnp.arange(length, dtype=jnp.int32)
    starts = jnp.sum((segments[..., None, :] < segments[..., :, None]).astype(jnp.int32), axis=-1)
    position = (order - starts).astype(jnp.float32)
    frequency = rope_base ** (-2.0 * jnp.arange(head_size // 2, dtype=jnp.float32) / head_size)
    angle = position[..., None] * frequency
    return (jnp.cos(angle), jnp.sin(angle))


def rotate(values, cosine, sine):
    half = values.shape[-1] // 2
    first = values[..., :half]
    second = values[..., half:]
    return jnp.concatenate(
        [first * cosine - second * sine, second * cosine + first * sine], axis=-1
    )


def rotate_back(upstream, cosine, sine):
    half = upstream.shape[-1] // 2
    first = upstream[..., :half]
    second = upstream[..., half:]
    return jnp.concatenate(
        [first * cosine + second * sine, second * cosine - first * sine], axis=-1
    )


VMEM_BYTES = 60 * 1024 * 1024


def dot_nt(a, b):
    return lax.dot_general(a, b, (((1,), (1,)), ((), ())), preferred_element_type=jnp.float32)


def dot_nn(a, b):
    return lax.dot_general(a, b, (((1,), (0,)), ((), ())), preferred_element_type=jnp.float32)


def dot_tn(a, b):
    return lax.dot_general(a, b, (((0,), (0,)), ((), ())), preferred_element_type=jnp.float32)


def block(start, size):
    return pl.ds(pl.multiple_of(start * size, size), size)


def swiglu(gate_pre, up_pre, back, gate):
    sig = 1.0 / (1.0 + jnp.exp(-gate_pre))
    act = gate_pre * sig
    hid = act * up_pre
    scaled = back * gate
    return (
        jnp.sum(hid * back, axis=1, keepdims=True),
        (scaled * up_pre * (sig + act * (1.0 - sig))).astype(jnp.bfloat16),
        (scaled * act).astype(jnp.bfloat16),
        (hid * gate).astype(jnp.bfloat16),
    )


def first_body(cap, ff, rb, nb, n_e, x_ref, g_ref, *rest):
    po, px, py = [rest[i * n_e : (i + 1) * n_e] for i in range(3)]
    (rr_ref, gt_ref, rg_ref, h_ref, gate_ref, dgr_ref, sx, kx, ky, sy,
     p, xs, gs, r, g, hb, dp, p_sem, in_sem, rg_sem, h_sem, d_sem) = rest[3 * n_e :]
    _, src, _, tok = rr_ref.shape
    rows, width = r.shape[1:]
    team = xs.shape[1]
    half = width // 2
    shards = (po, px, py)

    def load(f, e, slot):
        return pltpu.make_async_copy(shards[f][e], p.at[slot], p_sem.at[slot])

    load(0, 0, 0).start()

    def fetch(s, slot):
        return (
            pltpu.make_async_copy(x_ref.at[block(s, team), pl.ds(0, tok)], xs.at[slot], in_sem.at[0, slot]),
            pltpu.make_async_copy(g_ref.at[block(s, team), pl.ds(0, tok)], gs.at[slot], in_sem.at[1, slot]),
        )

    for c in fetch(0, 0):
        c.start()

    @pl.loop(0, src // team)
    def _(s):
        slot = lax.rem(s, 2)

        @pl.when(s + 1 < src // team)
        def _():
            for c in fetch(s + 1, 1 - slot):
                c.start()

        for c in fetch(s, slot):
            c.wait()
        got = [[[], [], []] for _ in range(n_e)]
        for j in range(team):
            hits = [lax.broadcasted_iota(jnp.int32, (cap, tok), 0) == rr_ref[e, s * team + j] for e in range(n_e)]
            one = jnp.concatenate([hit.astype(jnp.float32) for hit in hits], axis=0).astype(jnp.bfloat16)
            rx, rg = dot_nn(one, xs[slot, j]), dot_nn(one, gs[slot, j])
            for e in range(n_e):
                got[e][0].append(rx[e * cap : (e + 1) * cap])
                got[e][1].append(rg[e * cap : (e + 1) * cap])
                got[e][2].append(jnp.sum(jnp.where(hits[e], gt_ref[e, s * team + j], 0.0), axis=1, keepdims=True))
        at = block(s, team * cap)
        for e in range(n_e):
            a, b, c = [v[0] if team == 1 else jnp.concatenate(v, axis=0) for v in got[e]]
            r[e, at, :] = a.astype(jnp.bfloat16)
            g[e, at, :] = b.astype(jnp.bfloat16)
            gate_ref[e, at, :] = c

    keep = []
    for e in range(n_e):
        for i, v in enumerate((r, g)):
            c = pltpu.make_async_copy(v.at[e], rg_ref.at[e, i], rg_sem.at[e, i])
            c.start()
            keep.append(c)
    dgr_ref[...] = jnp.zeros_like(dgr_ref)

    def put_h(f, e, slot):
        return pltpu.make_async_copy(hb.at[slot], h_ref.at[e, :, :, pl.ds(f * ff, ff)], h_sem.at[slot])

    def put_d(f, e, slot):
        low, high = ((sx, kx), (ky, sy))[f - 1]
        return (
            pltpu.make_async_copy(dp.at[slot, :, pl.ds(0, half)], low.at[e], d_sem.at[0, slot]),
            pltpu.make_async_copy(dp.at[slot, :, pl.ds(half, half)], high.at[e], d_sem.at[1, slot]),
        )

    for f in range(3):
        for e in range(n_e):
            slot = e % 2
            if e + 1 < n_e:
                load(f, e + 1, 1 - slot).start()
            elif f < 2:
                load(f + 1, 0, 1 - slot).start()
            load(f, e, slot).wait()
            if f > 0:
                put_h(f - 1, e, slot).wait()

            @pl.loop(0, rows // rb)
            def _(m):
                at = block(m, rb)
                pre = dot_nt(r[e, at, :], p[slot, pl.ds(0, 2 * ff), :])
                back = dot_nt(g[e, at, :], p[slot, pl.ds(2 * ff, ff), :])
                total, a, b, c = swiglu(pre[:, :ff], pre[:, ff:], back, gate_ref[e, at, :])
                dgr_ref[e, at, :] += total
                hb[slot, 0, at, :] = a
                hb[slot, 1, at, :] = b
                hb[slot, 2, at, :] = c

            put_h(f, e, slot).start()
            if f > 0:
                if f > 1:
                    for c in put_d(f - 1, e, slot):
                        c.wait()
                both = jnp.concatenate([hb[slot, 0], hb[slot, 1]], axis=1)

                @pl.loop(0, width // nb)
                def _(n):
                    at = block(n, nb)
                    dp[slot, 0 : 2 * ff, at] = dot_tn(both, r[e, :, at]).astype(jnp.bfloat16)
                    dp[slot, 2 * ff : 3 * ff, at] = dot_tn(hb[slot, 2], g[e, :, at]).astype(jnp.bfloat16)

                for c in put_d(f, e, slot):
                    c.start()
    for e in range(n_e):
        put_h(2, e, e % 2).wait()
        for c in put_d(2, e, e % 2):
            c.wait()
    for c in keep:
        c.wait()


def experts_first(x, g, po, px, py, rr, gt, cap, rb=640, nb=1024):
    n_e, src, _, tok = rr.shape
    width = x.shape[2]
    ff = po[0].shape[0] // 3
    rows = src * cap
    team = 16 // math.gcd(cap, 16)
    bf, f32 = jnp.bfloat16, jnp.float32
    anys, vm = pl.BlockSpec(memory_space=pl.ANY), pl.BlockSpec(memory_space=pltpu.VMEM)
    part = jax.ShapeDtypeStruct((n_e, 3 * ff, width // 2), bf)
    return pl.pallas_call(
        functools.partial(first_body, cap, ff, rb, nb, n_e),
        out_shape=(
            jax.ShapeDtypeStruct((n_e, 2, rows, width), bf),
            jax.ShapeDtypeStruct((n_e, 3, rows, 3 * ff), bf),
            jax.ShapeDtypeStruct((n_e, rows, 1), f32),
            jax.ShapeDtypeStruct((n_e, rows, 1), f32),
            part, part, part, part,
        ),
        in_specs=[anys] * (2 + 3 * n_e) + [vm] * 2,
        out_specs=(anys, anys, vm, vm, anys, anys, anys, anys),
        scratch_shapes=[
            pltpu.VMEM((2, 3 * ff, width), bf),
            pltpu.VMEM((2, team, tok, width), bf),
            pltpu.VMEM((2, team, tok, width), bf),
            pltpu.VMEM((n_e, rows, width), bf),
            pltpu.VMEM((n_e, rows, width), bf),
            pltpu.VMEM((2, 3, rows, ff), bf),
            pltpu.VMEM((2, 3 * ff, width), bf),
            pltpu.SemaphoreType.DMA((2,)),
            pltpu.SemaphoreType.DMA((2, 2)),
            pltpu.SemaphoreType.DMA((n_e, 2)),
            pltpu.SemaphoreType.DMA((2,)),
            pltpu.SemaphoreType.DMA((2, 2)),
        ],
        compiler_params=pltpu.CompilerParams(vmem_limit_bytes=VMEM_BYTES),
    )(x, g, *po, *px, *py, rr, gt)


def spread_tiles(cap, nb, h, p, rc_ref, own_ref, sib_ref, acc, stage, st_sem):
    n_e = h.shape[0]
    nz, tok = stage.shape[2:4]
    tiles = p.shape[2] // nb

    def put(n, slot):
        return [
            pltpu.make_async_copy(stage.at[slot, w], ref.at[:, :, block(n, nb)], st_sem.at[slot, w])
            for w, ref in enumerate((own_ref, sib_ref))
        ]

    @pl.loop(0, tiles)
    def _(n):
        slot = lax.rem(n, 2)
        for e in range(n_e):
            acc[e] = dot_nn(h[e], p[e, :, block(n, nb)])

        @pl.when(n >= 2)
        def _():
            for c in put(n, slot):
                c.wait()

        def one(z, w):
            s = 2 * z + w
            hits = [
                (lax.broadcasted_iota(jnp.int32, (tok, cap), 1) == rc_ref[e, s]).astype(jnp.float32) for e in range(n_e)
            ]
            hit = jnp.concatenate(hits, axis=1).astype(jnp.bfloat16)
            part = jnp.concatenate([acc[e, block(s, cap)] for e in range(n_e)], axis=0).astype(jnp.bfloat16)
            stage[slot, w, z] = dot_nn(hit, part).astype(jnp.bfloat16)

        if nz <= 4:
            for z in range(nz):
                for w in range(2):
                    one(z, w)
        else:

            @pl.loop(0, nz)
            def _(z):
                for w in range(2):
                    one(z, w)

        for c in put(n, slot):
            c.start()

    for slot in range(2):
        for c in put(slot, slot):
            c.wait()


def last_body(cap, ff, rb, nb, n_e, rg_ref, ha_ref, gate_ref, dgr_in, *rest):
    po, px, py, da, db = [rest[i * n_e : (i + 1) * n_e] for i in range(5)]
    (rr_ref, rc_ref, hd_ref, dg_ref, own_ref, sib_ref,
     p, pd, h, r, g, hb, dgr, acc, stage, p_sem, h_sem, rg_sem, hb_sem, st_sem) = rest[5 * n_e :]
    _, src, _, tok = rr_ref.shape
    rows, width = ha_ref.shape[2], rg_ref.shape[3]
    half = width // 2
    hidden = 4 * ff
    early, late = [], []
    for e in range(n_e):
        for i in range(2):
            for j, ref in enumerate((da, db)):
                early.append(pltpu.make_async_copy(
                    ref[e].at[pl.ds(i * ff, ff)], p.at[e, pl.ds(i * hidden + 3 * ff, ff), pl.ds(j * half, half)], p_sem.at[e, 2 * i + j]))
            for j, ref in enumerate((po, px, py)):
                late.append(pltpu.make_async_copy(
                    ref[e].at[pl.ds(i * ff, ff)], p.at[e, pl.ds(i * hidden + j * ff, ff)], p_sem.at[e, 6 + 3 * i + j]))
            late.append(pltpu.make_async_copy(ha_ref.at[e, i], h.at[e, :, pl.ds(i * hidden, 3 * ff)], h_sem.at[e, i]))
        for j, ref in enumerate((da, db)):
            early.append(pltpu.make_async_copy(
                ref[e].at[pl.ds(2 * ff, ff)], pd.at[e, :, pl.ds(j * half, half)], p_sem.at[e, 4 + j]))
    per = rows // rb
    steps = [(e, m) for e in range(n_e) for m in range(per)]

    def fetch(k):
        e, m = steps[k]
        at = pl.ds(m * rb, rb)
        return [
            pltpu.make_async_copy(rg_ref.at[e, i, at], v.at[k % 2], rg_sem.at[i, k % 2]) for i, v in enumerate((r, g))
        ]

    for c in early + fetch(0):
        c.start()
    for c in late:
        c.start()
    for c in early:
        c.wait()
    dgr[...] = dgr_in[...]
    for k, (e, m) in enumerate(steps):
        if k + 1 < len(steps):
            for c in fetch(k + 1):
                c.start()
        for c in fetch(k):
            c.wait()
        at = pl.ds(m * rb, rb)
        rm, gm = r[k % 2], g[k % 2]
        gate_pre = dot_nt(rm, p[e, pl.ds(3 * ff, ff), :])
        up_pre = dot_nt(rm, p[e, pl.ds(hidden + 3 * ff, ff), :])
        back = dot_nt(gm, pd[e])
        total, a, b, c = swiglu(gate_pre, up_pre, back, gate_ref[e, at, :])
        dgr[e, at, :] += total
        h[e, at, pl.ds(3 * ff, ff)] = a
        h[e, at, pl.ds(hidden + 3 * ff, ff)] = b
        hb[e, 0, at, :] = a
        hb[e, 1, at, :] = b
        hb[e, 2, at, :] = c
    outs = [pltpu.make_async_copy(hb.at[e], hd_ref.at[e], hb_sem.at[e]) for e in range(n_e)]
    for c in outs:
        c.start()
    for e in range(n_e):

        @pl.loop(0, src)
        def _(s):
            hit = lax.broadcasted_iota(jnp.int32, (cap, tok), 0) == rr_ref[e, s]
            dg_ref[e, s] = jnp.sum(jnp.where(hit, dgr[e, block(s, cap), :], 0.0), axis=0, keepdims=True)

    for c in late:
        c.wait()
    spread_tiles(cap, nb, h, p, rc_ref, own_ref, sib_ref, acc, stage, st_sem)
    for c in outs:
        c.wait()


def tile_width(src):
    return 512 if src <= 8 else 128


def experts_last(rg, ha, gate, dgr, po, px, py, da, db, rr, rc, cap, rb=320):
    n_e, src, _, tok = rr.shape
    rows, width = rg.shape[2:]
    ff = po[0].shape[0] // 3
    nz = src // 2
    nb = tile_width(src)
    bf, f32 = jnp.bfloat16, jnp.float32
    anys, vm = pl.BlockSpec(memory_space=pl.ANY), pl.BlockSpec(memory_space=pltpu.VMEM)
    side = jax.ShapeDtypeStruct((nz, tok, width), bf)
    return pl.pallas_call(
        functools.partial(last_body, cap, ff, rb, nb, n_e),
        out_shape=(
            jax.ShapeDtypeStruct((n_e, 3, rows, ff), bf),
            jax.ShapeDtypeStruct((n_e, src, 1, tok), f32),
            side, side,
        ),
        in_specs=[anys] * 2 + [vm] * 2 + [anys] * (5 * n_e) + [vm] * 2,
        out_specs=(anys, vm, anys, anys),
        scratch_shapes=[
            pltpu.VMEM((n_e, 8 * ff, width), bf),
            pltpu.VMEM((n_e, ff, width), bf),
            pltpu.VMEM((n_e, rows, 8 * ff), bf),
            pltpu.VMEM((2, rb, width), bf),
            pltpu.VMEM((2, rb, width), bf),
            pltpu.VMEM((n_e, 3, rows, ff), bf),
            pltpu.VMEM((n_e, rows, 1), f32),
            pltpu.VMEM((n_e, rows, nb), f32),
            pltpu.VMEM((2, 2, nz, tok, nb), bf),
            pltpu.SemaphoreType.DMA((n_e, 12)),
            pltpu.SemaphoreType.DMA((n_e, 2)),
            pltpu.SemaphoreType.DMA((2, 2)),
            pltpu.SemaphoreType.DMA((n_e,)),
            pltpu.SemaphoreType.DMA((2, 2)),
        ],
        compiler_params=pltpu.CompilerParams(vmem_limit_bytes=VMEM_BYTES),
    )(rg, ha, gate, dgr, *po, *px, *py, *da, *db, rr, rc)


def mixture_body(cap, ff, nb, n_e, ha_ref, hd_ref, *rest):
    po, px, py, da, db = [rest[i * n_e : (i + 1) * n_e] for i in range(5)]
    rc_ref, own_ref, sib_ref, p, h, acc, stage, p_sem, st_sem = rest[5 * n_e :]
    half = p.shape[2] // 2
    copies = []
    for e in range(n_e):
        for j, ref in enumerate((po, px, py)):
            copies.append(pltpu.make_async_copy(ref[e].at[pl.ds(2 * ff, ff)], p.at[e, pl.ds(j * ff, ff)], p_sem.at[e, j]))
        for j, ref in enumerate((da, db)):
            copies.append(pltpu.make_async_copy(
                ref[e].at[pl.ds(2 * ff, ff)], p.at[e, pl.ds(3 * ff, ff), pl.ds(j * half, half)], p_sem.at[e, 3 + j]))
        copies.append(pltpu.make_async_copy(ha_ref.at[e, 2], h.at[e, :, pl.ds(0, 3 * ff)], p_sem.at[e, 5]))
        copies.append(pltpu.make_async_copy(hd_ref.at[e, 2], h.at[e, :, pl.ds(3 * ff, ff)], p_sem.at[e, 6]))
    for c in copies:
        c.start()
    for c in copies:
        c.wait()
    spread_tiles(cap, nb, h, p, rc_ref, own_ref, sib_ref, acc, stage, st_sem)


def experts_mixture(ha, hd, po, px, py, da, db, rc, cap):
    n_e, src, tok, _ = rc.shape
    rows, width = ha.shape[2], po[0].shape[1]
    ff = po[0].shape[0] // 3
    nz = src // 2
    nb = tile_width(src)
    bf, f32 = jnp.bfloat16, jnp.float32
    anys, vm = pl.BlockSpec(memory_space=pl.ANY), pl.BlockSpec(memory_space=pltpu.VMEM)
    side = jax.ShapeDtypeStruct((nz, tok, width), bf)
    return pl.pallas_call(
        functools.partial(mixture_body, cap, ff, nb, n_e),
        out_shape=(side, side),
        in_specs=[anys] * (2 + 5 * n_e) + [vm],
        out_specs=(anys, anys),
        scratch_shapes=[
            pltpu.VMEM((n_e, 4 * ff, width), bf),
            pltpu.VMEM((n_e, rows, 4 * ff), bf),
            pltpu.VMEM((n_e, rows, nb), f32),
            pltpu.VMEM((2, 2, nz, tok, nb), bf),
            pltpu.SemaphoreType.DMA((n_e, 7)),
            pltpu.SemaphoreType.DMA((2, 2)),
        ],
        compiler_params=pltpu.CompilerParams(vmem_limit_bytes=VMEM_BYTES),
    )(ha, hd, *po, *px, *py, *da, *db, rc)


def grads_body(ff, h_ref, rg_ref, low, high, ht):
    part = pl.program_id(1)

    @pl.when(part == 0)
    def _():
        for i in range(3):
            ht[pl.ds(i * ff, ff), :] = h_ref[0, i].T

    def out(ref):
        ref[0, 0 : 2 * ff, :] = dot_nn(ht[0 : 2 * ff, :], rg_ref[0, 0]).astype(jnp.bfloat16)
        ref[0, 2 * ff : 3 * ff, :] = dot_nn(ht[2 * ff : 3 * ff, :], rg_ref[0, 1]).astype(jnp.bfloat16)

    @pl.when(part == 0)
    def _():
        out(low)

    @pl.when(part == 1)
    def _():
        out(high)


def expert_grads(h, rg, quarter, ff):
    n_e, _, rows, _ = h.shape
    half = rg.shape[3] // 2
    side = jax.ShapeDtypeStruct((n_e, 3 * ff, half), jnp.bfloat16)
    return pl.pallas_call(
        functools.partial(grads_body, ff),
        out_shape=(side, side),
        grid=(n_e, 2),
        in_specs=[
            pl.BlockSpec((1, 3, rows, ff), lambda e, j: (e, 0, 0, quarter)),
            pl.BlockSpec((1, 2, rows, half), lambda e, j: (e, 0, 0, j)),
        ],
        out_specs=(pl.BlockSpec((1, 3 * ff, half), lambda e, j: (e, 0, 0)),) * 2,
        scratch_shapes=[pltpu.VMEM((3 * ff, rows), jnp.bfloat16)],
        compiler_params=pltpu.CompilerParams(vmem_limit_bytes=VMEM_BYTES),
    )(h, rg)


fence = lax.optimization_barrier


def all_heads(values):
    return values.reshape(values.shape[0], values.shape[1] // HD, HD)


def plus(a, b):
    return a.astype(jnp.float32) + b.astype(jnp.float32)


def on_device(
    hidden_in,
    cotangent,
    attention_gain,
    query_gain,
    key_gain,
    mixture_gain,
    query_weight,
    key_weight,
    value_weight,
    output_weight,
    router_weight,
    gate_weight,
    up_weight,
    down_weight,
    routes,
    segments,
):
    bf16, f32 = jnp.bfloat16, jnp.float32
    n_dp, owners = lax.axis_size("dp"), lax.axis_size("expert")
    nz = owners // 2
    n_dev = n_dp * owners
    tokens, width = hidden_in.shape
    half = width // 2
    unit = width // (n_dev // 2)
    top = routes.shape[1]
    exp_dev = gate_weight.shape[0]
    experts = exp_dev * owners
    cap = max(2, tokens * top * 5 // (experts * 4))
    ff = gate_weight.shape[2]
    rows_dev = attention_gain.shape[0]
    score_scale = HD ** (-0.5)
    dp, ex = lax.axis_index("dp"), lax.axis_index("expert")
    core, zc = ex % 2, ex // 2
    device = dp * owners + ex

    def swap(v, axis, bit):
        size = n_dp if axis == "dp" else owners
        return lax.ppermute(v, axis, [(i, i ^ bit) for i in range(size)])

    def swap_core(v):
        return swap(v, "expert", 1)

    def ring(v):
        return lax.ppermute(v, "expert", [(i, (i + 2) % owners) for i in range(owners)])

    def swap_x(v):
        return swap(v, "dp", 1)

    def swap_y(v):
        return swap(v, "dp", 2)

    def in_order(bit, mine, other, axis):
        return jnp.where(
            bit == 0,
            jnp.concatenate([mine, other], axis=axis),
            jnp.concatenate([other, mine], axis=axis),
        )

    def half_of(v, which, axis):
        return lax.dynamic_slice_in_dim(v, which * (v.shape[axis] // 2), v.shape[axis] // 2, axis)

    def other_first(v):
        return jnp.concatenate([v[tokens:], v[:tokens]], axis=0)

    def chip_row(plane, r):
        return ((dp ^ plane) * nz + (zc - r) % nz) * unit

    def turn(v):
        flipped = jnp.flip(v, 0)
        doubled = jnp.concatenate([flipped, flipped], axis=0)
        return lax.dynamic_slice_in_dim(doubled, nz - 1 - zc, nz, 0)

    def relative_sources(v):
        v = turn(v.reshape((nz, 2) + v.shape[1:]))
        v = jnp.where(core == 1, jnp.flip(v, 1), v)
        return v.reshape((owners,) + v.shape[2:])

    bits = []
    b = 1
    while b < owners:
        bits.append(("expert", b, (ex // b) % 2))
        b *= 2
    b = 1
    while b < n_dp:
        bits.append(("dp", b, (dp // b) % 2))
        b *= 2

    sources = (query_weight, key_weight, value_weight, output_weight)
    theirs = jnp.concatenate([half_of(w, 1 - core, 1) for w in sources], axis=1)
    mine = jnp.concatenate([half_of(w, core, 1) for w in sources], axis=1)
    small = jnp.concatenate(
        [attention_gain, query_gain, key_gain, mixture_gain, router_weight.T.reshape(-1)]
    )[None]
    theirs = swap_core(theirs)
    documents = jnp.concatenate([segments, swap_core(segments)], axis=0)
    for axis, bit, mark in bits:
        small = in_order(mark, small, swap(small, axis, bit), 0)
    piece = in_order(core, mine, theirs, 0)
    own_parts = tuple(
        jnp.concatenate([gate_weight[e].T, up_weight[e].T, down_weight[e]], axis=0)
        for e in range(exp_dev)
    )
    route_rows = routes.T.astype(bf16).reshape(-1, width)
    pad = -route_rows.shape[0] % 16
    cot_piece = jnp.concatenate(
        [cotangent, route_rows, jnp.zeros((pad, width), bf16)], axis=0
    )
    nought = jnp.zeros((1, 1), bf16)
    piece, small, documents, own_parts, cot_piece, nought = fence(
        (piece, small, documents, own_parts, cot_piece, nought)
    )

    weights = jnp.broadcast_to(nought, (width, 4 * half))
    cut = unit // 2
    before = None
    cot_steps = [cot_piece]
    for r in range(nz):
        by_x, by_y = swap_x(piece), swap_y(piece)
        following, low, high = (), (), ()
        if r + 1 < nz:
            following = ring(piece)
        if before is not None:
            low, high = swap_y(before[0][:cut]), swap_x(before[1][cut:])
        if r + 1 == nz:
            cot_steps.append(ring(cot_steps[-1]))
        weights = lax.dynamic_update_slice(weights, piece, (chip_row(0, r), 0))
        if before is not None:
            weights = lax.dynamic_update_slice(weights, before[0], (chip_row(1, r - 1), 0))
            weights = lax.dynamic_update_slice(weights, before[1], (chip_row(2, r - 1), 0))
        by_x, by_y, following, low, high, weights, cot_steps = fence(
            (by_x, by_y, following, low, high, weights, cot_steps)
        )
        if before is not None:
            weights = lax.dynamic_update_slice(weights, low, (chip_row(3, r - 1), 0))
            weights = lax.dynamic_update_slice(weights, high, (chip_row(3, r - 1) + cut, 0))
        before = (by_x, by_y)
        piece = following
    low, high = swap_y(before[0][:cut]), swap_x(before[1][cut:])
    weights = lax.dynamic_update_slice(weights, before[0], (chip_row(1, nz - 1), 0))
    weights = lax.dynamic_update_slice(weights, before[1], (chip_row(2, nz - 1), 0))

    gains_all = small[:, : 4 * rows_dev].reshape(n_dev, 4, rows_dev)
    gains_all = gains_all.swapaxes(0, 1).reshape(4, width).astype(f32)
    attention_gain_full, query_gain_full, key_gain_full, mixture_gain_full = (
        gains_all[0],
        gains_all[1],
        gains_all[2],
        gains_all[3],
    )
    router_t = (
        small[:, 4 * rows_dev :]
        .reshape(n_dev, experts, rows_dev)
        .swapaxes(0, 1)
        .reshape(experts, width)
    )
    query_gain_half = half_of(query_gain_full, core, 0)
    key_gain_half = half_of(key_gain_full, core, 0)
    residual = hidden_in.astype(f32)
    scale_one = norm_scale(residual)
    cosine, sine = rotary_tables(documents, HD)
    cosine = cosine.reshape(2 * tokens, 1, HD // 2)
    sine = sine.reshape(2 * tokens, 1, HD // 2)
    order = jnp.arange(tokens, dtype=jnp.int32)
    allowed = (documents[:, :, None] == documents[:, None, :]) & (
        order[:, None] >= order[None, :]
    )
    unit_one = residual * scale_one
    normed = (unit_one * attention_gain_full).astype(bf16)
    normed = jnp.concatenate([normed, swap_core(normed)], axis=0)
    (low, high, weights, normed, cosine, sine, router_t) = fence(
        (low, high, weights, normed, cosine, sine, router_t)
    )
    weights = lax.dynamic_update_slice(weights, low, (chip_row(3, nz - 1), 0))
    weights = lax.dynamic_update_slice(weights, high, (chip_row(3, nz - 1) + cut, 0))
    qkv_weight, out_weight = weights[:, : 3 * half], weights[:, 3 * half :]

    by_x = [swap_x(own_parts[0])]
    by_y = [swap_y(own_parts[0])]

    raw = jnp.dot(normed, qkv_weight, preferred_element_type=f32)
    query_raw, key_raw = raw[:, :half], raw[:, half : 2 * half]
    value_heads = raw[:, 2 * half :].astype(bf16)
    squares = jnp.stack(
        [jnp.sum(query_raw * query_raw, axis=-1), jnp.sum(key_raw * key_raw, axis=-1)]
    )
    squares = squares + jnp.roll(swap_core(squares), tokens, axis=1)
    scales = lax.rsqrt(squares / width + epsilon)
    query_scale, key_scale = scales[0][:, None], scales[1][:, None]
    query_unit, key_unit = query_raw * query_scale, key_raw * key_scale
    heads = half // HD

    def by_sequence(v):
        return v.reshape(2, tokens, heads, HD)

    query_heads = by_sequence(
        rotate(all_heads(query_unit * query_gain_half), cosine, sine).astype(bf16)
    )
    key_heads = by_sequence(rotate(all_heads(key_unit * key_gain_half), cosine, sine).astype(bf16))
    value_heads = by_sequence(value_heads)
    scores = (
        jnp.einsum("nthd,nshd->nhts", query_heads, key_heads, preferred_element_type=f32)
        * score_scale
    )
    scores = jnp.where(allowed[:, None], scores, masked_score)
    peak = jnp.max(scores, axis=-1, keepdims=True)
    grown = jnp.exp(scores - peak)
    chances = grown / jnp.sum(grown, axis=-1, keepdims=True)
    chances_low = chances.astype(bf16)
    context = jnp.einsum("nhts,nshd->nthd", chances_low, value_heads, preferred_element_type=f32)
    context = context.astype(bf16).reshape(2 * tokens, half)
    context_full = in_order(core, context, other_first(swap_core(context)), 1)
    while len(cot_steps) < nz:
        cot_steps.append(ring(cot_steps[-1]))
    out_half = jnp.dot(context_full, out_weight, preferred_element_type=f32)
    attended = in_order(core, out_half[:tokens], swap_core(out_half[tokens:]), 1)
    middle = residual + attended
    scale_two = norm_scale(middle)
    unit_two = middle * scale_two
    mixed_in = (unit_two * mixture_gain_full).astype(bf16)
    logits = jnp.einsum("et,dt->ed", router_t, mixed_in, preferred_element_type=f32)
    router_probs = jax.nn.softmax(logits, axis=0)
    prob_high = router_probs.astype(bf16)
    prob_low = (router_probs - prob_high.astype(f32)).astype(bf16)
    prob_rows = jnp.concatenate([prob_high, prob_low], axis=0).reshape(-1, width)
    n_prob = prob_rows.shape[0]
    pad = -n_prob % 16
    mixed_piece = jnp.concatenate([mixed_in, prob_rows, jnp.zeros((pad, width), bf16)], axis=0)
    mixed_piece, by_x[0], by_y[0], cot_steps = fence((mixed_piece, by_x[0], by_y[0], cot_steps))

    def place(buffer, piece, r, which):
        return lax.dynamic_update_slice(buffer, piece[None], (2 * r + which, 0, 0))

    for e in range(1, exp_dev):
        by_x.append(swap_x(own_parts[e]))
        by_y.append(swap_y(own_parts[e]))
    mixed_last = mixed_piece
    mixed_all = jnp.broadcast_to(nought, (owners,) + mixed_piece.shape)
    cot_all = jnp.broadcast_to(nought, (owners,) + cot_piece.shape)
    for r in range(nz):
        following = ring(mixed_last) if r + 1 < nz else ()
        other, cot_other = swap_core(mixed_last), swap_core(cot_steps[r])
        mixed_all = place(mixed_all, mixed_last, r, 0)
        cot_all = place(cot_all, cot_steps[r], r, 0)
        other, following, cot_other, mixed_all, cot_all = fence(
            (other, following, cot_other, mixed_all, cot_all)
        )
        mixed_all = place(mixed_all, other, r, 1)
        cot_all = place(cot_all, cot_other, r, 1)
        mixed_last = following
    probs = mixed_all[:, tokens : tokens + n_prob].reshape(owners, 2, experts, tokens)
    probs_all = probs[:, 0].astype(f32) + probs[:, 1].astype(f32)
    routes_all = cot_all[:, tokens : tokens + top * tokens // width]
    routes_all = routes_all.reshape(owners, top, tokens).astype(jnp.int32)

    lower = (order[:, None] <= order[None, :]).astype(bf16)

    number = ex * exp_dev + jnp.arange(exp_dev, dtype=jnp.int32)[:, None, None]
    hit = jnp.any(routes_all[None] == number[..., None], axis=2)
    rank = jnp.dot(
        hit.reshape(exp_dev * owners, tokens).astype(bf16), lower, preferred_element_type=f32
    )
    rank = jnp.where(hit, rank.reshape(hit.shape).astype(jnp.int32) - 1, -1)
    rank_row, rank_col = rank[:, :, None, :], rank[:, :, :, None]
    gate_row = lax.dynamic_slice_in_dim(probs_all, ex * exp_dev, exp_dev, 1).swapaxes(0, 1)[
        :, :, None, :
    ]
    mixed_all, cot_all, by_x, by_y, rank_row, rank_col, gate_row = fence(
        (mixed_all, cot_all, by_x, by_y, rank_row, rank_col, gate_row)
    )

    corner_low = tuple(swap_y(v[:, :half]) for v in by_x)
    corner_high = tuple(swap_x(v[:, half:]) for v in by_y)
    shards = (own_parts, tuple(by_x), tuple(by_y))
    rows, acts, gates, products, send_x, keep_x, keep_y, send_y = experts_first(
        mixed_all, cot_all, *shards, rank_row, gate_row, cap
    )
    got_x, got_y = swap_x(send_x), swap_y(send_y)
    shards = shards + (corner_low, corner_high)
    acts_last, gate_backs, copied, copied_other = experts_last(
        rows, acts, gates, products, *shards, rank_row, rank_col, cap
    )

    gate_block = jnp.zeros((owners, experts, tokens), f32)
    gate_block = lax.dynamic_update_slice(
        gate_block, gate_backs[:, :, 0].swapaxes(0, 1), (0, ex * exp_dev, 0)
    )
    gate_block = gate_block.reshape(nz, 2, experts, tokens)

    def blocks_of(v, got_v):
        return [plus(v[r], got_v[r]) for r in range(nz)]

    def sum_ring(blocks, kind):
        total = blocks[1]
        for r in range(2, nz):
            total = blocks[r] + ring(total.astype(kind)).astype(f32)
        return blocks[0] + ring(total.astype(kind)).astype(f32)

    got_gate, got_copy = swap_core(gate_block[:, 1]), swap_core(copied_other)
    got_gate, got_copy = fence((got_gate, got_copy))
    prob_upstream = sum_ring(blocks_of(gate_block[:, 0], got_gate), f32)
    copies_grad = sum_ring(blocks_of(copied, got_copy), bf16)
    send_last_x, send_last_y = expert_grads(acts_last, rows, 0, ff)
    got_last_x, got_last_y = swap_x(send_last_x), swap_y(send_last_y)
    own_low, own_high = expert_grads(acts, rows, 0, ff)
    mixture, mixture_other = experts_mixture(acts, acts_last, *shards, rank_col, cap)
    (prob_upstream, copies_grad, got_x, got_y, own_low, own_high, mixture, mixture_other) = fence(
        (prob_upstream, copies_grad, got_x, got_y, own_low, own_high, mixture, mixture_other)
    )

    own_low, own_high = plus(own_low, got_x), plus(own_high, got_y)
    upstream = cotangent.astype(f32)
    picked = jnp.any(
        routes.T[None] == jnp.arange(experts, dtype=jnp.int32)[:, None, None], axis=1
    )
    prob_upstream = jnp.where(picked, prob_upstream, 0.0)
    logit_upstream = (
        router_probs
        * (prob_upstream - jnp.sum(router_probs * prob_upstream, axis=0, keepdims=True))
    ).astype(bf16)
    mixed_upstream = copies_grad + jnp.einsum(
        "et,ed->td", logit_upstream, router_t, preferred_element_type=f32
    )
    router_grad = jnp.einsum("et,td->ed", logit_upstream, mixed_in, preferred_element_type=f32)
    mixture_gain_grad = jnp.sum(mixed_upstream * unit_two, axis=0)
    middle_grad = upstream + norm_back(mixed_upstream * mixture_gain_full, unit_two, scale_two)
    branch = middle_grad.astype(bf16)
    branch_half = jnp.concatenate(
        [half_of(branch, core, 1), swap_core(half_of(branch, 1 - core, 1))], axis=0
    )
    context_part = jnp.einsum(
        "td,cd->tc", branch_half, out_weight, preferred_element_type=f32
    ).astype(bf16)
    context_up = half_of(context_part, core, 1).astype(f32) + other_first(
        swap_core(half_of(context_part, 1 - core, 1))
    ).astype(f32)
    context_up = by_sequence(context_up.astype(bf16))
    output_grad = jnp.einsum("tc,td->cd", context_full, branch_half, preferred_element_type=f32)
    output_grad = output_grad.astype(bf16)
    context_up, got_last_x, got_last_y, output_grad = fence(
        (context_up, got_last_x, got_last_y, output_grad)
    )
    more_y = swap_y(plus(keep_y, got_last_x).astype(bf16))
    more_x = swap_x(plus(keep_x, got_last_y).astype(bf16))
    chance_up = jnp.einsum("nthd,nshd->nhts", context_up, value_heads, preferred_element_type=f32)
    value_term = jnp.einsum(
        "nhts,nthd->nshd", chances_low, context_up, preferred_element_type=f32
    )
    score_up = (
        chances * (chance_up - jnp.sum(chances * chance_up, axis=-1, keepdims=True))
    ).astype(bf16)
    query_term = (
        jnp.einsum("nhts,nshd->nthd", score_up, key_heads, preferred_element_type=f32)
        * score_scale
    )
    key_term = (
        jnp.einsum("nhts,nthd->nshd", score_up, query_heads, preferred_element_type=f32)
        * score_scale
    )
    value_up = value_term.astype(bf16).reshape(2 * tokens, half)
    value_grad = jnp.einsum("tc,td->cd", normed, value_up, preferred_element_type=f32).astype(bf16)

    def unturn(v):
        return rotate_back(v.reshape(2 * tokens, heads, HD), cosine, sine).reshape(
            2 * tokens, half
        )

    query_back, key_back = unturn(query_term), unturn(key_term)
    query_gain_grad = jnp.sum(query_back * query_unit, axis=0)
    key_gain_grad = jnp.sum(key_back * key_unit, axis=0)
    query_back, key_back = query_back * query_gain_half, key_back * key_gain_half
    means = jnp.stack(
        [jnp.sum(query_back * query_unit, axis=-1), jnp.sum(key_back * key_unit, axis=-1)]
    )
    means = (means + jnp.roll(swap_core(means), tokens, axis=1)) / width
    query_up = (query_scale * (query_back - query_unit * means[0][:, None])).astype(bf16)
    key_up = (key_scale * (key_back - key_unit * means[1][:, None])).astype(bf16)
    qk_up = jnp.concatenate([query_up, key_up], axis=1)
    first = jnp.einsum("tc,td->cd", normed, qk_up, preferred_element_type=f32).astype(bf16)
    second = jnp.concatenate([value_grad, output_grad], axis=1)
    first, second, more_y, more_x = fence((first, second, more_y, more_x))

    def chip_rows(v, plane, r):
        return lax.dynamic_slice_in_dim(v, chip_row(plane, r), unit, 0)

    def several(v, picks):
        return jnp.concatenate([chip_rows(v, plane, r) for plane, r in picks], axis=0)

    near = list(range(1, nz // 2 + 1))
    far = list(range(nz // 2 + 1, nz)) + [0]

    def step_one(rs):
        sent = several(first, [(1, r) for r in rs] + [(3, r) for r in rs])
        back = several(second, [(2, r) for r in rs] + [(3, r) for r in rs])
        return swap_x(sent), swap_y(back)

    def step_two(rs, by_x, by_y):
        n = len(rs) * unit
        more_y = plus(several(first, [(2, r) for r in rs]), by_x[n:]).astype(bf16)
        more_x = plus(several(second, [(1, r) for r in rs]), by_y[n:]).astype(bf16)
        return swap_y(more_y), swap_x(more_x)

    def step_three(rs, by_x, by_y, more_y, more_x):
        n = len(rs) * unit
        left = plus(several(first, [(0, r) for r in rs]), by_x[:n]) + more_y.astype(f32)
        right = plus(several(second, [(0, r) for r in rs]), by_y[:n]) + more_x.astype(f32)
        whole = jnp.concatenate([left, right], axis=1)
        return {r: whole[i * unit : (i + 1) * unit] for i, r in enumerate(rs)}

    near_x, near_y = step_one(near)
    own_low = own_low + more_y.astype(f32)
    own_high = own_high + more_x.astype(f32)
    got_mix = swap_core(mixture_other)
    qkv_up = jnp.concatenate([qk_up, value_up], axis=1)
    normed_part = jnp.einsum("td,cd->tc", qkv_up, qkv_weight, preferred_element_type=f32)
    normed_up = normed_part[:tokens] + swap_core(normed_part[tokens:].astype(bf16)).astype(f32)
    attention_gain_grad = jnp.sum(normed_up * unit_one, axis=0)
    hidden_grad = middle_grad + norm_back(normed_up * attention_gain_full, unit_one, scale_one)
    zeros = jnp.zeros_like(query_gain_grad)
    small_sum = jnp.concatenate(
        [
            attention_gain_grad.reshape(n_dev, rows_dev),
            in_order(core, query_gain_grad, zeros, 0).reshape(n_dev, rows_dev),
            in_order(core, key_gain_grad, zeros, 0).reshape(n_dev, rows_dev),
            mixture_gain_grad.reshape(n_dev, rows_dev),
            router_grad.reshape(experts, n_dev, rows_dev)
            .swapaxes(0, 1)
            .reshape(n_dev, experts * rows_dev),
        ],
        axis=1,
    )

    def fold(v, i):
        axis, bit, mark = bits[i]
        return half_of(v, mark, 0) + swap(half_of(v, 1 - mark, 0), axis, bit)

    near_x, near_y, got_mix, hidden_grad, small_sum = fence(
        (near_x, near_y, got_mix, hidden_grad, small_sum)
    )
    small_sum = fold(small_sum, len(bits) - 1)
    mix_blocks = blocks_of(mixture, got_mix)
    mixed = sum_ring(mix_blocks, bf16)
    near_more = step_two(near, near_x, near_y)
    far_x, far_y = step_one(far)
    near_more, far_x, far_y, small_sum, mixed = fence((near_more, far_x, far_y, small_sum, mixed))
    small_sum = fold(small_sum, len(bits) - 2)
    far_more = step_two(far, far_x, far_y)
    blocks = step_three(near, near_x, near_y, *near_more)
    total = blocks[near[0]]
    for r in near[1:]:
        total = blocks[r] + ring(total.astype(bf16)).astype(f32)
    got_total = ring(total.astype(bf16))
    layer_out = (middle + mixed).astype(bf16)
    far_more, got_total, small_sum = fence((far_more, got_total, small_sum))
    blocks = step_three(far, far_x, far_y, *far_more)
    for i, r in enumerate(far):
        total = blocks[r] + got_total.astype(f32)
        if i + 1 < len(far):
            got_total = ring(total.astype(bf16))
    for i in reversed(range(len(bits) - 2)):
        small_sum = fold(small_sum, i)
    small_sum = small_sum[0]
    gain_parts = small_sum[: 4 * rows_dev].reshape(4, rows_dev)
    router_part = small_sum[4 * rows_dev :].reshape(experts, rows_dev).T
    kept_rows = half_of(total, core, 0)
    got_rows = swap_core(half_of(total, 1 - core, 0))
    weight_grads = [
        in_order(
            core, kept_rows[:, i * half : (i + 1) * half], got_rows[:, i * half : (i + 1) * half], 1
        )
        for i in range(4)
    ]
    expert_grad = jnp.concatenate([own_low, own_high], axis=2)
    return (
        layer_out,
        hidden_grad,
        gain_parts[0],
        gain_parts[1],
        gain_parts[2],
        gain_parts[3],
        weight_grads[0],
        weight_grads[1],
        weight_grads[2],
        weight_grads[3],
        router_part,
        expert_grad[:, :ff].swapaxes(1, 2),
        expert_grad[:, ff : 2 * ff].swapaxes(1, 2),
        expert_grad[:, 2 * ff :],
    )


def solution(mesh):
    return jax.shard_map(
        on_device,
        mesh=mesh,
        in_specs=(
            P(("dp", "expert"), None),
            P(("dp", "expert"), None),
            P(("dp", "expert")),
            P(("dp", "expert")),
            P(("dp", "expert")),
            P(("dp", "expert")),
            P(("dp", "expert"), None),
            P(("dp", "expert"), None),
            P(("dp", "expert"), None),
            P(("dp", "expert"), None),
            P(("dp", "expert"), None),
            P("expert", None, "dp"),
            P("expert", None, "dp"),
            P("expert", "dp", None),
            P(("dp", "expert"), None),
            P(("dp", "expert"), None),
        ),
        out_specs=(
            P(("dp", "expert"), None),
            P(("dp", "expert"), None),
            P(("dp", "expert")),
            P(("dp", "expert")),
            P(("dp", "expert")),
            P(("dp", "expert")),
            P(("dp", "expert"), None),
            P(("dp", "expert"), None),
            P(("dp", "expert"), None),
            P(("dp", "expert"), None),
            P(("dp", "expert"), None),
            P("expert", None, "dp"),
            P("expert", None, "dp"),
            P("expert", "dp", None),
        ),
        check_vma=False,
    )
```

time: 2530 us -> 1140 us (0.45)
  waiting for transfers between devices: 1510 us -> 567 us
  blocking collectives: 341 us -> 0 us
  matrix products: 287 us -> 70 us
  Pallas kernels: 0 us -> 178 us
  local copies, waits for them, and re-layouts: 261 us -> 125 us
  starting transfers between devices: 22 us -> 62.2 us
  other arithmetic: 85.7 us -> 125 us
    all_to_all x4 -> x0, waiting for transfers between devices: 668 us -> none  [the longest x1 238 us: on_device(): lax.all_to_all(outgoing_grad, 'expert', split_axis=0, concat_axis=1, tile...]
    reduce_scatter x7 -> x0, waiting for transfers between devices: 612 us -> none  [the longest x1 187 us: on_device(): lax.psum_scatter(value_grad, ('dp', 'expert'), scatter_dimension=0, tiled...]
    ppermute x0 -> x91, waiting for transfers between devices: none -> 567 us  [the longest x70 306 us: swap(): return lax.ppermute(v, axis, [(i, i ^ bit) for i in range(size)])]
    all_gather x1 -> x0, blocking collectives: 258 us -> none  [on_device(): lax.all_gather(router_weight, ('dp', 'expert'), axis=0, tiled=True)]
    all_gather x7 -> x0, waiting for transfers between devices: 225 us -> none  [the longest x1 71.2 us: on_device(): lax.all_gather(query_weight, ('dp', 'expert'), axis=0, tiled=True)]
    dot_general x31 -> x16, matrix products: 285 us -> 64.1 us  [the longest x1 11.7 us: on_device(): jnp.einsum('tc,td->cd', context_full, branch_half, preferred_element_type...]
    pallas_call x0 -> x5, Pallas kernels: none -> 178 us  [the longest x1 63.3 us: experts_first(): pl.pallas_call(functools.partial(first_body, cap, ff, rb, nb, n_e), out_s...]
    gather x6 -> x0, local copies, waits for them, and re-layouts: 114 us -> none  [the longest x2 42 us: on_device(): out_upstream[pick]]
  transfers between devices with their start and end apart: 19 -> 91, of which waited for: 11 -> 42; matrix products, arithmetic and copies ran while one was open for 18% -> 23% of each run, Pallas kernels for 0% -> 11%
where the time goes in v1:
time: 1140 us; the launch traced here: 1130 us
  waiting for transfers between devices  567 us (50%)
  Pallas kernels  178 us (16%)
  local copies, waits for them, and re-layouts  125 us (11%)
  other arithmetic  125 us (11%)
  matrix products  70 us (6%)
  starting transfers between devices  62.2 us (5%)
    ppermute x70, waiting for transfers between devices, swap(): return lax.ppermute(v, axis, [(i, i ^ bit) for i in range(size)])  306 us
    ppermute x21, waiting for transfers between devices, ring(): lax.ppermute(v, 'expert', [(i, (i + 2) % owners) for i in range(owners)])  261 us
    pallas_call x1, Pallas kernels, experts_first(): pl.pallas_call(functools.partial(first_body, cap, ff, rb, nb, n_e), out_s...  63.3 us
    pallas_call x1, Pallas kernels, experts_last(): pl.pallas_call(functools.partial(last_body, cap, ff, rb, nb, n_e), out_sh...  57.5 us
    ppermute x70, starting transfers between devices, swap(): return lax.ppermute(v, axis, [(i, i ^ bit) for i in range(size)])  55.6 us
    unnamed x229, local copies, waits for them, and re-layouts  36.9 us
    pallas_call x2, Pallas kernels, expert_grads(): pl.pallas_call(functools.partial(grads_body, ff), out_shape=(side, side),...  30.8 us
    pallas_call x1, Pallas kernels, experts_mixture(): pl.pallas_call(functools.partial(mixture_body, cap, ff, nb, n_e), out_sha...  26.2 us
  transfers between devices with their start and end apart: 91, of which 42 were waited for; matrix products, arithmetic and copies ran while one was open for 23% of the time, Pallas kernels for 11%

profile of v1, /device:TPU:0, one launch (start us, length us, event | category | flops | bytes accessed | tf_op | source)
XLA Modules:
  0.0 1130.0 jit_solution(16083589211898106170)
XLA Ops:
  83.8 20.1 %collective-permute-done.13 = bf16[64,4096]{1,0:T(8,128)(2,1)S(1)} collective-permute-done((bf16[64,4096]{1,0:T(8,128)(2,1)S(1)}, bf16[64,4096]{1,0:T(8,128)(2,1)S(1)}, u32[]{:S(2)}, u32[]{:S(2)}) %collective-permute-start.13) | collective-permute-done | bytes 524320 | tf_op jit(solution)/shard_map/ppermute | solution.py:538
  110.0 28.5 %collective-permute-done.18 = bf16[64,4096]{1,0:T(8,128)(2,1)S(1)} collective-permute-done((bf16[64,4096]{1,0:T(8,128)(2,1)S(1)}, bf16[64,4096]{1,0:T(8,128)(2,1)S(1)}, u32[]{:S(2)}, u32[]{:S(2)}) %collective-permute-start.18) | collective-permute-done | bytes 524320 | tf_op jit(solution)/shard_map/ppermute | solution.py:538
  144.7 29.4 %collective-permute-done.22 = bf16[64,4096]{1,0:T(8,128)(2,1)S(1)} collective-permute-done((bf16[64,4096]{1,0:T(8,128)(2,1)S(1)}, bf16[64,4096]{1,0:T(8,128)(2,1)S(1)}, u32[]{:S(2)}, u32[]{:S(2)}) %collective-permute-start.22) | collective-permute-done | bytes 524320 | tf_op jit(solution)/shard_map/ppermute | solution.py:538
  176.4 7.0 collective-permute-done.25
  223.8 16.1 %collective-permute-done.33 = bf16[272,2048]{1,0:T(8,128)(2,1)} collective-permute-done((bf16[272,2048]{1,0:T(8,128)(2,1)}, bf16[272,2048]{1,0:T(8,128)(2,1)}, u32[]{:S(2)}, u32[]{:S(2)}) %collective-permute-start.33) | collective-permute-done | bytes 1114144 | tf_op jit(solution)/shard_map/ppermute | solution.py:544
  245.6 45.4 %collective-permute-done.31.rest_2_ = bf16[768,2048]{1,0:T(8,128)(2,1)} collective-permute-done((bf16[768,2048]{1,0:T(8,128)(2,1)}, bf16[768,2048]{1,0:T(8,128)(2,1)}, u32[]{:S(2)}, u32[]{:S(2)}) %collective-permute-start.31) | collective-permute-done | bytes 3145760 | tf_op jit(solution)/shard_map/ppermute | solution.py:538
  302.8 18.0 %collective-permute-done.36 = bf16[272,2048]{1,0:T(8,128)(2,1)} collective-permute-done((bf16[272,2048]{1,0:T(8,128)(2,1)}, bf16[272,2048]{1,0:T(8,128)(2,1)}, u32[]{:S(2)}, u32[]{:S(2)}) %collective-permute-start.36) | collective-permute-done | bytes 1114144 | tf_op jit(solution)/shard_map/ppermute | solution.py:544
  328.8 21.1 %collective-permute-done.39 = bf16[272,2048]{1,0:T(8,128)(2,1)S(1)} collective-permute-done((bf16[272,2048]{1,0:T(8,128)(2,1)}, bf16[272,2048]{1,0:T(8,128)(2,1)S(1)}, u32[]{:S(2)}, u32[]{:S(2)}) %collective-permute-start.39) | collective-permute-done | bytes 1114144 | tf_op jit(solution)/shard_map/ppermute | solution.py:544
  354.3 24.5 %collective-permute-done.42 = bf16[272,2048]{1,0:T(8,128)(2,1)S(1)} collective-permute-done((bf16[272,2048]{1,0:T(8,128)(2,1)S(1)}, bf16[272,2048]{1,0:T(8,128)(2,1)S(1)}, u32[]{:S(2)}, u32[]{:S(2)}) %collective-permute-start.42) | collective-permute-done | bytes 1114144 | tf_op jit(solution)/shard_map/ppermute | solution.py:544
  406.8 63.3 %shard_map.263 = (bf16[2,2,1280,2048]{3,2,1,0:T(8,128)(2,1)}, bf16[2,3,1280,768]{3,2,1,0:T(8,128)(2,1)}, f32[2,1280,1]{2,1,0:T(8,128)}, f32[2,1280,1]{2,1,0:T(8,...) custom-call(bf16[8,272,2048]{2,1,0:T(8,128)(2,1)} %copy-done.3, ...), custom_call_target="tpu_custom_call" | custom-call | tf_op jit(solution)/shard_map/pallas_call | solution.py:210
  470.4 57.5 %shard_map.264 = (bf16[2,3,1280,256]{3,2,1,0:T(8,128)(2,1)}, f32[2,8,1,256]{3,2,1,0:T(1,128)}, bf16[4,256,2048]{2,1,0:T(8,128)(2,1)}, bf16[4,256,2048]{2,1,0:T(8,128)(2,1)}) custom-call(bf16[2,2,1280,2048]{3,2,1,0:T(8,128)(2,1)} %get-tuple-element.214.rg_ref, bf16[2,3,1280,768]{3,2,1,0:T(8,128)(2,1)} %get-tuple-element.215.ha_ref.h_ref, ...), custom_call_target="tpu_custom_call" | custom-call | tf_op jit(solution)/shard_map/pallas_call | solution.py:375
  537.8 27.0 %collective-permute-done.57 = bf16[256,2048]{1,0:T(8,128)(2,1)S(1)} collective-permute-done((bf16[256,2048]{1,0:T(8,128)(2,1)S(1)}, bf16[256,2048]{1,0:T(8,128)(2,1)S(1)}, u32[]{:S(2)}, u32[]{:S(2)}) %collective-permute-start.57) | collective-permute-done | bytes 1048608 | tf_op jit(solution)/shard_map/ppermute | solution.py:544
  568.9 23.9 %collective-permute-done.58 = bf16[256,2048]{1,0:T(8,128)(2,1)S(1)} collective-permute-done((bf16[256,2048]{1,0:T(8,128)(2,1)S(1)}, bf16[256,2048]{1,0:T(8,128)(2,1)S(1)}, u32[]{:S(2)}, u32[]{:S(2)}) %collective-permute-start.58) | collective-permute-done | bytes 1048608 | tf_op jit(solution)/shard_map/ppermute | solution.py:544
  595.5 25.7 %collective-permute-done.54 = f32[16,256]{1,0:T(8,128)S(1)} collective-permute-done((f32[16,256]{1,0:T(8,128)S(1)}, f32[16,256]{1,0:T(8,128)S(1)}, u32[]{:S(2)}, u32[]{:S(2)}) %collective-permute-start.54) | collective-permute-done | bytes 16416 | tf_op jit(solution)/shard_map/ppermute | solution.py:544
  626.9 15.5 %shard_map.265 = (bf16[2,768,1024]{2,1,0:T(8,128)(2,1)}, bf16[2,768,1024]{2,1,0:T(8,128)(2,1)}) custom-call(bf16[2,3,1280,768]{3,2,1,0:T(8,128)(2,1)} %get-tuple-element.215.ha_ref.h_ref, bf16[2,2,1280,2048]{3,2,1,0:T(8,128)(2,1)} %get-tuple-element.214.rg_ref), custom_call_target="tpu_custom_call" | custom-call | tf_op jit(solution)/shard_map/pallas_call | solution.py:475
  642.4 15.3 %shard_map.267 = (bf16[2,768,1024]{2,1,0:T(8,128)(2,1)}, bf16[2,768,1024]{2,1,0:T(8,128)(2,1)}) custom-call(bf16[2,3,1280,256]{3,2,1,0:T(8,128)(2,1)} %get-tuple-element.228.hd_ref.h_ref, bf16[2,2,1280,2048]{3,2,1,0:T(8,128)(2,1)} %get-tuple-element.214.rg_ref), custom_call_target="tpu_custom_call" | custom-call | tf_op jit(solution)/shard_map/pallas_call | solution.py:475
  658.6 26.2 %shard_map.266 = (bf16[4,256,2048]{2,1,0:T(8,128)(2,1)}, bf16[4,256,2048]{2,1,0:T(8,128)(2,1)}) custom-call(bf16[2,3,1280,768]{3,2,1,0:T(8,128)(2,1)} %get-tuple-element.215.ha_ref.h_ref, bf16[2,3,1280,256]{3,2,1,0:T(8,128)(2,1)} %get-tuple-element.228.hd_ref.h_ref, bf16[768,2048]{1,0:T(8,128)(2,1)} %pad_maximum_fusion.2.rest_0_, ...), custom_call_target="tpu_custom_call" | custom-call | tf_op jit(solution)/shard_map/pallas_call | solution.py:433
  699.8 11.7 %convolution_convert_fusion.2 = bf16[2048,1024]{1,0:T(8,128)(2,1)} fusion(bf16[256,1024]{1,0:T(8,128)(2,1)S(1)} %collective-permute-done.62, bf16[256,1024]{1,0:T(8,128)(2,1)S(1)} %get-tuple-element.407, bf16[256,1024]{1,0:T(8,128)(2,1)S(1)} %copy-done.75, bf16[256,1024]{1,0:T(8,128)(2,1)S(1)} %copy-done.73, bf16[512,1024]{1,0:T(8,128)(2,1)S(1)} %bitcast.265, ...), kind=kOutput, calls=%fused_computation.29 | convolution fusion | flops 2165309440 | bytes 7340033 | tf_op jit(solution)/shard_map/tc,td->cd/dot_general | solution.py:837
  712.3 12.1 %collective-permute-done.64 = bf16[2,768,1024]{2,1,0:T(8,128)(2,1)} collective-permute-done((bf16[2,768,1024]{2,1,0:T(8,128)(2,1)}, bf16[2,768,1024]{2,1,0:T(8,128)(2,1)}, u32[]{:S(2)}, u32[]{:S(2)}) %collective-permute-start.64) | collective-permute-done | bytes 3145760 | tf_op jit(solution)/shard_map/ppermute | solution.py:538
  724.3 27.0 %collective-permute-done.65 = bf16[2,768,1024]{2,1,0:T(8,128)(2,1)} collective-permute-done((bf16[2,768,1024]{2,1,0:T(8,128)(2,1)}, bf16[2,768,1024]{2,1,0:T(8,128)(2,1)}, u32[]{:S(2)}, u32[]{:S(2)}) %collective-permute-start.65) | collective-permute-done | bytes 3145760 | tf_op jit(solution)/shard_map/ppermute | solution.py:538
  798.0 8.5 pad_maximum_fusion
  810.9 10.4 fusion.1
  824.4 6.9 convolution_convert_fusion
  831.3 29.5 %collective-permute-done.67 = bf16[2,768,1024]{2,1,0:T(8,128)(2,1)} collective-permute-done((bf16[2,768,1024]{2,1,0:T(8,128)(2,1)}, bf16[2,768,1024]{2,1,0:T(8,128)(2,1)}, u32[]{:S(2)}, u32[]{:S(2)}) %collective-permute-start.67) | collective-permute-done | bytes 3145760 | tf_op jit(solution)/shard_map/ppermute | solution.py:538
  885.0 33.2 %collective-permute-done.69 = bf16[512,2048]{1,0:T(8,128)(2,1)} collective-permute-done((bf16[512,2048]{1,0:T(8,128)(2,1)}, bf16[512,2048]{1,0:T(8,128)(2,1)}, u32[]{:S(2)}, u32[]{:S(2)}) %collective-permute-start.69) | collective-permute-done | bytes 2097184 | tf_op jit(solution)/shard_map/ppermute | solution.py:538
  927.9 22.7 %collective-permute-done.78 = bf16[256,2048]{1,0:T(8,128)(2,1)} collective-permute-done((bf16[256,2048]{1,0:T(8,128)(2,1)S(1)}, bf16[256,2048]{1,0:T(8,128)(2,1)}, u32[]{:S(2)}, u32[]{:S(2)}) %collective-permute-start.78) | collective-permute-done | bytes 1048608 | tf_op jit(solution)/shard_map/ppermute | solution.py:544
  958.3 18.3 %collective-permute-done.79 = bf16[256,2048]{1,0:T(8,128)(2,1)S(1)} collective-permute-done((bf16[256,2048]{1,0:T(8,128)(2,1)S(1)}, bf16[256,2048]{1,0:T(8,128)(2,1)S(1)}, u32[]{:S(2)}, u32[]{:S(2)}) %collective-permute-start.79) | collective-permute-done | bytes 1048608 | tf_op jit(solution)/shard_map/ppermute | solution.py:544
  979.7 17.6 %collective-permute-done.77 = f32[16,1280]{1,0:T(8,128)S(1)} collective-permute-done((f32[16,1280]{1,0:T(8,128)S(1)}, f32[16,1280]{1,0:T(8,128)S(1)}, u32[]{:S(2)}, u32[]{:S(2)}) %collective-permute-start.77) | collective-permute-done | bytes 81952 | tf_op jit(solution)/shard_map/ppermute | solution.py:538
  1003.1 18.7 %collective-permute-done.80 = bf16[256,2048]{1,0:T(8,128)(2,1)} collective-permute-done((bf16[256,2048]{1,0:T(8,128)(2,1)}, bf16[256,2048]{1,0:T(8,128)(2,1)}, u32[]{:S(2)}, u32[]{:S(2)}) %collective-permute-start.80) | collective-permute-done | bytes 1048608 | tf_op jit(solution)/shard_map/ppermute | solution.py:544
  1033.4 18.8 %collective-permute-done.83 = bf16[128,4096]{1,0:T(8,128)(2,1)S(1)} collective-permute-done((bf16[128,4096]{1,0:T(8,128)(2,1)S(1)}, bf16[128,4096]{1,0:T(8,128)(2,1)S(1)}, u32[]{:S(2)}, u32[]{:S(2)}) %collective-permute-start.83) | collective-permute-done | bytes 1048608 | tf_op jit(solution)/shard_map/ppermute | solution.py:544
  1058.6 17.6 %collective-permute-done.84 = bf16[128,4096]{1,0:T(8,128)(2,1)} collective-permute-done((bf16[128,4096]{1,0:T(8,128)(2,1)}, bf16[128,4096]{1,0:T(8,128)(2,1)}, u32[]{:S(2)}, u32[]{:S(2)}) %collective-permute-start.84) | collective-permute-done | bytes 1048608 | tf_op jit(solution)/shard_map/ppermute | solution.py:544
  1081.2 21.3 %collective-permute-done.86 = f32[4,1280]{1,0:T(4,128)S(1)} collective-permute-done((f32[4,1280]{1,0:T(4,128)S(1)}, f32[4,1280]{1,0:T(4,128)S(1)}, u32[]{:S(2)}, u32[]{:S(2)}) %collective-permute-start.86) | collective-permute-done | bytes 20512 | tf_op jit(solution)/shard_map/ppermute | solution.py:538
  (631 shorter events, 388.0 us)
Async XLA Ops:
  6.3 36.1 %collective-permute-start = (bf16[64,4096]{1,0:T(8,128)(2,1)}, bf16[64,4096]{1,0:T(8,128)(2,1)}, u32[]{:S(2)}, u32[]{:S(2)}) collective-permute-start(bf16[64,4096]{1,0:T(8,128)(2,1)} %pad_maximum_fusion.18), channel_id=1, source_target_pairs={{0,1},{1,0},{2,3},{3,2},{4,5},{5,4},{6,7},{7,6},{8,9},{9,8},{10,11... | collective-permute-start | bytes 1572872 | tf_op jit(solution)/shard_map/ppermute | solution.py:538
  69.9 34.7 %collective-permute-start.10 = (bf16[128,4096]{1,0:T(8,128)(2,1)}, bf16[128,4096]{1,0:T(8,128)(2,1)S(1)}, u32[]{:S(2)}, u32[]{:S(2)}) collective-permute-start(bf16[128,4096]{1,0:T(8,128)(2,1)} %collective-permute-done.9), channel_id=1, source_target_pairs={{0,8},{8,0},{16,24},{24,16},{1,9},{9,1},{17,25},{25,17},{2,10},{10... | collective-permute-start | bytes 3145736 | tf_op jit(solution)/shard_map/ppermute | solution.py:538
  70.4 34.2 %collective-permute-start.11 = (bf16[128,4096]{1,0:T(8,128)(2,1)}, bf16[128,4096]{1,0:T(8,128)(2,1)S(1)}, u32[]{:S(2)}, u32[]{:S(2)}) collective-permute-start(bf16[128,4096]{1,0:T(8,128)(2,1)} %collective-permute-done.9), channel_id=1, source_target_pairs={{0,16},{8,24},{16,0},{24,8},{1,17},{9,25},{17,1},{25,9},{2,18},{10... | collective-permute-start | bytes 3145736 | tf_op jit(solution)/shard_map/ppermute | solution.py:538
  70.9 33.7 %collective-permute-start.12 = (bf16[128,4096]{1,0:T(8,128)(2,1)}, bf16[128,4096]{1,0:T(8,128)(2,1)S(1)}, u32[]{:S(2)}, u32[]{:S(2)}) collective-permute-start(bf16[128,4096]{1,0:T(8,128)(2,1)} %collective-permute-done.9), channel_id=1, source_target_pairs={{0,2},{1,3},{2,4},{3,5},{4,6},{5,7},{6,0},{7,1},{8,10},{9,11},{10,... | collective-permute-start | bytes 3145736 | tf_op jit(solution)/shard_map/ppermute | solution.py:544
  104.6 34.6 %collective-permute-start.15 = (bf16[128,4096]{1,0:T(8,128)(2,1)S(1)}, bf16[128,4096]{1,0:T(8,128)(2,1)S(1)}, u32[]{:S(2)}, u32[]{:S(2)}) collective-permute-start(bf16[128,4096]{1,0:T(8,128)(2,1)S(1)} %collective-permute-done.12), channel_id=1, source_target_pairs={{0,8},{8,0},{16,24},{24,16},{1,9},{9,1},{17,25},{25,17},{2,10},{10... | collective-permute-start | bytes 3145736 | tf_op jit(solution)/shard_map/ppermute | solution.py:538
  139.1 34.9 %collective-permute-start.20 = (bf16[128,4096]{1,0:T(8,128)(2,1)S(1)}, bf16[128,4096]{1,0:T(8,128)(2,1)S(1)}, u32[]{:S(2)}, u32[]{:S(2)}) collective-permute-start(bf16[128,4096]{1,0:T(8,128)(2,1)S(1)} %collective-permute-done.17), channel_id=1, source_target_pairs={{0,8},{8,0},{16,24},{24,16},{1,9},{9,1},{17,25},{25,17},{2,10},{10... | collective-permute-start | bytes 3145736 | tf_op jit(solution)/shard_map/ppermute | solution.py:538
  220.2 70.7 %collective-permute-start.31 = (bf16[768,2048]{1,0:T(8,128)(2,1)}, bf16[768,2048]{1,0:T(8,128)(2,1)}, u32[]{:S(2)}, u32[]{:S(2)}) collective-permute-start(bf16[768,2048]{1,0:T(8,128)(2,1)} %pad_maximum_fusion.2.rest_0_), channel_id=1, source_target_pairs={{0,8},{8,0},{16,24},{24,16},{1,9},{9,1},{17,25},{25,17},{2,10},{10... | collective-permute-start | bytes 9437192 | tf_op jit(solution)/shard_map/ppermute | solution.py:538
  221.3 70.4 %collective-permute-start.32 = (bf16[768,2048]{1,0:T(8,128)(2,1)}, bf16[768,2048]{1,0:T(8,128)(2,1)}, u32[]{:S(2)}, u32[]{:S(2)}) collective-permute-start(bf16[768,2048]{1,0:T(8,128)(2,1)} %pad_maximum_fusion.2.rest_0_), channel_id=1, source_target_pairs={{0,16},{8,24},{16,0},{24,8},{1,17},{9,25},{17,1},{25,9},{2,18},{10... | collective-permute-start | bytes 9437192 | tf_op jit(solution)/shard_map/ppermute | solution.py:538
  239.9 51.9 %collective-permute-start.34 = (bf16[272,2048]{1,0:T(8,128)(2,1)}, bf16[272,2048]{1,0:T(8,128)(2,1)}, u32[]{:S(2)}, u32[]{:S(2)}) collective-permute-start(bf16[272,2048]{1,0:T(8,128)(2,1)} %collective-permute-done.33), channel_id=1, source_target_pairs={{0,2},{1,3},{2,4},{3,5},{4,6},{5,7},{6,0},{7,1},{8,10},{9,11},{10,... | collective-permute-start | bytes 3342344 | tf_op jit(solution)/shard_map/ppermute | solution.py:544
  292.5 97.6 %collective-permute-start.46 = (bf16[768,2048]{1,0:T(8,128)(2,1)}, bf16[768,2048]{1,0:T(8,128)(2,1)}, u32[]{:S(2)}, u32[]{:S(2)}) collective-permute-start(bf16[768,2048]{1,0:T(8,128)(2,1)} %pad_maximum_fusion.3.rest_1_), channel_id=1, source_target_pairs={{0,8},{8,0},{16,24},{24,16},{1,9},{9,1},{17,25},{25,17},{2,10},{10... | collective-permute-start | bytes 9437192 | tf_op jit(solution)/shard_map/ppermute | solution.py:538
  294.0 96.1 %collective-permute-start.47 = (bf16[768,2048]{1,0:T(8,128)(2,1)}, bf16[768,2048]{1,0:T(8,128)(2,1)}, u32[]{:S(2)}, u32[]{:S(2)}) collective-permute-start(bf16[768,2048]{1,0:T(8,128)(2,1)} %pad_maximum_fusion.3.rest_1_), channel_id=1, source_target_pairs={{0,16},{8,24},{16,0},{24,8},{1,17},{9,25},{17,1},{25,9},{2,18},{10... | collective-permute-start | bytes 9437192 | tf_op jit(solution)/shard_map/ppermute | solution.py:538
  392.8 77.4 %collective-permute-start.48 = (bf16[768,1024]{1,0:T(8,128)(2,1)}, bf16[768,1024]{1,0:T(8,128)(2,1)}, u32[]{:S(2)}, u32[]{:S(2)}) collective-permute-start(bf16[768,1024]{1,0:T(8,128)(2,1)} %slice.406), channel_id=1, source_target_pairs={{0,16},{8,24},{16,0},{24,8},{1,17},{9,25},{17,1},{25,9},{2,18},{10... | collective-permute-start | bytes 4718600 | tf_op jit(solution)/shard_map/ppermute | solution.py:538
  397.2 73.0 %collective-permute-start.49 = (bf16[768,1024]{1,0:T(8,128)(2,1)}, bf16[768,1024]{1,0:T(8,128)(2,1)}, u32[]{:S(2)}, u32[]{:S(2)}) collective-permute-start(bf16[768,1024]{1,0:T(8,128)(2,1)} %slice.407), channel_id=1, source_target_pairs={{0,16},{8,24},{16,0},{24,8},{1,17},{9,25},{17,1},{25,9},{2,18},{10... | collective-permute-start | bytes 4718600 | tf_op jit(solution)/shard_map/ppermute | solution.py:538
  400.1 70.0 %collective-permute-start.50 = (bf16[768,1024]{1,0:T(8,128)(2,1)}, bf16[768,1024]{1,0:T(8,128)(2,1)}, u32[]{:S(2)}, u32[]{:S(2)}) collective-permute-start(bf16[768,1024]{1,0:T(8,128)(2,1)} %slice.408), channel_id=1, source_target_pairs={{0,8},{8,0},{16,24},{24,16},{1,9},{9,1},{17,25},{25,17},{2,10},{10... | collective-permute-start | bytes 4718600 | tf_op jit(solution)/shard_map/ppermute | solution.py:538
  403.7 66.7 %collective-permute-start.51 = (bf16[768,1024]{1,0:T(8,128)(2,1)}, bf16[768,1024]{1,0:T(8,128)(2,1)}, u32[]{:S(2)}, u32[]{:S(2)}) collective-permute-start(bf16[768,1024]{1,0:T(8,128)(2,1)} %slice.409), channel_id=1, source_target_pairs={{0,8},{8,0},{16,24},{24,16},{1,9},{9,1},{17,25},{25,17},{2,10},{10... | collective-permute-start | bytes 4718600 | tf_op jit(solution)/shard_map/ppermute | solution.py:538
  566.6 121.8 %collective-permute-start.60 = (bf16[2,768,1024]{2,1,0:T(8,128)(2,1)}, bf16[2,768,1024]{2,1,0:T(8,128)(2,1)}, u32[]{:S(2)}, u32[]{:S(2)}) collective-permute-start(bf16[2,768,1024]{2,1,0:T(8,128)(2,1)} %get-tuple-element.224), channel_id=1, source_target_pairs={{0,8},{8,0},{16,24},{24,16},{1,9},{9,1},{17,25},{25,17},{2,10},{10... | collective-permute-start | bytes 9437192 | tf_op jit(solution)/shard_map/ppermute | solution.py:538
  567.6 120.8 %collective-permute-start.61 = (bf16[2,768,1024]{2,1,0:T(8,128)(2,1)}, bf16[2,768,1024]{2,1,0:T(8,128)(2,1)}, u32[]{:S(2)}, u32[]{:S(2)}) collective-permute-start(bf16[2,768,1024]{2,1,0:T(8,128)(2,1)} %get-tuple-element.225), channel_id=1, source_target_pairs={{0,16},{8,24},{16,0},{24,8},{1,17},{9,25},{17,1},{25,9},{2,18},{10... | collective-permute-start | bytes 9437192 | tf_op jit(solution)/shard_map/ppermute | solution.py:538
  595.5 90.8 %collective-permute-start.59 = (bf16[256,2048]{1,0:T(8,128)(2,1)}, bf16[256,2048]{1,0:T(8,128)(2,1)S(1)}, u32[]{:S(2)}, u32[]{:S(2)}) collective-permute-start(bf16[256,2048]{1,0:T(8,128)(2,1)} %fusion.49), channel_id=1, source_target_pairs={{0,2},{1,3},{2,4},{3,5},{4,6},{5,7},{6,0},{7,1},{8,10},{9,11},{10,... | collective-permute-start | bytes 3145736 | tf_op jit(solution)/shard_map/ppermute | solution.py:544
  626.8 58.0 %collective-permute-start.56 = (f32[16,256]{1,0:T(8,128)S(1)}, f32[16,256]{1,0:T(8,128)S(1)}, u32[]{:S(2)}, u32[]{:S(2)}) collective-permute-start(f32[16,256]{1,0:T(8,128)S(1)} %fusion.77), channel_id=1, source_target_pairs={{0,2},{1,3},{2,4},{3,5},{4,6},{5,7},{6,0},{7,1},{8,10},{9,11},{10,... | collective-permute-start | bytes 49160 | tf_op jit(solution)/shard_map/ppermute | solution.py:544
  657.7 66.6 %collective-permute-start.64 = (bf16[2,768,1024]{2,1,0:T(8,128)(2,1)}, bf16[2,768,1024]{2,1,0:T(8,128)(2,1)}, u32[]{:S(2)}, u32[]{:S(2)}) collective-permute-start(bf16[2,768,1024]{2,1,0:T(8,128)(2,1)} %get-tuple-element.233), channel_id=1, source_target_pairs={{0,8},{8,0},{16,24},{24,16},{1,9},{9,1},{17,25},{25,17},{2,10},{10... | collective-permute-start | bytes 9437192 | tf_op jit(solution)/shard_map/ppermute | solution.py:538
  684.9 66.4 %collective-permute-start.65 = (bf16[2,768,1024]{2,1,0:T(8,128)(2,1)}, bf16[2,768,1024]{2,1,0:T(8,128)(2,1)}, u32[]{:S(2)}, u32[]{:S(2)}) collective-permute-start(bf16[2,768,1024]{2,1,0:T(8,128)(2,1)} %get-tuple-element.234), channel_id=1, source_target_pairs={{0,16},{8,24},{16,0},{24,8},{1,17},{9,25},{17,1},{25,9},{2,18},{10... | collective-permute-start | bytes 9437192 | tf_op jit(solution)/shard_map/ppermute | solution.py:538
  698.7 186.4 %collective-permute-start.71 = (bf16[4,256,2048]{2,1,0:T(8,128)(2,1)}, bf16[4,256,2048]{2,1,0:T(8,128)(2,1)}, u32[]{:S(2)}, u32[]{:S(2)}) collective-permute-start(bf16[4,256,2048]{2,1,0:T(8,128)(2,1)} %get-tuple-element.243), channel_id=1, source_target_pairs={{0,1},{1,0},{2,3},{3,2},{4,5},{5,4},{6,7},{7,6},{8,9},{9,8},{10,11... | collective-permute-start | bytes 12582920 | tf_op jit(solution)/shard_map/ppermute | solution.py:538
  790.2 70.7 %collective-permute-start.67 = (bf16[2,768,1024]{2,1,0:T(8,128)(2,1)}, bf16[2,768,1024]{2,1,0:T(8,128)(2,1)}, u32[]{:S(2)}, u32[]{:S(2)}) collective-permute-start(bf16[2,768,1024]{2,1,0:T(8,128)(2,1)} %add_convert_fusion.1), channel_id=1, source_target_pairs={{0,16},{8,24},{16,0},{24,8},{1,17},{9,25},{17,1},{25,9},{2,18},{10... | collective-permute-start | bytes 9437192 | tf_op jit(solution)/shard_map/ppermute | solution.py:538
  796.5 70.4 %collective-permute-start.68 = (bf16[2,768,1024]{2,1,0:T(8,128)(2,1)}, bf16[2,768,1024]{2,1,0:T(8,128)(2,1)}, u32[]{:S(2)}, u32[]{:S(2)}) collective-permute-start(bf16[2,768,1024]{2,1,0:T(8,128)(2,1)} %add_convert_fusion), channel_id=1, source_target_pairs={{0,8},{8,0},{16,24},{24,16},{1,9},{9,1},{17,25},{25,17},{2,10},{10... | collective-permute-start | bytes 9437192 | tf_op jit(solution)/shard_map/ppermute | solution.py:538
  824.4 53.6 %collective-permute-start.72 = (bf16[256,2048]{1,0:T(8,128)(2,1)}, bf16[256,2048]{1,0:T(8,128)(2,1)}, u32[]{:S(2)}, u32[]{:S(2)}) collective-permute-start(bf16[256,2048]{1,0:T(8,128)(2,1)} %slice.687), channel_id=1, source_target_pairs={{0,1},{1,0},{2,3},{3,2},{4,5},{5,4},{6,7},{7,6},{8,9},{9,8},{10,11... | collective-permute-start | bytes 3145736 | tf_op jit(solution)/shard_map/ppermute | solution.py:538
  871.1 47.1 %collective-permute-start.69 = (bf16[512,2048]{1,0:T(8,128)(2,1)}, bf16[512,2048]{1,0:T(8,128)(2,1)}, u32[]{:S(2)}, u32[]{:S(2)}) collective-permute-start(bf16[512,2048]{1,0:T(8,128)(2,1)} %pad_maximum_fusion.9), channel_id=1, source_target_pairs={{0,8},{8,0},{16,24},{24,16},{1,9},{9,1},{17,25},{25,17},{2,10},{10... | collective-permute-start | bytes 6291464 | tf_op jit(solution)/shard_map/ppermute | solution.py:538
  876.8 46.8 %collective-permute-start.70 = (bf16[512,2048]{1,0:T(8,128)(2,1)}, bf16[512,2048]{1,0:T(8,128)(2,1)}, u32[]{:S(2)}, u32[]{:S(2)}) collective-permute-start(bf16[512,2048]{1,0:T(8,128)(2,1)} %pad_maximum_fusion.10), channel_id=1, source_target_pairs={{0,16},{8,24},{16,0},{24,8},{1,17},{9,25},{17,1},{25,9},{2,18},{10... | collective-permute-start | bytes 6291464 | tf_op jit(solution)/shard_map/ppermute | solution.py:538
  926.0 99.3 %collective-permute-start.75 = (bf16[512,2048]{1,0:T(8,128)(2,1)S(1)}, bf16[512,2048]{1,0:T(8,128)(2,1)S(1)}, u32[]{:S(2)}, u32[]{:S(2)}) collective-permute-start(bf16[512,2048]{1,0:T(8,128)(2,1)S(1)} %pad_maximum_fusion.11), channel_id=1, source_target_pairs={{0,8},{8,0},{16,24},{24,16},{1,9},{9,1},{17,25},{25,17},{2,10},{10... | collective-permute-start | bytes 6291464 | tf_op jit(solution)/shard_map/ppermute | solution.py:538
  927.5 97.8 %collective-permute-start.76 = (bf16[512,2048]{1,0:T(8,128)(2,1)S(1)}, bf16[512,2048]{1,0:T(8,128)(2,1)S(1)}, u32[]{:S(2)}, u32[]{:S(2)}) collective-permute-start(bf16[512,2048]{1,0:T(8,128)(2,1)S(1)} %pad_maximum_fusion.12), channel_id=1, source_target_pairs={{0,16},{8,24},{16,0},{24,8},{1,17},{9,25},{17,1},{25,9},{2,18},{10... | collective-permute-start | bytes 6291464 | tf_op jit(solution)/shard_map/ppermute | solution.py:538
  954.4 70.8 %collective-permute-start.73 = (bf16[256,2048]{1,0:T(8,128)(2,1)S(1)}, bf16[256,2048]{1,0:T(8,128)(2,1)S(1)}, u32[]{:S(2)}, u32[]{:S(2)}) collective-permute-start(bf16[256,2048]{1,0:T(8,128)(2,1)S(1)} %add_convert_fusion.7), channel_id=1, source_target_pairs={{0,16},{8,24},{16,0},{24,8},{1,17},{9,25},{17,1},{25,9},{2,18},{10... | collective-permute-start | bytes 3145736 | tf_op jit(solution)/shard_map/ppermute | solution.py:538
  957.4 67.9 %collective-permute-start.74 = (bf16[256,2048]{1,0:T(8,128)(2,1)}, bf16[256,2048]{1,0:T(8,128)(2,1)S(1)}, u32[]{:S(2)}, u32[]{:S(2)}) collective-permute-start(bf16[256,2048]{1,0:T(8,128)(2,1)} %add_convert_fusion.6), channel_id=1, source_target_pairs={{0,8},{8,0},{16,24},{24,16},{1,9},{9,1},{17,25},{25,17},{2,10},{10... | collective-permute-start | bytes 3145736 | tf_op jit(solution)/shard_map/ppermute | solution.py:538
  1081.2 37.0 %collective-permute-start.89 = (bf16[128,4096]{1,0:T(8,128)(2,1)}, bf16[128,4096]{1,0:T(8,128)(2,1)S(1)}, u32[]{:S(2)}, u32[]{:S(2)}) collective-permute-start(bf16[128,4096]{1,0:T(8,128)(2,1)} %fusion.41), channel_id=1, source_target_pairs={{0,2},{1,3},{2,4},{3,5},{4,6},{5,7},{6,0},{7,1},{8,10},{9,11},{10,... | collective-permute-start | bytes 3145736 | tf_op jit(solution)/shard_map/ppermute | solution.py:544
  (166 other events, 3060.1 us)

commit v2 on v0

v2 whole, which is shorter than its diff:
```python
import functools
import math

import jax
import jax.numpy as jnp
from jax import lax
from jax.experimental import pallas as pl
from jax.experimental.layout import Layout, with_layout_constraint
from jax.experimental.pallas import tpu as pltpu
from jax.sharding import PartitionSpec as P

HD = 128


epsilon = 1e-05
rope_base = 10000.0
masked_score = -1e30


def rotary_tables(segments, head_size):
    length = segments.shape[-1]
    order = jnp.arange(length, dtype=jnp.int32)
    starts = jnp.sum((segments[..., None, :] < segments[..., :, None]).astype(jnp.int32), axis=-1)
    position = (order - starts).astype(jnp.float32)
    frequency = rope_base ** (-2.0 * jnp.arange(head_size // 2, dtype=jnp.float32) / head_size)
    angle = position[..., None] * frequency
    return (jnp.cos(angle), jnp.sin(angle))


VMEM_BYTES = 60 * 1024 * 1024


def dot_nt(a, b):
    return lax.dot_general(a, b, (((1,), (1,)), ((), ())), preferred_element_type=jnp.float32)


def dot_nn(a, b):
    return lax.dot_general(a, b, (((1,), (0,)), ((), ())), preferred_element_type=jnp.float32)


def dot_tn(a, b):
    return lax.dot_general(a, b, (((0,), (0,)), ((), ())), preferred_element_type=jnp.float32)


def flat(shards):
    return [v for pair in shards for side in pair for v in side]


def counts(shards):
    return tuple(tuple(len(side) for side in pair) for pair in shards)


def unflat(refs, shape):
    out, at = [], 0
    for pair in shape:
        sides = []
        for n in pair:
            sides.append(refs[at : at + n])
            at += n
        out.append(sides)
    return out, refs[at:]


def third(side, i, e, ff):
    for ref in side:
        n = ref.shape[1] // ff
        if i < n:
            return ref.at[e, pl.ds(i * ff, ff)]
        i -= n


def block(start, size):
    return pl.ds(pl.multiple_of(start * size, size), size)


def swiglu(gate_pre, up_pre, back, gate):
    sig = 1.0 / (1.0 + jnp.exp(-gate_pre))
    act = gate_pre * sig
    hid = act * up_pre
    scaled = back * gate
    return (
        jnp.sum(hid * back, axis=1, keepdims=True),
        (scaled * up_pre * (sig + act * (1.0 - sig))).astype(jnp.bfloat16),
        (scaled * act).astype(jnp.bfloat16),
        (hid * gate).astype(jnp.bfloat16),
    )


def first_body(cap, ff, rb, nb, src, team, shape, pieces, *rest):
    xr, gr, rest = rest[:src], rest[src : 2 * src], rest[2 * src :]
    shards, rest = unflat(rest, shape)
    rr_ref, gt_ref, rg_ref, h_ref, gate_ref, dgr_ref = rest[:6]
    k = len(pieces)
    sx, kx, ky, sy, rest = rest[6 : 6 + k], rest[6 + k], rest[7 + k], rest[8 + k : 8 + 2 * k], rest[8 + 2 * k :]
    (p, xs, gs, r, g, hb, dp, p_sem, in_sem, rg_sem, h_sem, d_sem) = rest
    n_e, _, _, tok = rr_ref.shape
    rows, width = r.shape[1:]
    half = width // 2

    def load(f, e, slot):
        return [
            pltpu.make_async_copy(
                third(shards[f][j], i, e, ff), p.at[slot, pl.ds(i * ff, ff), pl.ds(j * half, half)], p_sem.at[slot, 3 * j + i]
            )
            for j in range(2)
            for i in range(3)
        ]

    for c in load(0, 0, 0):
        c.start()

    def fetch(k, j, slot):
        return (
            pltpu.make_async_copy(xr[k].at[pl.ds(0, tok)], xs.at[slot, j], in_sem.at[0, slot, j]),
            pltpu.make_async_copy(gr[k].at[pl.ds(0, tok)], gs.at[slot, j], in_sem.at[1, slot, j]),
        )

    def fetch_start(s, slot):
        for k in range(src):

            @pl.when(s == k // team)
            def _():
                for c in fetch(k, k % team, slot):
                    c.start()

    fetch_start(0, 0)

    @pl.loop(0, src // team)
    def _(s):
        slot = lax.rem(s, 2)

        @pl.when(s + 1 < src // team)
        def _():
            fetch_start(s + 1, 1 - slot)

        for j in range(team):
            for c in fetch(j, j, slot):
                c.wait()
        got = [[[], [], []] for _ in range(n_e)]
        for j in range(team):
            hits = [lax.broadcasted_iota(jnp.int32, (cap, tok), 0) == rr_ref[e, s * team + j] for e in range(n_e)]
            one = jnp.concatenate([hit.astype(jnp.float32) for hit in hits], axis=0).astype(jnp.bfloat16)
            rx, rg = dot_nn(one, xs[slot, j]), dot_nn(one, gs[slot, j])
            for e in range(n_e):
                got[e][0].append(rx[e * cap : (e + 1) * cap])
                got[e][1].append(rg[e * cap : (e + 1) * cap])
                got[e][2].append(jnp.sum(jnp.where(hits[e], gt_ref[e, s * team + j], 0.0), axis=1, keepdims=True))
        at = block(s, team * cap)
        for e in range(n_e):
            a, b, c = [v[0] if team == 1 else jnp.concatenate(v, axis=0) for v in got[e]]
            r[e, at, :] = a.astype(jnp.bfloat16)
            g[e, at, :] = b.astype(jnp.bfloat16)
            gate_ref[e, at, :] = c

    keep = []
    for e in range(n_e):
        for i, v in enumerate((r, g)):
            c = pltpu.make_async_copy(v.at[e], rg_ref.at[e, i], rg_sem.at[e, i])
            c.start()
            keep.append(c)
    dgr_ref[...] = jnp.zeros_like(dgr_ref)

    def put_h(f, e, slot):
        return pltpu.make_async_copy(hb.at[slot], h_ref.at[e, :, :, pl.ds(f * ff, ff)], h_sem.at[slot])

    def put_d(f, e, slot):
        kept, j, sent = ((kx, 1, sx), (ky, 0, sy))[f - 1]
        other = dp.at[slot, :, pl.ds(j * half, half)]
        return [pltpu.make_async_copy(other, kept.at[e], d_sem.at[len(pieces), slot])] + [
            pltpu.make_async_copy(
                dp.at[slot, pl.ds(at, n), pl.ds((1 - j) * half, half)], sent[i].at[e], d_sem.at[i, slot]
            )
            for i, (at, n) in enumerate(pieces)
        ]

    for f in range(3):
        for e in range(n_e):
            slot = e % 2
            following = load(f, e + 1, 1 - slot) if e + 1 < n_e else load(f + 1, 0, 1 - slot) if f < 2 else []
            for c in following:
                c.start()
            for c in load(f, e, slot):
                c.wait()
            if f > 0:
                put_h(f - 1, e, slot).wait()

            @pl.loop(0, rows // rb)
            def _(m):
                at = block(m, rb)
                pre = dot_nt(r[e, at, :], p[slot, pl.ds(0, 2 * ff), :])
                back = dot_nt(g[e, at, :], p[slot, pl.ds(2 * ff, ff), :])
                total, a, b, c = swiglu(pre[:, :ff], pre[:, ff:], back, gate_ref[e, at, :])
                dgr_ref[e, at, :] += total
                hb[slot, 0, at, :] = a
                hb[slot, 1, at, :] = b
                hb[slot, 2, at, :] = c

            put_h(f, e, slot).start()
            if f > 0:
                if f > 1:
                    for c in put_d(f - 1, e, slot):
                        c.wait()
                both = jnp.concatenate([hb[slot, 0], hb[slot, 1]], axis=1)

                @pl.loop(0, width // nb)
                def _(n):
                    at = block(n, nb)
                    dp[slot, 0 : 2 * ff, at] = dot_tn(both, r[e, :, at]).astype(jnp.bfloat16)
                    dp[slot, 2 * ff : 3 * ff, at] = dot_tn(hb[slot, 2], g[e, :, at]).astype(jnp.bfloat16)

                for c in put_d(f, e, slot):
                    c.start()
    for e in range(n_e):
        put_h(2, e, e % 2).wait()
        for c in put_d(2, e, e % 2):
            c.wait()
    for c in keep:
        c.wait()


def experts_first(xs, gs, shards, ff, rr, gt, cap, pieces, rb=640, nb=1024):
    n_e, src, _, tok = rr.shape
    width = xs[0].shape[1]
    shape = counts(shards)
    rows = src * cap
    team = 16 // math.gcd(cap, 16)
    bf, f32 = jnp.bfloat16, jnp.float32
    anys, vm = pl.BlockSpec(memory_space=pl.ANY), pl.BlockSpec(memory_space=pltpu.VMEM)
    part = jax.ShapeDtypeStruct((n_e, 3 * ff, width // 2), bf)
    ones = [jax.ShapeDtypeStruct((n_e, n, width // 2), bf) for _, n in pieces]
    outs = pl.pallas_call(
        functools.partial(first_body, cap, ff, rb, nb, src, team, shape, pieces),
        out_shape=(
            jax.ShapeDtypeStruct((n_e, 2, rows, width), bf),
            jax.ShapeDtypeStruct((n_e, 3, rows, 3 * ff), bf),
            jax.ShapeDtypeStruct((n_e, rows, 1), f32),
            jax.ShapeDtypeStruct((n_e, rows, 1), f32),
            *ones, part, part, *ones,
        ),
        in_specs=[anys] * (2 * src + len(flat(shards))) + [vm] * 2,
        out_specs=(anys, anys, vm, vm) + (anys,) * (2 + 2 * len(pieces)),
        scratch_shapes=[
            pltpu.VMEM((2, 3 * ff, width), bf),
            pltpu.VMEM((2, team, tok, width), bf),
            pltpu.VMEM((2, team, tok, width), bf),
            pltpu.VMEM((n_e, rows, width), bf),
            pltpu.VMEM((n_e, rows, width), bf),
            pltpu.VMEM((2, 3, rows, ff), bf),
            pltpu.VMEM((2, 3 * ff, width), bf),
            pltpu.SemaphoreType.DMA((2, 6)),
            pltpu.SemaphoreType.DMA((2, 2, team)),
            pltpu.SemaphoreType.DMA((n_e, 2)),
            pltpu.SemaphoreType.DMA((2,)),
            pltpu.SemaphoreType.DMA((len(pieces) + 1, 2)),
        ],
        compiler_params=pltpu.CompilerParams(vmem_limit_bytes=VMEM_BYTES),
    )(*xs, *gs, *flat(shards), rr, gt)
    k = len(pieces)
    return *outs[:4], outs[4 : 4 + k], outs[4 + k], outs[5 + k], outs[6 + k :]


def tile_width(src):
    return 512 if src <= 8 else 128


def plan_body(n_prob, top, number_ref, *rest):
    src = (len(rest) - 9) // 2
    xr, gr, rest = rest[:src], rest[src : 2 * src], rest[2 * src :]
    row_ref, col_ref, gate_ref, mx, gx, probs, sems, gate_sem, rank = rest
    n_e, _, _, tok = row_ref.shape
    width = mx.shape[2]
    copies = []
    for s in range(src):
        copies.append(pltpu.make_async_copy(xr[s].at[pl.ds(tok, mx.shape[1])], mx.at[s], sems.at[s]))
        copies.append(pltpu.make_async_copy(gr[s].at[pl.ds(tok, gx.shape[1])], gx.at[s], gate_sem.at[s]))
    for c in copies:
        c.start()
    for c in copies:
        c.wait()
    for s in range(src):
        line = gx[s].astype(jnp.float32)
        both = mx[s].astype(jnp.float32)
        probs[s] = both[0:n_prob] + both[n_prob : 2 * n_prob]
        for e in range(n_e):
            number = number_ref[0] + e
            hit = None
            for k in range(top):
                at = k * tok
                same = line[at // width : at // width + 1, at % width : at % width + tok] == number.astype(jnp.float32)
                hit = same if hit is None else hit | same
            rank[e * src + s : e * src + s + 1, :] = hit.astype(jnp.float32)
            at = number * tok
            gate_ref[e, s] = probs[s, pl.ds(at // width, 1), pl.ds(pl.multiple_of(lax.rem(at, width), tok), tok)]
    lower = lax.broadcasted_iota(jnp.int32, (tok, tok), 0) <= lax.broadcasted_iota(jnp.int32, (tok, tok), 1)
    hits = rank[...]
    places = dot_nn(hits.astype(jnp.bfloat16), lower.astype(jnp.float32).astype(jnp.bfloat16))
    places = jnp.where(hits > 0.0, places - 1.0, -1.0)
    col_ref[...] = places.T.astype(jnp.int32)
    for e in range(n_e):
        for s in range(src):
            i = e * src + s
            row_ref[e, s] = places[i : i + 1].astype(jnp.int32)


def plan(number, xs, gs, n_prob, top, n_e, tok):
    src, width = len(xs), xs[0].shape[1]
    anys, vm = pl.BlockSpec(memory_space=pl.ANY), pl.BlockSpec(memory_space=pltpu.VMEM)
    bf, f32 = jnp.bfloat16, jnp.float32
    return pl.pallas_call(
        functools.partial(plan_body, n_prob, top),
        out_shape=(
            jax.ShapeDtypeStruct((n_e, src, 1, tok), jnp.int32),
            jax.ShapeDtypeStruct((tok, n_e * src), jnp.int32),
            jax.ShapeDtypeStruct((n_e, src, 1, tok), f32),
        ),
        in_specs=[pl.BlockSpec(memory_space=pltpu.SMEM)] + [anys] * (2 * src),
        out_specs=(vm, vm, vm),
        scratch_shapes=[
            pltpu.VMEM((src, xs[0].shape[0] - tok, width), bf),
            pltpu.VMEM((src, gs[0].shape[0] - tok, width), bf),
            pltpu.VMEM((src, n_prob, width), f32),
            pltpu.SemaphoreType.DMA((src,)),
            pltpu.SemaphoreType.DMA((src,)),
            pltpu.VMEM((n_e * src, tok), f32),
        ],
        compiler_params=pltpu.CompilerParams(vmem_limit_bytes=VMEM_BYTES),
    )(number, *xs, *gs)


def last_body(ff, rb, nb, shape, pieces, rg_ref, gate_ref, dgr_in, *rest):
    (side,), rest = unflat(rest, shape)
    k = len(pieces)
    hd_ref, dgr_ref, low, high, rest = rest[0], rest[1], rest[2 : 2 + k], rest[2 + k : 2 + 2 * k], rest[2 + 2 * k :]
    p, r, g, hb, ht, dp, p_sem, rg_sem, h_sem, d_sem = rest
    n_e, rows, width = r.shape
    half = width // 2
    weights, loads = [], []
    for e in range(n_e):
        weights.append([
            pltpu.make_async_copy(
                third(side[j], i, e, ff), p.at[e, pl.ds(i * ff, ff), pl.ds(j * half, half)], p_sem.at[e, 3 * j + i])
            for j in range(2) for i in range(3)
        ])
        loads.append([[
            pltpu.make_async_copy(rg_ref.at[e, i, pl.ds(m * rb, rb)], v.at[e, pl.ds(m * rb, rb)], rg_sem.at[e, i, m])
            for i, v in enumerate((r, g))] for m in range(rows // rb)])
    def begin(e):
        for c in weights[e] + [c for m in loads[e] for c in m]:
            c.start()

    begin(0)
    outs = []
    for e in range(n_e):
        for c in weights[e]:
            c.wait()
        if e + 1 < n_e:
            begin(e + 1)
        for m in range(rows // rb):
            for c in loads[e][m]:
                c.wait()
            at = pl.ds(m * rb, rb)
            pre = dot_nt(r[e, at, :], p[e, pl.ds(0, 2 * ff), :])
            back = dot_nt(g[e, at, :], p[e, pl.ds(2 * ff, ff), :])
            total, a, b, c = swiglu(pre[:, :ff], pre[:, ff:], back, gate_ref[e, at, :])
            dgr_ref[e, at, :] = dgr_in[e, at, :] + total
            hb[e, 0, at, :] = a
            hb[e, 1, at, :] = b
            hb[e, 2, at, :] = c
        c = pltpu.make_async_copy(hb.at[e], hd_ref.at[e], h_sem.at[e])
        c.start()
        outs.append(c)
        for i in range(3):
            ht[pl.ds(i * ff, ff), :] = hb[e, i].T

        @pl.loop(0, width // nb)
        def _(n):
            at = block(n, nb)
            dp[e, 0 : 2 * ff, at] = dot_nn(ht[0 : 2 * ff, :], r[e, :, at]).astype(jnp.bfloat16)
            dp[e, 2 * ff : 3 * ff, at] = dot_nn(ht[2 * ff : 3 * ff, :], g[e, :, at]).astype(jnp.bfloat16)

        for j, refs in enumerate((low, high)):
            for i, (at, n) in enumerate(pieces):
                c = pltpu.make_async_copy(
                    dp.at[e, pl.ds(at, n), pl.ds(j * half, half)], refs[i].at[e], d_sem.at[e, len(pieces) * j + i]
                )
                c.start()
                outs.append(c)
    for c in outs:
        c.wait()


def experts_last(rg, gate, dgr, side, ff, pieces, rb=640, nb=1024):
    n_e, _, rows, width = rg.shape
    shape = counts((side,))
    bf, f32 = jnp.bfloat16, jnp.float32
    anys, vm = pl.BlockSpec(memory_space=pl.ANY), pl.BlockSpec(memory_space=pltpu.VMEM)
    parts = [jax.ShapeDtypeStruct((n_e, n, width // 2), bf) for _, n in pieces]
    outs = pl.pallas_call(
        functools.partial(last_body, ff, rb, nb, shape, pieces),
        out_shape=(
            jax.ShapeDtypeStruct((n_e, 3, rows, ff), bf),
            jax.ShapeDtypeStruct((n_e, rows, 1), f32),
            *parts, *parts,
        ),
        in_specs=[anys] + [vm] * 2 + [anys] * len(flat((side,))),
        out_specs=(anys, vm) + (anys,) * (2 * len(pieces)),
        scratch_shapes=[
            pltpu.VMEM((n_e, 3 * ff, width), bf),
            pltpu.VMEM((n_e, rows, width), bf),
            pltpu.VMEM((n_e, rows, width), bf),
            pltpu.VMEM((n_e, 3, rows, ff), bf),
            pltpu.VMEM((3 * ff, rows), bf),
            pltpu.VMEM((n_e, 3 * ff, width), bf),
            pltpu.SemaphoreType.DMA((n_e, 6)),
            pltpu.SemaphoreType.DMA((n_e, 2, rows // rb)),
            pltpu.SemaphoreType.DMA((n_e,)),
            pltpu.SemaphoreType.DMA((n_e, 2 * len(pieces))),
        ],
        compiler_params=pltpu.CompilerParams(vmem_limit_bytes=VMEM_BYTES),
    )(rg, gate, dgr, *flat((side,)))
    k = len(pieces)
    return outs[0], outs[1], outs[2 : 2 + k], outs[2 + k :]


def spread_body(cap, ff, nb, shape, kinds, zs, extra, number_ref, ha_ref, hd_ref, dgr, *rest):
    shards, rest = unflat(rest, shape)
    rr_ref, cols_ref, own_ref, sib_ref, p, h, dg, acc, stage, p_sem, h_sem, st_sem = rest
    n_e = ha_ref.shape[0]
    width = p.shape[2]
    half = width // 2
    hidden = 4 * ff
    src, tok, tall = rr_ref.shape[1], rr_ref.shape[3], stage.shape[3]
    tiles = width // nb
    loads = []
    for e in range(n_e):
        copies = []
        loads.append(copies)
        for i, kind in enumerate(kinds):
            for q in range(4):
                for j in range(2):
                    copies.append(pltpu.make_async_copy(
                        third(shards[q][j], kind, e, ff),
                        p.at[e, pl.ds(i * hidden + q * ff, ff), pl.ds(j * half, half)], p_sem.at[e, i, 2 * q + j]))
            for m, z in enumerate(zs):
                at, to = pl.ds(2 * z * cap, 2 * cap), pl.ds(2 * m * cap, 2 * cap)
                copies.append(pltpu.make_async_copy(
                    ha_ref.at[e, kind, at], h.at[e, to, pl.ds(i * hidden, 3 * ff)], h_sem.at[e, i, m, 0]))
                copies.append(pltpu.make_async_copy(
                    hd_ref.at[e, kind, at], h.at[e, to, pl.ds(i * hidden + 3 * ff, ff)], h_sem.at[e, i, m, 1]))
    for copies in loads:
        for c in copies:
            c.start()
    if extra:
        for e in range(n_e):
            for m, z in enumerate(zs):
                for w in range(2):
                    s = 2 * z + w
                    hit = lax.broadcasted_iota(jnp.int32, (cap, tok), 0) == rr_ref[e, s]
                    dg[e, 2 * m + w] = jnp.sum(
                        jnp.where(hit, dgr[e, pl.ds(s * cap, cap), :], 0.0), axis=0, keepdims=True)

    def extras(n, s):
        shape = (tall - tok, nb)
        line = lax.broadcasted_iota(jnp.int32, shape, 0)
        place = n * nb + lax.broadcasted_iota(jnp.int32, shape, 1)
        total = jnp.zeros(shape, jnp.float32)
        for e in range(n_e):
            v = dg[e, s]
            if nb >= tok:
                v = jnp.concatenate([v] * (nb // tok), axis=1)
            else:
                v = jnp.where(lax.rem(n, 2) == 0, v[:, :nb], v[:, nb:])
            at = (number_ref[0] + e) * tok
            inside = (place >= lax.rem(at, width)) & (place < lax.rem(at, width) + tok)
            low = v.astype(jnp.bfloat16).astype(jnp.float32)
            row = at // width
            total = jnp.where(inside & (line == row), low, total)
            total = jnp.where(inside & (line == row + extra), v - low, total)
        return total.astype(jnp.bfloat16)

    def put(n, slot):
        return [
            pltpu.make_async_copy(stage.at[slot, w], ref.at[:, :, block(n, nb)], st_sem.at[slot, w])
            for w, ref in enumerate((own_ref, sib_ref))
        ]

    def column(e, s):
        i = e * src + s
        if isinstance(s, int):
            return cols_ref[:, i : i + 1]
        lane = lax.broadcasted_iota(jnp.int32, cols_ref.shape, 1)
        return jnp.sum(jnp.where(lane == i, cols_ref[...], 0), axis=1, keepdims=True)

    @pl.loop(0, tiles)
    def _(n):
        slot = lax.rem(n, 2)
        for e in range(n_e):

            @pl.when(n == 0)
            def _():
                for c in loads[e]:
                    c.wait()

            acc[e] = dot_nn(h[e], p[e, :, block(n, nb)])

        @pl.when(n >= 2)
        def _():
            for c in put(n, slot):
                c.wait()

        def one(m, z, w):
            hits = [
                (lax.broadcasted_iota(jnp.int32, (tok, cap), 1) == column(e, 2 * z + w)).astype(jnp.float32)
                for e in range(n_e)
            ]
            hit = jnp.concatenate(hits, axis=1).astype(jnp.bfloat16)
            s = 2 * m + w
            part = jnp.concatenate([acc[e, block(s, cap)] for e in range(n_e)], axis=0).astype(jnp.bfloat16)
            stage[slot, w, m, 0:tok, :] = dot_nn(hit, part).astype(jnp.bfloat16)
            if extra:
                stage[slot, w, m, tok:tall, :] = extras(n, s)

        if len(zs) <= 4:
            for m, z in enumerate(zs):
                for w in range(2):
                    one(m, z, w)
        else:

            @pl.loop(0, len(zs))
            def _(m):
                z = lax.rem(m + zs[0], src // 2)
                for w in range(2):
                    one(m, z, w)

        for c in put(n, slot):
            c.start()

    for slot in range(2):
        for c in put(slot, slot):
            c.wait()


def experts_spread(number, ha, hd, dgr, shards, ff, width, rr, cols, cap, kinds, zs, gates):
    n_e, src, _, tok = rr.shape
    nb = tile_width(src)
    extra = n_e * src * tok // width if gates else 0
    tall = tok + 2 * extra + -2 * extra % 16
    shape = counts(shards)
    rows = 2 * len(zs) * cap
    bf, f32 = jnp.bfloat16, jnp.float32
    anys, vm = pl.BlockSpec(memory_space=pl.ANY), pl.BlockSpec(memory_space=pltpu.VMEM)
    side = jax.ShapeDtypeStruct((len(zs), tall, width), bf)
    return pl.pallas_call(
        functools.partial(spread_body, cap, ff, nb, shape, kinds, zs, extra),
        out_shape=(side, side),
        in_specs=[pl.BlockSpec(memory_space=pltpu.SMEM), anys, anys, vm] + [anys] * len(flat(shards)) + [vm, vm],
        out_specs=(anys, anys),
        scratch_shapes=[
            pltpu.VMEM((n_e, 4 * ff * len(kinds), width), bf),
            pltpu.VMEM((n_e, rows, 4 * ff * len(kinds)), bf),
            pltpu.VMEM((n_e, 2 * len(zs), 1, tok), f32),
            pltpu.VMEM((n_e, rows, nb), f32),
            pltpu.VMEM((2, 2, len(zs), tall, nb), bf),
            pltpu.SemaphoreType.DMA((n_e, len(kinds), 8)),
            pltpu.SemaphoreType.DMA((n_e, len(kinds), len(zs), 2)),
            pltpu.SemaphoreType.DMA((2, 2)),
        ],
        compiler_params=pltpu.CompilerParams(vmem_limit_bytes=VMEM_BYTES),
    )(number, ha, hd, dgr, *flat(shards), rr, cols)


def grads_body(ff, h_ref, rg_ref, low, high, ht):
    part = pl.program_id(1)

    @pl.when(part == 0)
    def _():
        for i in range(3):
            ht[pl.ds(i * ff, ff), :] = h_ref[0, i].T

    def out(ref):
        ref[0, 0 : 2 * ff, :] = dot_nn(ht[0 : 2 * ff, :], rg_ref[0, 0]).astype(jnp.bfloat16)
        ref[0, 2 * ff : 3 * ff, :] = dot_nn(ht[2 * ff : 3 * ff, :], rg_ref[0, 1]).astype(jnp.bfloat16)

    @pl.when(part == 0)
    def _():
        out(low)

    @pl.when(part == 1)
    def _():
        out(high)


def expert_grads(h, rg, ff):
    n_e, _, rows, _ = h.shape
    half = rg.shape[3] // 2
    side = jax.ShapeDtypeStruct((n_e, 3 * ff, half), jnp.bfloat16)
    return pl.pallas_call(
        functools.partial(grads_body, ff),
        out_shape=(side, side),
        grid=(n_e, 2),
        in_specs=[
            pl.BlockSpec((1, 3, rows, ff), lambda e, j: (e, 0, 0, 0)),
            pl.BlockSpec((1, 2, rows, half), lambda e, j: (e, 0, 0, j)),
        ],
        out_specs=(pl.BlockSpec((1, 3 * ff, half), lambda e, j: (e, 0, 0)),) * 2,
        scratch_shapes=[pltpu.VMEM((3 * ff, rows), jnp.bfloat16)],
        compiler_params=pltpu.CompilerParams(vmem_limit_bytes=VMEM_BYTES),
    )(h, rg)


def blank(*shape):
    return pl.pallas_call(
        lambda ref: None,
        out_shape=jax.ShapeDtypeStruct(shape, jnp.bfloat16),
        out_specs=pl.BlockSpec(memory_space=pl.ANY),
    )()


def kernel_params():
    return pltpu.CompilerParams(vmem_limit_bytes=VMEM_BYTES)


def row_scale(squares, width):
    return lax.rsqrt(squares / width + epsilon)


def project_body(first, *refs):
    if first:
        x_ref, gain_ref, w_ref, normed_ref, raw_ref, qs_ref, ks_ref = refs
    else:
        normed_ref, w_ref, qs_in, ks_in, _, raw_ref, qs_ref, ks_ref = refs
    n = pl.program_id(0)

    @pl.when(n == 0)
    def _():
        if first:
            x = x_ref[...].astype(jnp.float32)
            scale = row_scale(jnp.sum(x * x, axis=1, keepdims=True), x.shape[1])
            normed_ref[...] = (x * scale * gain_ref[...]).astype(jnp.bfloat16)
            qs_ref[...] = jnp.zeros_like(qs_ref)
            ks_ref[...] = jnp.zeros_like(ks_ref)
        else:
            qs_ref[...] = qs_in[...]
            ks_ref[...] = ks_in[...]

    raw = dot_nn(normed_ref[...], w_ref[...])
    raw_ref[...] = raw
    squares = jnp.sum(raw * raw, axis=1, keepdims=True)
    qs_ref[...] += jnp.where(n == 0, squares, 0.0)
    ks_ref[...] += jnp.where(n == 1, squares, 0.0)


def project(x, gain, weights):
    tokens, width = x.shape
    half = width // 2
    f32 = jnp.float32
    sums = jax.ShapeDtypeStruct((tokens, 1), f32)

    def whole(*shape):
        return pl.BlockSpec(shape, lambda n: (0, 0))

    return pl.pallas_call(
        functools.partial(project_body, True),
        out_shape=(
            jax.ShapeDtypeStruct((tokens, width), jnp.bfloat16),
            jax.ShapeDtypeStruct((tokens, 6 * half), f32),
            sums,
            sums,
        ),
        grid=(3,),
        in_specs=[whole(tokens, width), whole(1, width), pl.BlockSpec((width, half), lambda n: (0, n))],
        out_specs=(whole(tokens, width), pl.BlockSpec((tokens, half), lambda n: (0, n)), whole(tokens, 1), whole(tokens, 1)),
        compiler_params=kernel_params(),
    )(x, gain[None], weights)


def project_other(normed, weights, qs, ks, raw):
    tokens, width = normed.shape
    half = width // 2
    f32 = jnp.float32
    sums = jax.ShapeDtypeStruct((tokens, 1), f32)

    def whole(*shape):
        return pl.BlockSpec(shape, lambda n: (0, 0))

    return pl.pallas_call(
        functools.partial(project_body, False),
        out_shape=(jax.ShapeDtypeStruct((tokens, 6 * half), f32), sums, sums),
        grid=(3,),
        in_specs=[whole(tokens, width), pl.BlockSpec((width, half), lambda n: (0, n)), whole(tokens, 1), whole(tokens, 1),
                  pl.BlockSpec(memory_space=pl.ANY)],
        out_specs=(pl.BlockSpec((tokens, half), lambda n: (0, 3 + n)), whole(tokens, 1), whole(tokens, 1)),
        input_output_aliases={4: 0},
        compiler_params=kernel_params(),
    )(normed, weights, qs, ks, raw)


def turned(v, cosine, sine):
    return v * cosine + pltpu.roll(v, v.shape[1] // 2, 1) * sine


def masked_chances(q, k, allowed, scale):
    scores = jnp.where(allowed, dot_nt(q, k) * scale, masked_score)
    grown = jnp.exp(scores - jnp.max(scores, axis=1, keepdims=True))
    return grown / jnp.sum(grown, axis=1, keepdims=True)


def allowed_pairs(row_ref, col_ref):
    n = row_ref.shape[1]
    rows = lax.broadcasted_iota(jnp.int32, (n, n), 0)
    cols = lax.broadcasted_iota(jnp.int32, (n, n), 1)
    return (row_ref[...] == col_ref[...]) & (rows >= cols)


def attend_body(width, q_ref, k_ref, v_ref, qs, ks, qg, kg, cos, sin, doc_row, doc_col, q_out, k_out, v_out, c_out):
    allowed = allowed_pairs(doc_row, doc_col)
    q_scale, k_scale = row_scale(qs[...], width), row_scale(ks[...], width)
    for i in range(q_ref.shape[1] // HD):
        at = slice(i * HD, (i + 1) * HD)
        q = turned(q_ref[:, at] * q_scale * qg[:, at], cos[...], sin[...]).astype(jnp.bfloat16)
        k = turned(k_ref[:, at] * k_scale * kg[:, at], cos[...], sin[...]).astype(jnp.bfloat16)
        v = v_ref[:, at].astype(jnp.bfloat16)
        q_out[:, at] = q
        k_out[:, at] = k
        v_out[:, at] = v
        chances = masked_chances(q, k, allowed, HD ** (-0.5)).astype(jnp.bfloat16)
        c_out[:, at] = dot_nn(chances, v).astype(jnp.bfloat16)


def attend(raw, qs, ks, qg, kg, cos, sin, document):
    tokens, width = raw.shape[0], raw.shape[1] // 3
    nb = width // 4

    def part(i):
        return pl.BlockSpec((tokens, nb), lambda h: (0, 6 * (h // 2) + 2 * i + h % 2))

    head = pl.BlockSpec((tokens, nb), lambda h: (0, h))
    gain = pl.BlockSpec((1, nb), lambda h: (0, h))

    def whole(*shape):
        return pl.BlockSpec(shape, lambda h: (0, 0))

    out = jax.ShapeDtypeStruct((tokens, width), jnp.bfloat16)
    return pl.pallas_call(
        functools.partial(attend_body, width),
        out_shape=(out,) * 4,
        grid=(4,),
        in_specs=[part(0), part(1), part(2), whole(tokens, 1), whole(tokens, 1), gain, gain]
        + [whole(tokens, HD), whole(tokens, HD), whole(1, tokens), whole(tokens, 1)],
        out_specs=(head,) * 4,
        compiler_params=kernel_params(),
    )(raw, raw, raw, qs, ks, qg[None], kg[None], cos, sin, document[None], document[:, None])


def lines(v, width):
    n, k = v.shape
    per = width // k
    return jnp.concatenate(
        [jnp.concatenate([v[i + j : i + j + 1] for j in range(per)], axis=1) for i in range(0, n, per)], axis=0
    )


def unlines(v, k):
    return jnp.concatenate([v[i : i + 1, j : j + k] for i in range(v.shape[0]) for j in range(0, v.shape[1], k)], axis=0)


def middle_body(core_ref, ctx_ref, wm_ref, wo_ref, x_ref, gain_ref, router_ref, middle_ref, piece_ref, probs_ref):
    w, j = pl.program_id(0), pl.program_id(1)
    tokens, width = x_ref.shape
    half = width // 2

    def out(ref, side):
        at = pl.ds(pl.multiple_of(side * half, half), half)
        part = dot_nn(ctx_ref[...], ref[...])

        @pl.when(j == 0)
        def _():
            middle_ref[:, at] = x_ref[:, at].astype(jnp.float32) + part

        @pl.when(j == 1)
        def _():
            middle_ref[:, at] += part

    @pl.when(w == 0)
    def _():
        out(wm_ref, core_ref[0])

    @pl.when(w == 1)
    def _():
        out(wo_ref, 1 - core_ref[0])

    @pl.when((w == 1) & (j == 1))
    def _():
        middle = middle_ref[...]
        scale = row_scale(jnp.sum(middle * middle, axis=1, keepdims=True), width)
        mixed = (middle * scale * gain_ref[...]).astype(jnp.bfloat16)
        piece_ref[0:tokens, :] = mixed
        logits = dot_nt(router_ref[...], mixed)
        grown = jnp.exp(logits - jnp.max(logits, axis=0, keepdims=True))
        probs = grown / jnp.sum(grown, axis=0, keepdims=True)
        probs_ref[...] = probs
        high = probs.astype(jnp.bfloat16).astype(jnp.float32)
        rows = [lines(high, width), lines(probs - high, width)]
        n = piece_ref.shape[0] - tokens - 2 * rows[0].shape[0]
        if n:
            rows.append(jnp.zeros((n, width), jnp.float32))
        piece_ref[tokens : piece_ref.shape[0], :] = jnp.concatenate(rows, axis=0).astype(jnp.bfloat16)


def half_specs(half):
    return [
        pl.BlockSpec((half, half), lambda w, j, core: (jnp.where(w == 0, core[0] ^ j, 1 - core[0]), 3)),
        pl.BlockSpec((half, half), lambda w, j, core: (jnp.where(w == 0, core[0], core[0] ^ j), 3)),
    ]


def middle_of(core, context, weights, weights_other, x, gain, router_t):
    tokens, width = x.shape
    half = width // 2
    experts = router_t.shape[0]
    extra = 2 * experts * tokens // width
    tall = tokens + extra + -extra % 16

    def whole(*shape):
        return pl.BlockSpec(shape, lambda w, j, core: (0, 0))

    return pl.pallas_call(
        middle_body,
        out_shape=(
            jax.ShapeDtypeStruct((tokens, width), jnp.float32),
            jax.ShapeDtypeStruct((tall, width), jnp.bfloat16),
            jax.ShapeDtypeStruct((experts, tokens), jnp.float32),
        ),
        grid_spec=pltpu.PrefetchScalarGridSpec(
            num_scalar_prefetch=1,
            grid=(2, 2),
            in_specs=[pl.BlockSpec((tokens, half), lambda w, j, core: (0, j))]
            + half_specs(half)
            + [whole(tokens, width), whole(1, width), whole(experts, width)],
            out_specs=(whole(tokens, width), whole(tall, width), whole(experts, tokens)),
        ),
        compiler_params=kernel_params(),
    )(core, context, weights, weights_other, x, gain[None], router_t)


def middle_back_body(core_ref, sum_ref, middle_ref, cot_ref, gain_ref, probs_ref, router_ref, wm_ref, wo_ref,
                     grad_ref, mine_ref, other_ref, up_ref, gain_out, router_out, logit_ref, branch, acc):
    j, w = pl.program_id(0), pl.program_id(1)
    tokens, width = middle_ref.shape
    half = width // 2

    @pl.when((j == 0) & (w == 0))
    def _():
        middle = middle_ref[...]
        scale = row_scale(jnp.sum(middle * middle, axis=1, keepdims=True), width)
        unit = middle * scale
        probs = probs_ref[...]
        n = probs.shape[0] * tokens // width
        total = sum_ref[tokens : tokens + n, :] + sum_ref[tokens + n : tokens + 2 * n, :]
        raised = unlines(total, tokens)
        logit = (probs * (raised - jnp.sum(probs * raised, axis=0, keepdims=True))).astype(jnp.bfloat16)
        logit_ref[...] = logit
        mixed_up = sum_ref[0:tokens, :] + dot_tn(logit, router_ref[...])
        gain_out[...] = jnp.sum(mixed_up * unit, axis=0, keepdims=True)
        router_out[...] = dot_nn(logit, (unit * gain_ref[...]).astype(jnp.bfloat16))
        raised = mixed_up * gain_ref[...]
        mean = jnp.sum(raised * unit, axis=1, keepdims=True) / width
        grad = cot_ref[...].astype(jnp.float32) + scale * (raised - unit * mean)
        grad_ref[...] = grad
        branch[...] = grad.astype(jnp.bfloat16)
        mine_ref[...] = branch[:, pl.ds(pl.multiple_of(core_ref[0] * half, half), half)]
        other_ref[...] = branch[:, pl.ds(pl.multiple_of((1 - core_ref[0]) * half, half), half)]

    @pl.when(w == 0)
    def _():
        acc[...] = dot_nt(mine_ref[...], wm_ref[...])

    @pl.when(w == 1)
    def _():
        up_ref[...] = (acc[...] + dot_nt(other_ref[...], wo_ref[...])).astype(jnp.bfloat16)


def middle_back(core, total, middle, cotangent, gain, probs, router_t, weights, weights_other):
    tokens, width = middle.shape
    half = width // 2
    experts = probs.shape[0]
    bf, f32 = jnp.bfloat16, jnp.float32

    def whole(*shape):
        return pl.BlockSpec(shape, lambda j, w, core: (0, 0))

    specs = [
        pl.BlockSpec((half, half), lambda j, w, core: (core[0] ^ j, 3)),
        pl.BlockSpec((half, half), lambda j, w, core: (core[0] ^ j, 3)),
    ]
    return pl.pallas_call(
        middle_back_body,
        out_shape=(
            jax.ShapeDtypeStruct((tokens, width), f32),
            jax.ShapeDtypeStruct((tokens, half), bf),
            jax.ShapeDtypeStruct((tokens, half), bf),
            jax.ShapeDtypeStruct((tokens, width), bf),
            jax.ShapeDtypeStruct((1, width), f32),
            jax.ShapeDtypeStruct((experts, width), f32),
            jax.ShapeDtypeStruct((experts, tokens), bf),
        ),
        grid_spec=pltpu.PrefetchScalarGridSpec(
            num_scalar_prefetch=1,
            grid=(2, 2),
            in_specs=[whole(*total.shape), whole(tokens, width), whole(tokens, width), whole(1, width),
                      whole(experts, tokens), whole(experts, width)] + specs,
            out_specs=(
                whole(tokens, width), whole(tokens, half), whole(tokens, half),
                pl.BlockSpec((tokens, half), lambda j, w, core: (0, j)),
                whole(1, width), whole(experts, width), whole(experts, tokens),
            ),
            scratch_shapes=[pltpu.VMEM((tokens, width), bf), pltpu.VMEM((tokens, half), f32)],
        ),
        compiler_params=kernel_params(),
    )(core, total, middle, cotangent, gain[None], probs, router_t, weights, weights_other)


def attend_back_body(width, q_ref, k_ref, v_ref, u_ref, q_raw, k_raw, qs, ks, qg, kg, cos, sin, doc_row, doc_col,
                     ups, qg_out, kg_out, q_back, k_back, v_back, q_mean, k_mean):
    phase, h = pl.program_id(0), pl.program_id(1)
    nb = q_ref.shape[1]
    q_scale, k_scale = row_scale(qs[...], width), row_scale(ks[...], width)
    cols = pl.ds(pl.multiple_of(h * nb, nb), nb)

    @pl.when((phase == 0) & (h == 0))
    def _():
        q_mean[...] = jnp.zeros_like(q_mean)
        k_mean[...] = jnp.zeros_like(k_mean)

    @pl.when(phase == 0)
    def _():
        allowed = allowed_pairs(doc_row, doc_col)
        dq, dk, dv = [], [], []
        for i in range(nb // HD):
            at = slice(i * HD, (i + 1) * HD)
            q, k, u = q_ref[:, at], k_ref[:, at], u_ref[:, at]
            chances = masked_chances(q, k, allowed, HD ** (-0.5))
            raised = dot_nt(u, v_ref[:, at])
            dv.append(dot_tn(chances.astype(jnp.bfloat16), u).astype(jnp.bfloat16))
            back = chances * (raised - jnp.sum(chances * raised, axis=1, keepdims=True))
            back = back.astype(jnp.bfloat16)
            dq.append(turned(dot_nn(back, k) * HD ** (-0.5), cos[...], -sin[...]))
            dk.append(turned(dot_tn(back, q) * HD ** (-0.5), cos[...], -sin[...]))
        for parts, raw, scale, gain, mean, kept, out in (
            (dq, q_raw, q_scale, qg, q_mean, q_back, qg_out),
            (dk, k_raw, k_scale, kg, k_mean, k_back, kg_out),
        ):
            back = jnp.concatenate(parts, axis=1)
            kept[h] = back
            grown = back * (raw[...] * scale)
            out[0:1, cols] = jnp.sum(grown, axis=0, keepdims=True)
            mean[...] += jnp.sum(grown * gain[...], axis=1, keepdims=True)
        v_back[h] = jnp.concatenate(dv, axis=1)

    @pl.when(phase == 1)
    def _():
        for i, (raw, scale, gain, mean, kept) in enumerate(
            ((q_raw, q_scale, qg, q_mean, q_back), (k_raw, k_scale, kg, k_mean, k_back))
        ):
            up = scale * (kept[h] * gain[...] - raw[...] * scale * (mean[...] / width))
            ups[0, i] = up.astype(jnp.bfloat16)
        ups[0, 2] = v_back[h]


def attend_back(q, k, v, up, raw, qs, ks, qg, kg, cos, sin, document):
    tokens, width = v.shape
    nb = width // 4
    f32 = jnp.float32

    def part(i):
        return pl.BlockSpec((tokens, nb), lambda p, h: (0, 6 * (h // 2) + 2 * i + h % 2))

    head = pl.BlockSpec((tokens, nb), lambda p, h: (0, jnp.where(p == 0, h, 3)))
    gain = pl.BlockSpec((1, nb), lambda p, h: (0, h))

    def whole(*shape):
        return pl.BlockSpec(shape, lambda p, h: (0, 0))

    def out_place(p, h):
        at = jnp.where(p == 0, 0, h)
        return (at // 2, 0, 0, at % 2)

    return pl.pallas_call(
        functools.partial(attend_back_body, width),
        out_shape=(
            jax.ShapeDtypeStruct((2, 3, tokens, width // 2), jnp.bfloat16),
            jax.ShapeDtypeStruct((1, width), f32),
            jax.ShapeDtypeStruct((1, width), f32),
        ),
        grid=(2, 4),
        in_specs=[head, head, head, head, part(0), part(1), whole(tokens, 1), whole(tokens, 1), gain, gain]
        + [whole(tokens, HD), whole(tokens, HD), whole(1, tokens), whole(tokens, 1)],
        out_specs=(pl.BlockSpec((1, 3, tokens, nb), out_place), whole(1, width), whole(1, width)),
        scratch_shapes=[
            pltpu.VMEM((4, tokens, nb), f32),
            pltpu.VMEM((4, tokens, nb), f32),
            pltpu.VMEM((4, tokens, nb), jnp.bfloat16),
            pltpu.VMEM((tokens, 1), f32),
            pltpu.VMEM((tokens, 1), f32),
        ],
        compiler_params=kernel_params(),
    )(q, k, v, up, raw, raw, qs, ks, qg[None], kg[None], cos, sin, document[None], document[:, None])


def qkv_grad_body(n_ref, no_ref, u_ref, uo_ref, first, second, pair):
    i = pl.program_id(0)
    tokens = n_ref.shape[0]

    @pl.when(i == 0)
    def _():
        pair[:, 0:tokens] = n_ref[...].T
        pair[:, tokens : 2 * tokens] = no_ref[...].T

    ups = jnp.concatenate([u_ref[0, 0], uo_ref[0]], axis=0)
    got = dot_nn(pair[...], ups).astype(jnp.bfloat16)

    @pl.when(i < 3)
    def _():
        first[...] = got

    @pl.when(i >= 3)
    def _():
        second[...] = got


def qkv_grad(normed, normed_other, ups, got):
    tokens, width = normed.shape
    nb = width // 4
    out = jax.ShapeDtypeStruct((width, 3 * nb), jnp.bfloat16)

    def whole(*shape):
        return pl.BlockSpec(shape, lambda i: (0, 0))

    return pl.pallas_call(
        qkv_grad_body,
        out_shape=(out, out),
        grid=(6,),
        in_specs=[
            whole(tokens, width),
            whole(tokens, width),
            pl.BlockSpec((1, 1, tokens, nb), lambda i: (0, i // 2, 0, i % 2)),
            pl.BlockSpec((1, tokens, nb), lambda i: (i // 2, 0, i % 2)),
        ],
        out_specs=(
            pl.BlockSpec((width, nb), lambda i: (0, jnp.minimum(i, 2))),
            pl.BlockSpec((width, nb), lambda i: (0, jnp.maximum(i - 3, 0))),
        ),
        scratch_shapes=[pltpu.VMEM((width, 2 * tokens), jnp.bfloat16)],
        compiler_params=kernel_params(),
    )(normed, normed_other, ups, got)


def input_grad_body(ups_ref, wm_ref, wo_ref, x_ref, grad_ref, gain_ref, out_ref, gain_out, total, turned_ups):
    n = pl.program_id(0)
    tokens, width = x_ref.shape
    half = width // 2
    nb = wm_ref.shape[0]

    @pl.when(n == 0)
    def _():
        for w in range(2):
            for i in range(3):
                turned_ups[w, i * half : (i + 1) * half, :] = ups_ref[w, i].T

    acc = dot_nn(wm_ref[...], turned_ups[0]) + dot_nn(wo_ref[...], turned_ups[1])
    total[n] = acc.T

    @pl.when(n == pl.num_programs(0) - 1)
    def _():
        x = x_ref[...].astype(jnp.float32)
        scale = row_scale(jnp.sum(x * x, axis=1, keepdims=True), width)
        unit = x * scale
        up = jnp.concatenate([total[i] for i in range(width // nb)], axis=1)
        gain_out[...] = jnp.sum(up * unit, axis=0, keepdims=True)
        raised = up * gain_ref[...]
        mean = jnp.sum(raised * unit, axis=1, keepdims=True) / width
        out_ref[...] = grad_ref[...] + scale * (raised - unit * mean)


def input_grad(ups, weights, weights_other, x, grad, gain):
    tokens, width = x.shape
    nb = 512
    f32 = jnp.float32

    def whole(*shape):
        return pl.BlockSpec(shape, lambda n: (0,) * len(shape))

    return pl.pallas_call(
        input_grad_body,
        out_shape=(jax.ShapeDtypeStruct((tokens, width), f32), jax.ShapeDtypeStruct((1, width), f32)),
        grid=(width // nb,),
        in_specs=[
            whole(*ups.shape),
            pl.BlockSpec((nb, 3 * width // 2), lambda n: (n, 0)),
            pl.BlockSpec((nb, 3 * width // 2), lambda n: (n, 0)),
            whole(tokens, width),
            whole(tokens, width),
            whole(1, width),
        ],
        out_specs=(whole(tokens, width), whole(1, width)),
        scratch_shapes=[
            pltpu.VMEM((width // nb, tokens, nb), f32),
            pltpu.VMEM((2, 3 * width // 2, tokens), jnp.bfloat16),
        ],
        compiler_params=kernel_params(),
    )(ups, weights, weights_other, x, grad, gain[None])


def cut_body(x_ref, y_ref, low, high):
    low[...] = x_ref[...]
    high[...] = y_ref[...]


def cut_pair(x, y):
    n, width = x.shape[0] // 2, x.shape[1]
    out = jax.ShapeDtypeStruct((n, width), x.dtype)
    place = pl.BlockSpec((n, width), lambda i: (0, 0))
    return pl.pallas_call(
        cut_body,
        out_shape=(out, out),
        grid=(1,),
        in_specs=[place, pl.BlockSpec((n, width), lambda i: (1, 0))],
        out_specs=(place, place),
    )(x, y)


def finish_body(k, low, high, *rest):
    got_x, got_y, more_y, more_x = rest[:k], rest[k : 2 * k], rest[2 * k : 2 * k + 3], rest[2 * k + 3 : 2 * k + 6]
    gate, up, down = rest[2 * k + 6 :]
    j = pl.program_id(1)
    ff = more_y[0].shape[1]

    def out(part, got, more):
        f32 = jnp.float32
        total = part[0].astype(f32) + jnp.concatenate([v[0].astype(f32) for v in got], axis=0)
        total = total + jnp.concatenate([v[0].astype(f32) for v in more], axis=0)
        gate[0] = total[:ff].T
        up[0] = total[ff : 2 * ff].T
        down[0] = total[2 * ff :]

    @pl.when(j == 0)
    def _():
        out(low, got_x, more_y)

    @pl.when(j == 1)
    def _():
        out(high, got_y, more_x)


def finish(low, high, got_x, got_y, more):
    n_e, rows, half = low.shape
    ff = rows // 3
    k = len(got_x)

    def place(v):
        return pl.BlockSpec((1,) + v.shape[1:], lambda e, j: (e, 0, 0))

    ins = [low, high, *got_x, *got_y, *[m[0] for m in more], *[m[1] for m in more]]
    f32 = jnp.float32
    turned_out = jax.ShapeDtypeStruct((n_e, 2 * half, ff), f32)
    return pl.pallas_call(
        functools.partial(finish_body, k),
        out_shape=(turned_out, turned_out, jax.ShapeDtypeStruct((n_e, ff, 2 * half), f32)),
        grid=(n_e, 2),
        in_specs=[place(v) for v in ins],
        out_specs=(
            pl.BlockSpec((1, half, ff), lambda e, j: (e, j, 0)),
            pl.BlockSpec((1, half, ff), lambda e, j: (e, j, 0)),
            pl.BlockSpec((1, ff, half), lambda e, j: (e, 0, j)),
        ),
        compiler_params=kernel_params(),
    )(*ins)


fence = lax.optimization_barrier


def plus(a, b):
    return a.astype(jnp.float32) + b.astype(jnp.float32)


def on_device(
    hidden_in,
    cotangent,
    attention_gain,
    query_gain,
    key_gain,
    mixture_gain,
    query_weight,
    key_weight,
    value_weight,
    output_weight,
    router_weight,
    gate_weight,
    up_weight,
    down_weight,
    routes,
    segments,
):
    bf16, f32 = jnp.bfloat16, jnp.float32
    n_dp, owners = lax.axis_size("dp"), lax.axis_size("expert")
    nz = owners // 2
    n_dev = n_dp * owners
    tokens, width = hidden_in.shape
    half = width // 2
    unit = width // (n_dev // 2)
    cut = unit // 2
    top = routes.shape[1]
    exp_dev = gate_weight.shape[0]
    experts = exp_dev * owners
    cap = max(2, tokens * top * 5 // (experts * 4))
    ff = gate_weight.shape[2]
    rows_dev = attention_gain.shape[0]
    score_scale = HD ** (-0.5)
    dp, ex = lax.axis_index("dp"), lax.axis_index("expert")
    core, zc = ex % 2, ex // 2

    def swap(v, axis, bit):
        size = n_dp if axis == "dp" else owners
        return lax.ppermute(v, axis, [(i, i ^ bit) for i in range(size)])

    def swap_core(v):
        return swap(v, "expert", 1)

    def swap_x(v):
        return swap(v, "dp", 1)

    def swap_y(v):
        return swap(v, "dp", 2)

    def ring(v):
        return lax.ppermute(v, "expert", [(i, (i + 2) % owners) for i in range(owners)])

    def in_order(bit, mine, other, axis):
        return jnp.where(
            bit == 0,
            jnp.concatenate([mine, other], axis=axis),
            jnp.concatenate([other, mine], axis=axis),
        )

    def half_of(v, which, axis):
        return lax.dynamic_slice_in_dim(v, which * (v.shape[axis] // 2), v.shape[axis] // 2, axis)

    def halves(v, axis):
        return half_of(v, core, axis), half_of(v, 1 - core, axis)

    def by_rows(v):
        return with_layout_constraint(v, Layout((0, 1)))

    def thirds(v):
        return [v[:, t * ff : (t + 1) * ff] for t in range(3)]

    def chip_row(plane, r):
        return ((dp ^ plane) * nz + (zc - r) % nz) * unit

    bits = []
    b = 1
    while b < owners:
        bits.append(("expert", b, (ex // b) % 2))
        b *= 2
    b = 1
    while b < n_dp:
        bits.append(("dp", b, (dp // b) % 2))
        b *= 2

    sources = (query_weight, key_weight, value_weight, output_weight)
    gains = (attention_gain, query_gain, key_gain, mixture_gain)
    small = jnp.concatenate([v[:, None] for v in gains] + [router_weight], axis=1)
    small = jnp.pad(small, ((0, 0), (0, -small.shape[1] % 128)))
    theirs = jnp.concatenate([half_of(w, 1 - core, 1) for w in sources] + [small], axis=1)
    mine = jnp.concatenate([half_of(w, core, 1) for w in sources] + [small], axis=1)
    piece = by_rows(in_order(core, mine, swap_core(theirs), 0))
    piece, gate_weight, up_weight, down_weight, cotangent, segments, hidden_in = fence(
        (piece, gate_weight, up_weight, down_weight, cotangent, segments, hidden_in)
    )

    main = 4 * half
    weights, small_all = blank(width, main), blank(width, small.shape[1])
    route_rows = routes.T.astype(bf16).reshape(-1, width)
    pad = -route_rows.shape[0] % 16
    cot_piece = jnp.concatenate([cotangent, route_rows, jnp.zeros((pad, width), bf16)], axis=0)
    cot_steps = [cot_piece]

    def put(buffers, v, row):
        kept, kept_small = buffers
        kept = lax.dynamic_update_slice(kept, v[:, :main], (row, 0))
        kept_small = by_rows(lax.dynamic_update_slice(kept_small, v[:, main:], (row, 0)))
        return kept, kept_small

    buffers = (weights, small_all)
    before, arrived = None, []
    for r in range(nz):
        by_x, by_y = by_rows(swap_x(piece)), by_rows(swap_y(piece))
        following, sent = (), ()
        if before is not None:
            sent = cut_pair(*before)
            sent = (by_rows(swap_y(sent[0])), by_rows(swap_x(sent[1])))
        if r + 1 < nz:
            following = by_rows(ring(piece))
        else:
            cot_steps.append(ring(cot_steps[-1]))
        for v, row in arrived + [(piece, chip_row(0, r))]:
            buffers = put(buffers, v, row)
        by_x, by_y, following, sent, buffers, cot_steps = fence(
            (by_x, by_y, following, sent, buffers, cot_steps)
        )
        arrived = [(by_x, chip_row(1, r)), (by_y, chip_row(2, r))]
        if before is not None:
            arrived += [(sent[0], chip_row(3, r - 1)), (sent[1], chip_row(3, r - 1) + cut)]
        before, piece = (by_x, by_y), following
    sent = cut_pair(*before)
    sent = (by_rows(swap_y(sent[0])), by_rows(swap_x(sent[1])))
    own_first, own_rest = [], []
    for j in range(2):
        part = slice(j * half, (j + 1) * half)
        own_first.append(gate_weight[:, part].swapaxes(1, 2))
        own_rest.append(
            jnp.concatenate([up_weight[:, part].swapaxes(1, 2), down_weight[:, :, part]], axis=1)
        )
    cosine, sine = rotary_tables(segments, HD)
    cosine = jnp.concatenate([cosine[0], cosine[0]], axis=1)
    sine = jnp.concatenate([-sine[0], sine[0]], axis=1)
    document = segments[0]
    for v, row in arrived:
        buffers = put(buffers, v, row)
    buffers, own_first, own_rest, cosine, sine, document, sent, cot_steps = fence(
        (buffers, own_first, own_rest, cosine, sine, document, sent, cot_steps)
    )
    buffers = put(buffers, sent[0], chip_row(3, nz - 1))
    buffers = put(buffers, sent[1], chip_row(3, nz - 1) + cut)
    weights, small_all = fence(buffers)

    weights_other = swap_core(weights)
    x_low, y_high = [swap_x(own_first[0])], [swap_y(own_first[1])]
    if len(cot_steps) < nz:
        cot_steps.append(ring(cot_steps[-1]))
    gains_all = small_all[:, :4].astype(f32).T
    router_t = small_all[:, 4 : 4 + experts].T
    attention_gain_full, mixture_gain_full = gains_all[0], gains_all[3]
    query_gain_rel = jnp.concatenate(halves(gains_all[1], 0))
    key_gain_rel = jnp.concatenate(halves(gains_all[2], 0))
    core_ref = core[None]
    normed, raw, query_squares, key_squares = project(hidden_in, attention_gain_full, weights)
    (
        weights,
        weights_other,
        mixture_gain_full,
        router_t,
        normed,
        raw,
        x_low,
        y_high,
        cot_steps,
        own_first,
        own_rest,
    ) = fence(
        (
            weights,
            weights_other,
            mixture_gain_full,
            router_t,
            normed,
            raw,
            x_low,
            y_high,
            cot_steps,
            own_first,
            own_rest,
        )
    )

    x_low.append(swap_x(own_rest[0]))
    y_high.append(swap_y(own_rest[1]))
    while len(cot_steps) < nz:
        cot_steps.append(ring(cot_steps[-1]))
    raw, query_squares, key_squares = project_other(
        normed, weights_other, query_squares, key_squares, raw
    )
    query_heads, key_heads, value_heads, context = attend(
        raw, query_squares, key_squares, query_gain_rel, key_gain_rel, cosine, sine, document
    )
    middle, mixed_piece, router_probs = middle_of(
        core_ref, context, weights, weights_other, hidden_in, mixture_gain_full, router_t
    )
    mixed_piece, x_low, y_high, cot_steps, context, middle, normed = fence(
        (mixed_piece, x_low, y_high, cot_steps, context, middle, normed)
    )
    n_prob = 2 * experts * tokens // width

    mixed_all, cot_all, mixed_last = [], [], mixed_piece
    x_high, y_low = [], []
    for r in range(nz):
        following = ring(mixed_last) if r + 1 < nz else ()
        got = ()
        if r < 3:
            sent = [(v[:, :ff], w[:, :ff], w[:, ff:])[r] for v, w in zip(own_first, own_rest)]
            got = (swap_x(sent[1]), swap_y(sent[0]))
        mixed_all += [mixed_last, swap_core(mixed_last)]
        cot_all += [cot_steps[r], swap_core(cot_steps[r])]
        following, mixed_all, cot_all, got = fence((following, mixed_all, cot_all, got))
        if r < 3:
            x_high.append(got[0])
            y_low.append(got[1])
        mixed_last = following
    number = (ex * exp_dev)[None]
    rank_row, rank_col, gate_row = plan(
        number, mixed_all, cot_all, n_prob // 2, top, exp_dev, tokens
    )

    send_pieces = ((0, 5 * ff // 4), (5 * ff // 4, 17 * ff // 16), (37 * ff // 16, 11 * ff // 16))
    last_pieces = ((0, 3 * ff // 4), (3 * ff // 4, 5 * ff // 4), (2 * ff, ff))
    corner_low, corner_high = [swap_y(v) for v in x_low], [swap_x(v) for v in y_high]
    shards = (tuple(zip(own_first, own_rest)), (x_low, x_high), (y_low, y_high))
    rows, acts, gates, products, send_x, keep_x, keep_y, send_y = experts_first(
        mixed_all, cot_all, shards, ff, rank_row, gate_row, cap, send_pieces
    )
    corner_low, corner_high, rows, acts, gates, products, send_x, send_y = fence(
        (corner_low, corner_high, rows, acts, gates, products, send_x, send_y)
    )

    got_x, got_y = [swap_x(send_x[0])], [swap_y(send_y[0])]
    parts = ()
    if nz > 4:
        parts = fence(expert_grads(acts, rows, ff))
    shards = shards + ((corner_low, corner_high),)
    acts_last, products, last_low, last_high = experts_last(
        rows, gates, products, shards[3], ff, last_pieces
    )
    acts_last, products, last_low, last_high, got_x, got_y, send_x, send_y = fence(
        (acts_last, products, last_low, last_high, got_x, got_y, send_x, send_y)
    )

    def spread(kinds, zs, gates):
        return experts_spread(
            number,
            acts,
            acts_last,
            products,
            shards,
            ff,
            width,
            rank_row,
            rank_col,
            cap,
            kinds,
            zs,
            gates,
        )

    near = tuple(range(1, nz // 2 + 1))
    far = tuple(range(nz // 2 + 1, nz)) + (0,)
    got_x.append(swap_x(send_x[1]))
    got_y.append(swap_y(send_y[1]))
    copied_near, other_near = spread((0, 1), near, True)
    copied_near, other_near, got_x, got_y, send_x, send_y = fence(
        (copied_near, other_near, got_x, got_y, send_x, send_y)
    )
    got_near = swap_core(other_near)
    got_near = fence(got_near)

    class Total:
        def __init__(self, blocks):
            self.blocks, self.value, self.at = blocks, blocks[1], 2

        def move(self):
            self.value = ring(self.value.astype(bf16))

        def add(self):
            self.value = plus(self.value, self.blocks[self.at % nz])
            self.at += 1

        def rest(self):
            while self.at <= nz:
                self.move()
                self.add()
            return self.value

    copies_sum = Total({r: plus(copied_near[i], got_near[i]) for i, r in enumerate(near)})
    copies_sum.move()
    got_x.append(swap_x(send_x[2]))
    got_y.append(swap_y(send_y[2]))
    got_last_x, got_last_y = [swap_x(last_low[0])], [swap_y(last_high[0])]
    copied_far, other_far = spread((0, 1), far, True)
    copies_sum.value, copied_far, other_far, got_x, got_y, got_last_x, got_last_y = fence(
        (copies_sum.value, copied_far, other_far, got_x, got_y, got_last_x, got_last_y)
    )
    got_far = swap_core(other_far)
    copies_sum.add()
    copies_sum.move()
    got_last_x.append(swap_x(last_low[1]))
    got_last_y.append(swap_y(last_high[1]))
    mixture, mixture_other = spread((2,), tuple(range(nz)), False)
    copies_sum.value, got_far, mixture, mixture_other, got_last_x, got_last_y = fence(
        (copies_sum.value, got_far, mixture, mixture_other, got_last_x, got_last_y)
    )
    copies_sum.blocks.update({r: plus(copied_far[i], got_far[i]) for i, r in enumerate(far)})
    copies_sum.add()
    copies_sum.move()
    got_last_x.append(swap_x(last_low[2]))
    got_last_y.append(swap_y(last_high[2]))
    got_mix = swap_core(mixture_other)
    context = in_order(core, context[:, :half], context[:, half:], 1)
    first_x = jnp.concatenate(got_last_x[:2], axis=1)
    first_y = jnp.concatenate(got_last_y[:2], axis=1)
    more_y = [plus(a, b).astype(bf16) for a, b in zip(thirds(keep_y)[:2], thirds(first_x)[:2])]
    more_x = [plus(a, b).astype(bf16) for a, b in zip(thirds(keep_x)[:2], thirds(first_y)[:2])]
    copies_sum.value, got_last_x, got_last_y, context, got_mix, more_x, more_y = fence(
        (copies_sum.value, got_last_x, got_last_y, context, got_mix, more_x, more_y)
    )
    for sums, kept, got in ((more_y, keep_y, got_last_x), (more_x, keep_x, got_last_y)):
        sums.append(plus(thirds(kept)[2], got[2]).astype(bf16))
    copies_sum.add()
    copies_sum = copies_sum.rest()

    def send_more(t):
        return swap_y(more_y[t]), swap_x(more_x[t])

    more = [send_more(0)]
    mixed = Total({r: plus(mixture[r], got_mix[r]) for r in range(nz)})
    mixed.move()
    normed_other, context_other = swap_core(normed), swap_core(context)
    (middle_grad, branch, branch_other, context_up, mixture_gain_grad, router_grad, _) = middle_back(
        core_ref,
        copies_sum,
        middle,
        cotangent,
        mixture_gain_full,
        router_probs,
        router_t,
        weights,
        weights_other,
    )
    (context_up, branch, branch_other, mixed.value, normed_other, context_other, more, more_x, more_y) = fence(
        (context_up, branch, branch_other, mixed.value, normed_other, context_other, more, more_x, more_y)
    )
    mixed.add()
    mixed.move()
    more.append(send_more(1))
    got_branch = swap_core(branch_other)
    ups, query_gain_grad, key_gain_grad = attend_back(
        query_heads,
        key_heads,
        value_heads,
        context_up,
        raw,
        query_squares,
        key_squares,
        query_gain_rel,
        key_gain_rel,
        cosine,
        sine,
        document,
    )
    ups, mixed.value, got_branch, more = fence((ups, mixed.value, got_branch, more))
    got_ups = swap_core(ups[1])
    more.append(send_more(2))
    first, second = qkv_grad(normed, normed_other, ups, got_ups)
    mixed.add()
    mixed.move()
    def several(v, picks):
        return jnp.concatenate(
            [lax.dynamic_slice_in_dim(v, chip_row(plane, r), unit, 0) for plane, r in picks],
            axis=0,
        )

    def pack(v, n):
        k = n * unit // v.shape[0]
        step = v.shape[1] // k
        return jnp.concatenate([v[:, i * step : (i + 1) * step] for i in range(k)], axis=0)

    def unpack(v, rows):
        return jnp.concatenate([v[i : i + rows] for i in range(0, v.shape[0], rows)], axis=1)

    side = 3 * half // 2

    def step_one(rs):
        sent = several(first, [(1, r) for r in rs] + [(3, r) for r in rs])
        back = several(second, [(2, r) for r in rs] + [(3, r) for r in rs])
        return sent, back

    def step_two(rs, by_x, by_y):
        n = len(rs) * unit
        more_y = plus(several(first, [(2, r) for r in rs]), by_x[n:]).astype(bf16)
        more_x = plus(several(second, [(1, r) for r in rs]), by_y[n:]).astype(bf16)
        return more_y, more_x

    def step_three(rs, by_x, by_y, more_y, more_x):
        n = len(rs) * unit
        left = plus(several(first, [(0, r) for r in rs]), by_x[:n]) + more_y.astype(f32)
        right = plus(several(second, [(0, r) for r in rs]), by_y[:n]) + more_x.astype(f32)
        whole = jnp.concatenate([left, right], axis=1)
        return {r: whole[i * unit : (i + 1) * unit] for i, r in enumerate(rs)}

    near_sent = step_one(near)
    near_sent, more, ups, first, second, branch, got_branch = fence(
        (near_sent, more, ups, first, second, branch, got_branch)
    )
    output_grad = jnp.einsum(
        "tc,td->cd",
        jnp.concatenate([context, context_other], axis=0),
        jnp.concatenate([branch, got_branch], axis=0),
        preferred_element_type=f32,
    ).astype(bf16)
    near_got = (swap_x(near_sent[0]), swap_y(near_sent[1]))
    output_sum = Total(
        [several(output_grad, [(plane, r) for plane in range(n_dp)]) for r in range(nz)]
    )
    output_sum.move()
    far_sent = step_one(far)
    hidden_grad, attention_gain_grad = input_grad(
        ups, weights, weights_other, hidden_in, middle_grad, attention_gain_full
    )

    def canonical(v):
        return in_order(core, v[:half], v[half:], 0)

    gain_grads = (
        attention_gain_grad[0],
        canonical(query_gain_grad[0]),
        canonical(key_gain_grad[0]),
        mixture_gain_grad[0],
    )
    small_sum = jnp.concatenate(
        [v.reshape(n_dev, rows_dev) for v in gain_grads]
        + [
            router_grad.reshape(experts, n_dev, rows_dev)
            .swapaxes(0, 1)
            .reshape(n_dev, experts * rows_dev)
        ],
        axis=1,
    )
    folded = []

    def fold(v):
        axis, bit, mark = bits[len(folded)]
        folded.append(bit)
        v = v.reshape(v.shape[0] // 2, 2, v.shape[1])
        keep = lax.dynamic_index_in_dim(v, mark, 1, False)
        return keep + swap(lax.dynamic_index_in_dim(v, 1 - mark, 1, False), axis, bit)

    near_got, output_sum.value, small_sum, hidden_grad, far_sent, mixed.value = fence(
        (near_got, output_sum.value, small_sum, hidden_grad, far_sent, mixed.value)
    )
    mixed.add()
    mixed = mixed.rest()
    layer_out = (middle + mixed).astype(bf16)
    near_more = step_two(near, *near_got)
    near_more = fence(near_more)
    near_more = (swap_y(near_more[0]), swap_x(near_more[1]))
    far_got = (swap_x(far_sent[0]), swap_y(far_sent[1]))
    output_sum.add()
    output_sum.move()
    near_more, output_sum.value = fence((near_more, output_sum.value))
    output_sum.add()
    output_sum.move()
    blocks = step_three(near, *near_got, *near_more)
    small_sum = fold(small_sum)
    far_got, output_sum.value, blocks, small_sum = fence(
        (far_got, output_sum.value, blocks, small_sum)
    )
    output_sum.add()
    output_sum = output_sum.rest()
    out_low = output_sum[:, : half // 2].astype(bf16)
    out_high = output_sum[:, half // 2 :].astype(bf16)
    far_more = step_two(far, *far_got)
    to_y = jnp.concatenate([far_more[0], pack(out_high[2 * unit :], len(far))], axis=1)
    to_x = jnp.concatenate(
        [
            far_more[1],
            pack(jnp.concatenate([out_low[unit : 2 * unit], out_low[3 * unit :]], axis=0), len(far)),
        ],
        axis=1,
    )
    by_y, by_x = swap_y(to_y), swap_x(to_x)
    weight_sum = Total(blocks)
    for _ in near[:-1]:
        weight_sum.move()
        if weight_sum.at < near[-1]:
            weight_sum.add()
    small_sum = fold(small_sum)
    if not parts:
        acts, rows, _ = fence((acts, rows, to_y))
        parts = expert_grads(acts, rows, ff)
    by_y, by_x, weight_sum.value, small_sum, parts, got_x, got_y, more = fence(
        (by_y, by_x, weight_sum.value, small_sum, parts, got_x, got_y, more)
    )
    expert_grad = finish(*parts, got_x, got_y, more)
    far_more = (by_y[:, :side], by_x[:, :side])
    got_out_x = unpack(by_x[:, side:], 2 * unit)
    got_out_y = unpack(by_y[:, side:], 2 * unit)
    out_more_y = plus(out_low[2 * unit : 3 * unit], got_out_x[unit:]).astype(bf16)
    out_more_x = plus(out_high[unit : 2 * unit], got_out_y[unit:]).astype(bf16)
    if len(near) > 1:
        weight_sum.add()
    weight_sum.move()
    out_more_y, out_more_x = swap_y(out_more_y), swap_x(out_more_x)
    small_sum = fold(small_sum)
    weight_sum.blocks.update(step_three(far, *far_got, *far_more))
    weight_sum.value, out_more_y, out_more_x, small_sum, expert_grad = fence(
        (weight_sum.value, out_more_y, out_more_x, small_sum, expert_grad)
    )
    weight_sum.add()
    while weight_sum.at <= nz:
        weight_sum.move()
        if len(folded) < len(bits):
            small_sum = fold(small_sum)
        weight_sum.value, small_sum = fence((weight_sum.value, small_sum))
        weight_sum.add()
    total = weight_sum.value
    while len(folded) < len(bits):
        small_sum = fold(small_sum)
    small_sum = small_sum[0]
    gain_parts = small_sum[: 4 * rows_dev].reshape(4, rows_dev)
    router_part = small_sum[4 * rows_dev :].reshape(experts, rows_dev).T
    out_total = jnp.concatenate(
        [
            plus(out_low[:unit], got_out_x[:unit]) + out_more_y.astype(f32),
            plus(out_high[:unit], got_out_y[:unit]) + out_more_x.astype(f32),
        ],
        axis=1,
    )
    total = jnp.concatenate([total, out_total], axis=1)
    kept_rows = half_of(total, core, 0)
    got_rows = swap_core(half_of(total, 1 - core, 0))
    weight_grads = [
        in_order(
            core, kept_rows[:, i * half : (i + 1) * half], got_rows[:, i * half : (i + 1) * half], 1
        )
        for i in range(4)
    ]
    return (
        layer_out,
        hidden_grad,
        gain_parts[0],
        gain_parts[1],
        gain_parts[2],
        gain_parts[3],
        weight_grads[0],
        weight_grads[1],
        weight_grads[2],
        weight_grads[3],
        router_part,
        *expert_grad,
    )


def solution(mesh):
    return jax.shard_map(
        on_device,
        mesh=mesh,
        in_specs=(
            P(("dp", "expert"), None),
            P(("dp", "expert"), None),
            P(("dp", "expert")),
            P(("dp", "expert")),
            P(("dp", "expert")),
            P(("dp", "expert")),
            P(("dp", "expert"), None),
            P(("dp", "expert"), None),
            P(("dp", "expert"), None),
            P(("dp", "expert"), None),
            P(("dp", "expert"), None),
            P("expert", None, "dp"),
            P("expert", None, "dp"),
            P("expert", "dp", None),
            P(("dp", "expert"), None),
            P(("dp", "expert"), None),
        ),
        out_specs=(
            P(("dp", "expert"), None),
            P(("dp", "expert"), None),
            P(("dp", "expert")),
            P(("dp", "expert")),
            P(("dp", "expert")),
            P(("dp", "expert")),
            P(("dp", "expert"), None),
            P(("dp", "expert"), None),
            P(("dp", "expert"), None),
            P(("dp", "expert"), None),
            P(("dp", "expert"), None),
            P("expert", None, "dp"),
            P("expert", None, "dp"),
            P("expert", "dp", None),
        ),
        check_vma=False,
    )
```

time: 2530 us -> 864 us (0.34)
  waiting for transfers between devices: 1510 us -> 242 us
  blocking collectives: 341 us -> 0 us
  Pallas kernels: 0 us -> 313 us
  matrix products: 287 us -> 3.94 us
  local copies, waits for them, and re-layouts: 261 us -> 123 us
  starting transfers between devices: 22 us -> 78.6 us
    all_to_all x4 -> x0, waiting for transfers between devices: 668 us -> none  [the longest x1 238 us: on_device(): lax.all_to_all(outgoing_grad, 'expert', split_axis=0, concat_axis=1, tile...]
    reduce_scatter x7 -> x0, waiting for transfers between devices: 612 us -> none  [the longest x1 187 us: on_device(): lax.psum_scatter(value_grad, ('dp', 'expert'), scatter_dimension=0, tiled...]
    pallas_call x0 -> x22, Pallas kernels: none -> 313 us  [the longest x3 76.1 us: experts_spread(): pl.pallas_call(functools.partial(spread_body, cap, ff, nb, shape, kinds,...]
    dot_general x31 -> x1, matrix products: 285 us -> 3.94 us  [on_device(): jnp.einsum('tc,td->cd', jnp.concatenate([context, context_other], axis=0)...]
    all_gather x1 -> x0, blocking collectives: 258 us -> none  [on_device(): lax.all_gather(router_weight, ('dp', 'expert'), axis=0, tiled=True)]
    ppermute x0 -> x102, waiting for transfers between devices: none -> 242 us  [the longest x81 200 us: swap(): return lax.ppermute(v, axis, [(i, i ^ bit) for i in range(size)])]
    all_gather x7 -> x0, waiting for transfers between devices: 225 us -> none  [the longest x1 71.2 us: on_device(): lax.all_gather(query_weight, ('dp', 'expert'), axis=0, tiled=True)]
    gather x6 -> x0, local copies, waits for them, and re-layouts: 114 us -> none  [the longest x2 42 us: on_device(): out_upstream[pick]]
  transfers between devices with their start and end apart: 19 -> 102, of which waited for: 11 -> 40; matrix products, arithmetic and copies ran while one was open for 18% -> 20% of each run, Pallas kernels for 0% -> 36%
where the time goes in v2:
time: 864 us; the launch traced here: 853 us
  Pallas kernels  313 us (36%)
  waiting for transfers between devices  242 us (28%)
  local copies, waits for them, and re-layouts  123 us (14%)
  other arithmetic  90.1 us (10%)
  starting transfers between devices  78.6 us (9%)
    ppermute x81, waiting for transfers between devices, swap(): return lax.ppermute(v, axis, [(i, i ^ bit) for i in range(size)])  200 us
    pallas_call x3, Pallas kernels, experts_spread(): pl.pallas_call(functools.partial(spread_body, cap, ff, nb, shape, kinds,...  76.1 us
    ppermute x81, starting transfers between devices, swap(): return lax.ppermute(v, axis, [(i, i ^ bit) for i in range(size)])  67.1 us
    pallas_call x1, Pallas kernels, experts_first(): pl.pallas_call(functools.partial(first_body, cap, ff, rb, nb, src, team,...  63.6 us
    ppermute x21, waiting for transfers between devices, ring(): lax.ppermute(v, 'expert', [(i, (i + 2) % owners) for i in range(owners)])  41.1 us
    dynamic_update_slice x20, local copies, waits for them, and re-layouts, put(): kept = lax.dynamic_update_slice(kept, v[:, :main], (row, 0))  40.8 us
    pallas_call x1, Pallas kernels, experts_last(): pl.pallas_call(functools.partial(last_body, ff, rb, nb, shape, pieces), o...  30.8 us
    convert_element_type x10, other arithmetic, move(): self.value = ring(self.value.astype(bf16))  28.1 us
  transfers between devices with their start and end apart: 102, of which 40 were waited for; matrix products, arithmetic and copies ran while one was open for 20% of the time, Pallas kernels for 36%

profile of v2, /device:TPU:0, one launch (start us, length us, event | category | flops | bytes accessed | tf_op | source)
XLA Modules:
  0.0 852.9 jit_solution(7468695896491544535)
XLA Ops:
  58.9 19.3 %collective-permute-done.7 = bf16[64,4224]{1,0:T(8,128)(2,1)} collective-permute-done((bf16[64,4224]{1,0:T(8,128)(2,1)}, bf16[64,4224]{1,0:T(8,128)(2,1)}, u32[]{:S(2)}, u32[]{:S(2)}) %collective-permute-start.7) | collective-permute-done | bytes 540704 | tf_op jit(solution)/shard_map/ppermute | solution.py:1225
  102.0 13.0 %collective-permute-done.12 = bf16[64,4224]{1,0:T(8,128)(2,1)} collective-permute-done((bf16[64,4224]{1,0:T(8,128)(2,1)}, bf16[64,4224]{1,0:T(8,128)(2,1)}, u32[]{:S(2)}, u32[]{:S(2)}) %collective-permute-start.12) | collective-permute-done | bytes 540704 | tf_op jit(solution)/shard_map/ppermute | solution.py:1225
  138.8 10.7 %collective-permute-done.16 = bf16[64,4224]{1,0:T(8,128)(2,1)} collective-permute-done((bf16[64,4224]{1,0:T(8,128)(2,1)}, bf16[64,4224]{1,0:T(8,128)(2,1)}, u32[]{:S(2)}, u32[]{:S(2)}) %collective-permute-start.16) | collective-permute-done | bytes 540704 | tf_op jit(solution)/shard_map/ppermute | solution.py:1225
  176.0 9.4 %shard_map.269 = (bf16[256,2048]{1,0:T(8,128)(2,1)}, f32[256,6144]{1,0:T(8,128)}, f32[256,1]{1,0:T(8,128)}, f32[256,1]{1,0:T(8,128)}) custom-call(bf16[256,2048]{1,0:T(8,128)(2,1)} %x_ref.1, f32[1,2048]{1,0:T(1,128)} %get-tuple-element.794.refs_1_.gain_ref, bf16[2048,4096]{1,0:T(8,128)(2,1)} %slice_dynamic-update-slice_fusion.12.refs_2_.wm_ref), custom_call_target="tpu_custom_call" | custom-call | tf_op jit(solution)/shard_map/pallas_call | solution.py:662
  187.0 11.0 %collective-permute-done.22.rest_20_.rest_4_ = bf16[2,256,1024]{2,1,0:T(8,128)(2,1)} collective-permute-done((bf16[2,256,1024]{2,1,0:T(8,128)(2,1)}, bf16[2,256,1024]{2,1,0:T(8,128)(2,1)}, u32[]{:S(2)}, u32[]{:S(2)}) %collective-permute-start.22) | collective-permute-done | bytes 1048608 | tf_op jit(solution)/shard_map/ppermute | solution.py:1225
  198.7 4.5 collective-permute-done.24.rest_12_
  206.9 9.0 %shard_map.270 = (f32[256,6144]{1,0:T(8,128)}, f32[256,1]{1,0:T(8,128)}, f32[256,1]{1,0:T(8,128)}) custom-call(bf16[256,2048]{1,0:T(8,128)(2,1)} %get-tuple-element.439.refs_0_.n_ref, bf16[2048,4096]{1,0:T(8,128)(2,1)} %collective-permute-done.21.refs_1_.wo_ref, f32[256,1]{1,0:T(8,128)} %get-tuple-element.416.refs_2_, ...), custom_call_target="tpu_custom_call", output_to_operand_aliasing={{0}: (4, {})} | custom-call | tf_op jit(solution)/shard_map/pallas_call | solution.py:686
  215.9 9.3 %shard_map.271 = (bf16[256,2048]{1,0:T(8,128)(2,1)}, bf16[256,2048]{1,0:T(8,128)(2,1)}, bf16[256,2048]{1,0:T(8,128)(2,1)}, bf16[256,2048]{1,0:T(8,128)(2,1)}) custom-call(f32[256,6144]{1,0:T(8,128)} %get-tuple-element.419.q_ref.k_ref.v_ref.q_raw.k_raw, f32[256,6144]{1,0:T(8,128)} %get-tuple-element.419.q_ref.k_ref.v_ref.q_raw.k_raw, ...), custom_call_target="tpu_custom_call" | custom-call | tf_op jit(solution)/shard_map/pallas_call | solution.py:744
  225.3 10.1 %shard_map.272 = (f32[256,2048]{1,0:T(8,128)}, bf16[272,2048]{1,0:T(8,128)(2,1)}, f32[16,256]{1,0:T(8,128)}) custom-call(s32[1]{0:T(128)} %bitcast.core_ref, bf16[256,2048]{1,0:T(8,128)(2,1)} %get-tuple-element.574.ctx_ref, bf16[2048,4096]{1,0:T(8,128)(2,1)} %slice_dynamic-update-slice_fusion.12.refs_2_.wm_ref, ...), custom_call_target="tpu_custom_call" | custom-call | tf_op jit(solution)/shard_map/pallas_call | solution.py:827
  235.4 14.6 %collective-permute-done.25.rest_21_.rest_5_ = bf16[2,512,1024]{2,1,0:T(8,128)(2,1)} collective-permute-done((bf16[2,512,1024]{2,1,0:T(8,128)(2,1)S(1)}, bf16[2,512,1024]{2,1,0:T(8,128)(2,1)}, u32[]{:S(2)}, u32[]{:S(2)}) %collective-permute-start.25) | collective-permute-done | bytes 2097184 | tf_op jit(solution)/shard_map/ppermute | solution.py:1225
  255.1 19.2 %collective-permute-done.35.rest_22_.rest_6_ = bf16[2,256,1024]{2,1,0:T(8,128)(2,1)S(1)} collective-permute-done((bf16[2,256,1024]{2,1,0:T(8,128)(2,1)S(1)}, bf16[2,256,1024]{2,1,0:T(8,128)(2,1)S(1)}, u32[]{:S(2)}, u32[]{:S(2)}) %collective-permute-start.35) | collective-permute-done | bytes 1048608 | tf_op jit(solution)/shard_map/ppermute | solution.py:1225
  277.9 19.7 %collective-permute-done.40.rest_23_.rest_7_ = bf16[2,256,1024]{2,1,0:T(8,128)(2,1)S(1)} collective-permute-done((bf16[2,256,1024]{2,1,0:T(8,128)(2,1)S(1)}, bf16[2,256,1024]{2,1,0:T(8,128)(2,1)S(1)}, u32[]{:S(2)}, u32[]{:S(2)}) %collective-permute-start.40) | collective-permute-done | bytes 1048608 | tf_op jit(solution)/shard_map/ppermute | solution.py:1225
  305.1 13.7 %collective-permute-done.45.rest_24_.rest_8_ = bf16[2,256,1024]{2,1,0:T(8,128)(2,1)S(1)} collective-permute-done((bf16[2,256,1024]{2,1,0:T(8,128)(2,1)S(1)}, bf16[2,256,1024]{2,1,0:T(8,128)(2,1)S(1)}, u32[]{:S(2)}, u32[]{:S(2)}) %collective-permute-start.45) | collective-permute-done | bytes 1048608 | tf_op jit(solution)/shard_map/ppermute | solution.py:1225
  318.9 8.6 %collective-permute-done.46.rest_27_.rest_11_ = bf16[2,256,1024]{2,1,0:T(8,128)(2,1)S(1)} collective-permute-done((bf16[2,256,1024]{2,1,0:T(8,128)(2,1)S(1)}, bf16[2,256,1024]{2,1,0:T(8,128)(2,1)S(1)}, u32[]{:S(2)}, u32[]{:S(2)}) %collective-permute-start.46) | collective-permute-done | bytes 1048608 | tf_op jit(solution)/shard_map/ppermute | solution.py:1225
  337.8 63.6 %shard_map.274 = (bf16[2,2,1280,2048]{3,2,1,0:T(8,128)(2,1)}, bf16[2,3,1280,768]{3,2,1,0:T(8,128)(2,1)}, f32[2,1280,1]{2,1,0:T(8,128)}, f32[2,1280,1]{2,1,0:T(8,...) custom-call(bf16[272,2048]{1,0:T(8,128)(2,1)} %get-tuple-element.478, ...), custom_call_target="tpu_custom_call" | custom-call | tf_op jit(solution)/shard_map/pallas_call | solution.py:231
  403.4 30.8 %shard_map.275 = (bf16[2,3,1280,256]{3,2,1,0:T(8,128)(2,1)}, f32[2,1280,1]{2,1,0:T(8,128)}, bf16[2,192,1024]{2,1,0:T(8,128)(2,1)}, bf16[2,320,1024]{2,1,0:T(8,12...) custom-call(bf16[2,2,1280,2048]{3,2,1,0:T(8,128)(2,1)} %get-tuple-el, ...), custom_call_target="tpu_custom_call" | custom-call | tf_op jit(solution)/shard_map/pallas_call | solution.py:398
  436.5 25.3 %shard_map.276 = (bf16[2,272,2048]{2,1,0:T(8,128)(2,1)}, bf16[2,272,2048]{2,1,0:T(8,128)(2,1)}) custom-call(s32[1]{0:T(128)} %bitcast.23.number_ref, bf16[2,3,1280,768]{3,2,1,0:T(8,128)(2,1)} %get-tuple-element.649.ha_ref.h_ref, bf16[2,3,1280,256]{3,2,1,0:T(8,128)(2,1)} %get-tuple-element.534.hd_ref, f32[2,1280,1]{2,1,0:T(8,128)} %get-tuple-element.535.dgr, ...), custom_call_target="tpu_custom_call" | custom-call | tf_op jit(solution)/shard_map/pallas_call | solution.py:553
  461.9 4.5 collective-permute-done.53
  474.6 25.3 %shard_map.277 = (bf16[2,272,2048]{2,1,0:T(8,128)(2,1)}, bf16[2,272,2048]{2,1,0:T(8,128)(2,1)}) custom-call(s32[1]{0:T(128)} %bitcast.23.number_ref, bf16[2,3,1280,768]{3,2,1,0:T(8,128)(2,1)} %get-tuple-element.649.ha_ref.h_ref, bf16[2,3,1280,256]{3,2,1,0:T(8,128)(2,1)} %get-tuple-element.534.hd_ref, f32[2,1280,1]{2,1,0:T(8,128)} %get-tuple-element.535.dgr, ...), custom_call_target="tpu_custom_call" | custom-call | tf_op jit(solution)/shard_map/pallas_call | solution.py:553
  500.0 5.9 collective-permute-done.55.rest_2_
  513.0 25.4 %shard_map.278 = (bf16[4,256,2048]{2,1,0:T(8,128)(2,1)}, bf16[4,256,2048]{2,1,0:T(8,128)(2,1)}) custom-call(s32[1]{0:T(128)} %bitcast.23.number_ref, bf16[2,3,1280,768]{3,2,1,0:T(8,128)(2,1)} %get-tuple-element.649.ha_ref.h_ref, bf16[2,3,1280,256]{3,2,1,0:T(8,128)(2,1)} %get-tuple-element.534.hd_ref, f32[2,1280,1]{2,1,0:T(8,128)} %get-tuple-element.535.dgr, ...), custom_call_target="tpu_custom_call" | custom-call | tf_op jit(solution)/shard_map/pallas_call | solution.py:553
  555.2 12.1 %collective-permute-done.64 = bf16[2,256,1024]{2,1,0:T(8,128)(2,1)S(1)} collective-permute-done((bf16[2,256,1024]{2,1,0:T(8,128)(2,1)S(1)}, bf16[2,256,1024]{2,1,0:T(8,128)(2,1)S(1)}, u32[]{:S(2)}, u32[]{:S(2)}) %collective-permute-start.64) | collective-permute-done | bytes 1048608 | tf_op jit(solution)/shard_map/ppermute | solution.py:1225
  568.1 6.6 collective-permute-done.63
  583.1 12.1 %shard_map.279 = (f32[256,2048]{1,0:T(8,128)}, bf16[256,1024]{1,0:T(8,128)(2,1)}, bf16[256,1024]{1,0:T(8,128)(2,1)}, bf16[256,2048]{1,0:T(8,128)(2,1)}, f32[1,20...) custom-call(s32[1]{0:T(128)} %bitcast.core_ref, f32[272,2048]{1,0:T(8,128)} %bitcast_add_fusion.sum_ref, ...), custom_call_target="tpu_custom_call" | custom-call | tf_op jit(solution)/shard_map/pallas_call | solution.py:896
  610.5 21.3 %shard_map.280 = (bf16[2,3,256,1024]{3,2,1,0:T(8,128)(2,1)}, f32[1,2048]{1,0:T(1,128)}, f32[1,2048]{1,0:T(1,128)}) custom-call(bf16[256,2048]{1,0:T(8,128)(2,1)} %get-tuple-element.593.q_ref, bf16[256,2048]{1,0:T(8,128)(2,1)} %get-tuple-element.594.k_ref, bf16[256,2048]{1,0:T(8,128)(2,1)} %get-tuple-element.595.v_ref, ...), custom_call_target="tpu_custom_call" | custom-call | tf_op jit(solution)/shard_map/pallas_call | solution.py:988
  650.4 13.7 %shard_map.281 = (bf16[2048,1536]{1,0:T(8,128)(2,1)}, bf16[2048,1536]{1,0:T(8,128)(2,1)}) custom-call(bf16[256,2048]{1,0:T(8,128)(2,1)} %get-tuple-element.439.refs_0_.n_ref, bf16[256,2048]{1,0:T(8,128)(2,1)} %collective-permute-done.68.no_ref, bf16[2,3,256,1024]{3,2,1,0:T(8,128)(2,1)} %get-tuple-element.620.u_ref.ups_ref, bf16[3,256,1024]{2,1,0:T(8,128)(2,1)} %copy-done.43), custom_call_target="tpu_custom_call" | custom-call | tf_op jit(solution)/shard_map/pallas_call | solution.py:1039
  682.2 17.0 %shard_map.282 = (f32[256,2048]{1,0:T(8,128)}, f32[1,2048]{1,0:T(1,128)}) custom-call(bf16[2,3,256,1024]{3,2,1,0:T(8,128)(2,1)} %get-tuple-element.620.u_ref.ups_ref, bf16[2048,4096]{1,0:T(8,128)(2,1)} %slice_dynamic-update-slice_fusion.12.refs_2_.wm_ref, bf16[2048,4096]{1,0:T(8,128)(2,1)} %collective-permute-done.21.refs_1_.wo_ref, ...), custom_call_target="tpu_custom_call" | custom-call | tf_op jit(solution)/shard_map/pallas_call | solution.py:1093
  726.1 11.3 %collective-permute-done.85 = bf16[256,1536]{1,0:T(8,128)(2,1)} collective-permute-done((bf16[256,1536]{1,0:T(8,128)(2,1)}, bf16[256,1536]{1,0:T(8,128)(2,1)}, u32[]{:S(2)}, u32[]{:S(2)}) %collective-permute-start.85) | collective-permute-done | bytes 786464 | tf_op jit(solution)/shard_map/ppermute | solution.py:1225
  747.8 21.0 %collective-permute-done.83 = bf16[512,1536]{1,0:T(8,128)(2,1)S(1)} collective-permute-done((bf16[512,1536]{1,0:T(8,128)(2,1)}, bf16[512,1536]{1,0:T(8,128)(2,1)S(1)}, u32[]{:S(2)}, u32[]{:S(2)}) %collective-permute-start.83) | collective-permute-done | bytes 1572896 | tf_op jit(solution)/shard_map/ppermute | solution.py:1225
  781.0 15.4 %shard_map.283 = (bf16[2,768,1024]{2,1,0:T(8,128)(2,1)}, bf16[2,768,1024]{2,1,0:T(8,128)(2,1)}) custom-call(bf16[2,3,1280,768]{3,2,1,0:T(8,128)(2,1)} %get-tuple-element.649.ha_ref.h_ref, bf16[2,2,1280,2048]{3,2,1,0:T(8,128)(2,1)} %get-tuple-element.650.rg_ref), custom_call_target="tpu_custom_call" | custom-call | tf_op jit(solution)/shard_map/pallas_call | solution.py:597
  809.6 14.0 %shard_map.284 = (f32[2,2048,256]{2,1,0:T(8,128)}, f32[2,2048,256]{2,1,0:T(8,128)}, f32[2,256,2048]{2,1,0:T(8,128)}) custom-call(bf16[2,768,1024]{2,1,0:T(8,128)(2,1)} %get-tuple-element.670.low, bf16[2,768,1024]{2,1,0:T(8,128)(2,1)} %get-tuple-element.671.high, bf16[2,320,1024]{2,1,0:T(8,128)(2,1)} %collective-permute-done.49.rest_0_, ...), custom_call_target="tpu_custom_call" | custom-call | tf_op jit(solution)/shard_map/pallas_call | solution.py:1166
  830.5 11.9 %collective-permute-done.98 = bf16[128,3072]{1,0:T(8,128)(2,1)} collective-permute-done((bf16[128,3072]{1,0:T(8,128)(2,1)}, bf16[128,3072]{1,0:T(8,128)(2,1)}, u32[]{:S(2)}, u32[]{:S(2)}) %collective-permute-start.98) | collective-permute-done | bytes 786464 | tf_op jit(solution)/shard_map/ppermute | solution.py:1237
  (533 shorter events, 340.9 us)
Async XLA Ops:
  41.5 36.7 %collective-permute-start.4 = (bf16[128,4224]{1,0:T(8,128)(2,1)}, bf16[128,4224]{1,0:T(8,128)(2,1)}, u32[]{:S(2)}, u32[]{:S(2)}) collective-permute-start(bf16[128,4224]{1,0:T(8,128)(2,1)} %collective-permute-done.3), channel_id=1, source_target_pairs={{0,8},{8,0},{16,24},{24,16},{1,9},{9,1},{17,25},{25,17},{2,10},{10... | collective-permute-start | bytes 3244040 | tf_op jit(solution)/shard_map/ppermute | solution.py:1225
  42.0 36.2 %collective-permute-start.5 = (bf16[128,4224]{1,0:T(8,128)(2,1)}, bf16[128,4224]{1,0:T(8,128)(2,1)}, u32[]{:S(2)}, u32[]{:S(2)}) collective-permute-start(bf16[128,4224]{1,0:T(8,128)(2,1)} %collective-permute-done.3), channel_id=1, source_target_pairs={{0,16},{8,24},{16,0},{24,8},{1,17},{9,25},{17,1},{25,9},{2,18},{10... | collective-permute-start | bytes 3244040 | tf_op jit(solution)/shard_map/ppermute | solution.py:1225
  42.5 35.7 %collective-permute-start.6 = (bf16[128,4224]{1,0:T(8,128)(2,1)}, bf16[128,4224]{1,0:T(8,128)(2,1)}, u32[]{:S(2)}, u32[]{:S(2)}) collective-permute-start(bf16[128,4224]{1,0:T(8,128)(2,1)} %collective-permute-done.3), channel_id=1, source_target_pairs={{0,2},{1,3},{2,4},{3,5},{4,6},{5,7},{6,0},{7,1},{8,10},{9,11},{10,... | collective-permute-start | bytes 3244040 | tf_op jit(solution)/shard_map/ppermute | solution.py:1237
  44.7 33.4 %collective-permute-start.7 = (bf16[64,4224]{1,0:T(8,128)(2,1)}, bf16[64,4224]{1,0:T(8,128)(2,1)}, u32[]{:S(2)}, u32[]{:S(2)}) collective-permute-start(bf16[64,4224]{1,0:T(8,128)(2,1)} %get-tuple-element.360), channel_id=1, source_target_pairs={{0,16},{8,24},{16,0},{24,8},{1,17},{9,25},{17,1},{25,9},{2,18},{10... | collective-permute-start | bytes 1622024 | tf_op jit(solution)/shard_map/ppermute | solution.py:1225
  46.3 31.9 %collective-permute-start.8 = (bf16[64,4224]{1,0:T(8,128)(2,1)}, bf16[64,4224]{1,0:T(8,128)(2,1)}, u32[]{:S(2)}, u32[]{:S(2)}) collective-permute-start(bf16[64,4224]{1,0:T(8,128)(2,1)} %get-tuple-element.361), channel_id=1, source_target_pairs={{0,8},{8,0},{16,24},{24,16},{1,9},{9,1},{17,25},{25,17},{2,10},{10... | collective-permute-start | bytes 1622024 | tf_op jit(solution)/shard_map/ppermute | solution.py:1225
  78.2 36.8 %collective-permute-start.9 = (bf16[128,4224]{1,0:T(8,128)(2,1)}, bf16[128,4224]{1,0:T(8,128)(2,1)}, u32[]{:S(2)}, u32[]{:S(2)}) collective-permute-start(bf16[128,4224]{1,0:T(8,128)(2,1)} %collective-permute-done.6), channel_id=1, source_target_pairs={{0,8},{8,0},{16,24},{24,16},{1,9},{9,1},{17,25},{25,17},{2,10},{10... | collective-permute-start | bytes 3244040 | tf_op jit(solution)/shard_map/ppermute | solution.py:1225
  79.8 35.3 %collective-permute-start.10 = (bf16[128,4224]{1,0:T(8,128)(2,1)}, bf16[128,4224]{1,0:T(8,128)(2,1)}, u32[]{:S(2)}, u32[]{:S(2)}) collective-permute-start(bf16[128,4224]{1,0:T(8,128)(2,1)} %collective-permute-done.6), channel_id=1, source_target_pairs={{0,16},{8,24},{16,0},{24,8},{1,17},{9,25},{17,1},{25,9},{2,18},{10... | collective-permute-start | bytes 3244040 | tf_op jit(solution)/shard_map/ppermute | solution.py:1225
  80.3 34.8 %collective-permute-start.11 = (bf16[128,4224]{1,0:T(8,128)(2,1)}, bf16[128,4224]{1,0:T(8,128)(2,1)}, u32[]{:S(2)}, u32[]{:S(2)}) collective-permute-start(bf16[128,4224]{1,0:T(8,128)(2,1)} %collective-permute-done.6), channel_id=1, source_target_pairs={{0,2},{1,3},{2,4},{3,5},{4,6},{5,7},{6,0},{7,1},{8,10},{9,11},{10,... | collective-permute-start | bytes 3244040 | tf_op jit(solution)/shard_map/ppermute | solution.py:1237
  82.5 32.5 %collective-permute-start.12 = (bf16[64,4224]{1,0:T(8,128)(2,1)}, bf16[64,4224]{1,0:T(8,128)(2,1)}, u32[]{:S(2)}, u32[]{:S(2)}) collective-permute-start(bf16[64,4224]{1,0:T(8,128)(2,1)} %get-tuple-element.368), channel_id=1, source_target_pairs={{0,16},{8,24},{16,0},{24,8},{1,17},{9,25},{17,1},{25,9},{2,18},{10... | collective-permute-start | bytes 1622024 | tf_op jit(solution)/shard_map/ppermute | solution.py:1225
  115.0 34.5 %collective-permute-start.14 = (bf16[128,4224]{1,0:T(8,128)(2,1)}, bf16[128,4224]{1,0:T(8,128)(2,1)}, u32[]{:S(2)}, u32[]{:S(2)}) collective-permute-start(bf16[128,4224]{1,0:T(8,128)(2,1)} %collective-permute-done.11), channel_id=1, source_target_pairs={{0,8},{8,0},{16,24},{24,16},{1,9},{9,1},{17,25},{25,17},{2,10},{10... | collective-permute-start | bytes 3244040 | tf_op jit(solution)/shard_map/ppermute | solution.py:1225
  115.4 34.1 %collective-permute-start.15 = (bf16[128,4224]{1,0:T(8,128)(2,1)}, bf16[128,4224]{1,0:T(8,128)(2,1)}, u32[]{:S(2)}, u32[]{:S(2)}) collective-permute-start(bf16[128,4224]{1,0:T(8,128)(2,1)} %collective-permute-done.11), channel_id=1, source_target_pairs={{0,16},{8,24},{16,0},{24,8},{1,17},{9,25},{17,1},{25,9},{2,18},{10... | collective-permute-start | bytes 3244040 | tf_op jit(solution)/shard_map/ppermute | solution.py:1225
  170.1 33.1 %collective-permute-start.21 = (bf16[2048,4096]{1,0:T(8,128)(2,1)}, bf16[2048,4096]{1,0:T(8,128)(2,1)}, u32[]{:S(2)}, u32[]{:S(2)}) collective-permute-start(bf16[2048,4096]{1,0:T(8,128)(2,1)} %slice_dynamic-update-slice_fusion.12.refs_2_.wm_ref), channel_id=1, source_target_pairs={{0,1},{1,0},{2,3},{3,2},{4,5},{5,4},{6,7},{7,6},{8,9},{9,8},{10,11... | collective-permute-start | bytes 50331656 | tf_op jit(solution)/shard_map/ppermute | solution.py:1225
  203.2 46.7 %collective-permute-start.25 = (bf16[2,512,1024]{2,1,0:T(8,128)(2,1)S(1)}, bf16[2,512,1024]{2,1,0:T(8,128)(2,1)}, u32[]{:S(2)}, u32[]{:S(2)}) collective-permute-start(bf16[2,512,1024]{2,1,0:T(8,128)(2,1)S(1)} %pad_maximum_fusion.rest_17_.rest_1_), channel_id=1, source_target_pairs={{0,8},{8,0},{16,24},{24,16},{1,9},{9,1},{17,25},{25,17},{2,10},{10... | collective-permute-start | bytes 6291464 | tf_op jit(solution)/shard_map/ppermute | solution.py:1225
  204.2 46.7 %collective-permute-start.26 = (bf16[2,512,1024]{2,1,0:T(8,128)(2,1)}, bf16[2,512,1024]{2,1,0:T(8,128)(2,1)}, u32[]{:S(2)}, u32[]{:S(2)}) collective-permute-start(bf16[2,512,1024]{2,1,0:T(8,128)(2,1)} %pad_maximum_fusion.1.rest_19_.rest_3_), channel_id=1, source_target_pairs={{0,16},{8,24},{16,0},{24,8},{1,17},{9,25},{17,1},{25,9},{2,18},{10... | collective-permute-start | bytes 6291464 | tf_op jit(solution)/shard_map/ppermute | solution.py:1225
  327.5 74.0 %collective-permute-start.29 = (bf16[2,512,1024]{2,1,0:T(8,128)(2,1)}, bf16[2,512,1024]{2,1,0:T(8,128)(2,1)S(1)}, u32[]{:S(2)}, u32[]{:S(2)}) collective-permute-start(bf16[2,512,1024]{2,1,0:T(8,128)(2,1)} %collective-permute-done.25.rest_21_.rest_5_), channel_id=1, source_target_pairs={{0,16},{8,24},{16,0},{24,8},{1,17},{9,25},{17,1},{25,9},{2,18},{10... | collective-permute-start | bytes 6291464 | tf_op jit(solution)/shard_map/ppermute | solution.py:1225
  328.2 73.3 %collective-permute-start.31 = (bf16[2,512,1024]{2,1,0:T(8,128)(2,1)}, bf16[2,512,1024]{2,1,0:T(8,128)(2,1)}, u32[]{:S(2)}, u32[]{:S(2)}) collective-permute-start(bf16[2,512,1024]{2,1,0:T(8,128)(2,1)} %collective-permute-done.26.rest_29_.rest_13_), channel_id=1, source_target_pairs={{0,8},{8,0},{16,24},{24,16},{1,9},{9,1},{17,25},{25,17},{2,10},{10... | collective-permute-start | bytes 6291464 | tf_op jit(solution)/shard_map/ppermute | solution.py:1225
  331.8 69.6 %collective-permute-start.28 = (bf16[2,256,1024]{2,1,0:T(8,128)(2,1)}, bf16[2,256,1024]{2,1,0:T(8,128)(2,1)S(1)}, u32[]{:S(2)}, u32[]{:S(2)}) collective-permute-start(bf16[2,256,1024]{2,1,0:T(8,128)(2,1)} %collective-permute-done.22.rest_20_.rest_4_), channel_id=1, source_target_pairs={{0,16},{8,24},{16,0},{24,8},{1,17},{9,25},{17,1},{25,9},{2,18},{10... | collective-permute-start | bytes 3145736 | tf_op jit(solution)/shard_map/ppermute | solution.py:1225
  334.3 67.1 %collective-permute-start.30 = (bf16[2,256,1024]{2,1,0:T(8,128)(2,1)}, bf16[2,256,1024]{2,1,0:T(8,128)(2,1)}, u32[]{:S(2)}, u32[]{:S(2)}) collective-permute-start(bf16[2,256,1024]{2,1,0:T(8,128)(2,1)} %collective-permute-done.23.rest_28_.rest_12_), channel_id=1, source_target_pairs={{0,8},{8,0},{16,24},{24,16},{1,9},{9,1},{17,25},{25,17},{2,10},{10... | collective-permute-start | bytes 3145736 | tf_op jit(solution)/shard_map/ppermute | solution.py:1225
  401.5 32.8 %collective-permute-start.49 = (bf16[2,320,1024]{2,1,0:T(8,128)(2,1)}, bf16[2,320,1024]{2,1,0:T(8,128)(2,1)}, u32[]{:S(2)}, u32[]{:S(2)}) collective-permute-start(bf16[2,320,1024]{2,1,0:T(8,128)(2,1)} %get-tuple-element.528), channel_id=1, source_target_pairs={{0,8},{8,0},{16,24},{24,16},{1,9},{9,1},{17,25},{25,17},{2,10},{10... | collective-permute-start | bytes 3932168 | tf_op jit(solution)/shard_map/ppermute | solution.py:1225
  402.5 31.7 %collective-permute-start.50 = (bf16[2,320,1024]{2,1,0:T(8,128)(2,1)}, bf16[2,320,1024]{2,1,0:T(8,128)(2,1)}, u32[]{:S(2)}, u32[]{:S(2)}) collective-permute-start(bf16[2,320,1024]{2,1,0:T(8,128)(2,1)} %get-tuple-element.529), channel_id=1, source_target_pairs={{0,16},{8,24},{16,0},{24,8},{1,17},{9,25},{17,1},{25,9},{2,18},{10... | collective-permute-start | bytes 3932168 | tf_op jit(solution)/shard_map/ppermute | solution.py:1225
  470.5 36.1 %collective-permute-start.54 = (bf16[272,2048]{1,0:T(8,128)(2,1)}, bf16[272,2048]{1,0:T(8,128)(2,1)S(1)}, u32[]{:S(2)}, u32[]{:S(2)}) collective-permute-start(bf16[272,2048]{1,0:T(8,128)(2,1)} %fusion.14), channel_id=1, source_target_pairs={{0,2},{1,3},{2,4},{3,5},{4,6},{5,7},{6,0},{7,1},{8,10},{9,11},{10,... | collective-permute-start | bytes 3342344 | tf_op jit(solution)/shard_map/ppermute | solution.py:1237
  472.4 33.5 %collective-permute-start.55 = (bf16[2,176,1024]{2,1,0:T(8,128)(2,1)}, bf16[2,176,1024]{2,1,0:T(8,128)(2,1)}, u32[]{:S(2)}, u32[]{:S(2)}) collective-permute-start(bf16[2,176,1024]{2,1,0:T(8,128)(2,1)} %get-tuple-element.551), channel_id=1, source_target_pairs={{0,8},{8,0},{16,24},{24,16},{1,9},{9,1},{17,25},{25,17},{2,10},{10... | collective-permute-start | bytes 2162696 | tf_op jit(solution)/shard_map/ppermute | solution.py:1225
  473.4 33.2 %collective-permute-start.56 = (bf16[2,176,1024]{2,1,0:T(8,128)(2,1)}, bf16[2,176,1024]{2,1,0:T(8,128)(2,1)}, u32[]{:S(2)}, u32[]{:S(2)}) collective-permute-start(bf16[2,176,1024]{2,1,0:T(8,128)(2,1)} %get-tuple-element.554), channel_id=1, source_target_pairs={{0,16},{8,24},{16,0},{24,8},{1,17},{9,25},{17,1},{25,9},{2,18},{10... | collective-permute-start | bytes 2162696 | tf_op jit(solution)/shard_map/ppermute | solution.py:1225
  507.6 34.0 %collective-permute-start.60 = (bf16[2,272,2048]{2,1,0:T(8,128)(2,1)}, bf16[2,272,2048]{2,1,0:T(8,128)(2,1)}, u32[]{:S(2)}, u32[]{:S(2)}) collective-permute-start(bf16[2,272,2048]{2,1,0:T(8,128)(2,1)} %get-tuple-element.558), channel_id=1, source_target_pairs={{0,1},{1,0},{2,3},{3,2},{4,5},{5,4},{6,7},{7,6},{8,9},{9,8},{10,11... | collective-permute-start | bytes 6684680 | tf_op jit(solution)/shard_map/ppermute | solution.py:1225
  507.6 31.4 %collective-permute-start.61 = (bf16[2,320,1024]{2,1,0:T(8,128)(2,1)}, bf16[2,320,1024]{2,1,0:T(8,128)(2,1)S(1)}, u32[]{:S(2)}, u32[]{:S(2)}) collective-permute-start(bf16[2,320,1024]{2,1,0:T(8,128)(2,1)} %get-tuple-element.562), channel_id=1, source_target_pairs={{0,8},{8,0},{16,24},{24,16},{1,9},{9,1},{17,25},{25,17},{2,10},{10... | collective-permute-start | bytes 3932168 | tf_op jit(solution)/shard_map/ppermute | solution.py:1225
  541.6 33.1 %collective-permute-start.66 = (bf16[4,256,2048]{2,1,0:T(8,128)(2,1)}, bf16[4,256,2048]{2,1,0:T(8,128)(2,1)S(1)}, u32[]{:S(2)}, u32[]{:S(2)}) collective-permute-start(bf16[4,256,2048]{2,1,0:T(8,128)(2,1)} %get-tuple-element.575), channel_id=1, source_target_pairs={{0,1},{1,0},{2,3},{3,2},{4,5},{5,4},{6,7},{7,6},{8,9},{9,8},{10,11... | collective-permute-start | bytes 12582920 | tf_op jit(solution)/shard_map/ppermute | solution.py:1225
  541.6 59.0 %collective-permute-start.68 = (bf16[256,2048]{1,0:T(8,128)(2,1)}, bf16[256,2048]{1,0:T(8,128)(2,1)}, u32[]{:S(2)}, u32[]{:S(2)}) collective-permute-start(bf16[256,2048]{1,0:T(8,128)(2,1)} %get-tuple-element.439.refs_0_.n_ref), channel_id=1, source_target_pairs={{0,1},{1,0},{2,3},{3,2},{4,5},{5,4},{6,7},{7,6},{8,9},{9,8},{10,11... | collective-permute-start | bytes 3145736 | tf_op jit(solution)/shard_map/ppermute | solution.py:1225
  649.3 58.5 %collective-permute-start.82 = (bf16[256,2048]{1,0:T(8,128)(2,1)}, bf16[256,2048]{1,0:T(8,128)(2,1)}, u32[]{:S(2)}, u32[]{:S(2)}) collective-permute-start(bf16[256,2048]{1,0:T(8,128)(2,1)} %fusion.7), channel_id=1, source_target_pairs={{0,2},{1,3},{2,4},{3,5},{4,6},{5,7},{6,0},{7,1},{8,10},{9,11},{10,... | collective-permute-start | bytes 3145736 | tf_op jit(solution)/shard_map/ppermute | solution.py:1237
  669.6 38.1 %collective-permute-start.79 = (bf16[512,1536]{1,0:T(8,128)(2,1)}, bf16[512,1536]{1,0:T(8,128)(2,1)}, u32[]{:S(2)}, u32[]{:S(2)}) collective-permute-start(bf16[512,1536]{1,0:T(8,128)(2,1)} %pad_maximum_fusion.5), channel_id=1, source_target_pairs={{0,8},{8,0},{16,24},{24,16},{1,9},{9,1},{17,25},{25,17},{2,10},{10... | collective-permute-start | bytes 4718600 | tf_op jit(solution)/shard_map/ppermute | solution.py:1225
  670.7 37.0 %collective-permute-start.80 = (bf16[512,1536]{1,0:T(8,128)(2,1)}, bf16[512,1536]{1,0:T(8,128)(2,1)}, u32[]{:S(2)}, u32[]{:S(2)}) collective-permute-start(bf16[512,1536]{1,0:T(8,128)(2,1)} %pad_maximum_fusion.6), channel_id=1, source_target_pairs={{0,16},{8,24},{16,0},{24,8},{1,17},{9,25},{17,1},{25,9},{2,18},{10... | collective-permute-start | bytes 4718600 | tf_op jit(solution)/shard_map/ppermute | solution.py:1225
  721.8 46.9 %collective-permute-start.83 = (bf16[512,1536]{1,0:T(8,128)(2,1)}, bf16[512,1536]{1,0:T(8,128)(2,1)S(1)}, u32[]{:S(2)}, u32[]{:S(2)}) collective-permute-start(bf16[512,1536]{1,0:T(8,128)(2,1)} %pad_maximum_fusion.7), channel_id=1, source_target_pairs={{0,8},{8,0},{16,24},{24,16},{1,9},{9,1},{17,25},{25,17},{2,10},{10... | collective-permute-start | bytes 4718600 | tf_op jit(solution)/shard_map/ppermute | solution.py:1225
  723.4 45.3 %collective-permute-start.84 = (bf16[512,1536]{1,0:T(8,128)(2,1)}, bf16[512,1536]{1,0:T(8,128)(2,1)S(1)}, u32[]{:S(2)}, u32[]{:S(2)}) collective-permute-start(bf16[512,1536]{1,0:T(8,128)(2,1)} %pad_maximum_fusion.8), channel_id=1, source_target_pairs={{0,16},{8,24},{16,0},{24,8},{1,17},{9,25},{17,1},{25,9},{2,18},{10... | collective-permute-start | bytes 4718600 | tf_op jit(solution)/shard_map/ppermute | solution.py:1225
  (154 other events, 3088.5 us)

commit v3 on v2

--- a/solution.py
+++ b/solution.py
@@ -921,7 +921,7 @@
 
 
 def attend_back_body(width, q_ref, k_ref, v_ref, u_ref, q_raw, k_raw, qs, ks, qg, kg, cos, sin, doc_row, doc_col,
-                     ups, qg_out, kg_out, q_back, k_back, v_back, q_mean, k_mean):
+                     ups_mine, ups_other, qg_out, kg_out, q_back, k_back, v_back, q_mean, k_mean):
     phase, h = pl.program_id(0), pl.program_id(1)
     nb = q_ref.shape[1]
     q_scale, k_scale = row_scale(qs[...], width), row_scale(ks[...], width)
@@ -959,12 +959,24 @@
 
     @pl.when(phase == 1)
     def _():
-        for i, (raw, scale, gain, mean, kept) in enumerate(
-            ((q_raw, q_scale, qg, q_mean, q_back), (k_raw, k_scale, kg, k_mean, k_back))
+        ups = []
+        for raw, scale, gain, mean, kept in (
+            (q_raw, q_scale, qg, q_mean, q_back),
+            (k_raw, k_scale, kg, k_mean, k_back),
         ):
             up = scale * (kept[h] * gain[...] - raw[...] * scale * (mean[...] / width))
-            ups[0, i] = up.astype(jnp.bfloat16)
-        ups[0, 2] = v_back[h]
+            ups.append(up.astype(jnp.bfloat16))
+        ups.append(v_back[h])
+
+        @pl.when(h < 2)
+        def _():
+            for i in range(3):
+                ups_mine[i] = ups[i]
+
+        @pl.when(h >= 2)
+        def _():
+            for i in range(3):
+                ups_other[i] = ups[i]
 
 
 def attend_back(q, k, v, up, raw, qs, ks, qg, kg, cos, sin, document):
@@ -981,21 +993,30 @@
     def whole(*shape):
         return pl.BlockSpec(shape, lambda p, h: (0, 0))
 
-    def out_place(p, h):
-        at = jnp.where(p == 0, 0, h)
-        return (at // 2, 0, 0, at % 2)
-
+    def mine_place(p, h):
+        return (0, 0, jnp.where(p == 0, 0, jnp.minimum(h, 1)))
+
+    def other_place(p, h):
+        return (0, 0, jnp.where(p == 0, 0, jnp.maximum(h - 2, 0)))
+
+    side = jax.ShapeDtypeStruct((3, tokens, width // 2), jnp.bfloat16)
     return pl.pallas_call(
         functools.partial(attend_back_body, width),
         out_shape=(
-            jax.ShapeDtypeStruct((2, 3, tokens, width // 2), jnp.bfloat16),
+            side,
+            side,
             jax.ShapeDtypeStruct((1, width), f32),
             jax.ShapeDtypeStruct((1, width), f32),
         ),
         grid=(2, 4),
         in_specs=[head, head, head, head, part(0), part(1), whole(tokens, 1), whole(tokens, 1), gain, gain]
         + [whole(tokens, HD), whole(tokens, HD), whole(1, tokens), whole(tokens, 1)],
-        out_specs=(pl.BlockSpec((1, 3, tokens, nb), out_place), whole(1, width), whole(1, width)),
+        out_specs=(
+            pl.BlockSpec((3, tokens, nb), mine_place),
+            pl.BlockSpec((3, tokens, nb), other_place),
+            whole(1, width),
+            whole(1, width),
+        ),
         scratch_shapes=[
             pltpu.VMEM((4, tokens, nb), f32),
             pltpu.VMEM((4, tokens, nb), f32),
@@ -1016,7 +1037,7 @@
         pair[:, 0:tokens] = n_ref[...].T
         pair[:, tokens : 2 * tokens] = no_ref[...].T
 
-    ups = jnp.concatenate([u_ref[0, 0], uo_ref[0]], axis=0)
+    ups = jnp.concatenate([u_ref[0], uo_ref[0]], axis=0)
     got = dot_nn(pair[...], ups).astype(jnp.bfloat16)
 
     @pl.when(i < 3)
@@ -1043,7 +1064,7 @@
         in_specs=[
             whole(tokens, width),
             whole(tokens, width),
-            pl.BlockSpec((1, 1, tokens, nb), lambda i: (0, i // 2, 0, i % 2)),
+            pl.BlockSpec((1, tokens, nb), lambda i: (i // 2, 0, i % 2)),
             pl.BlockSpec((1, tokens, nb), lambda i: (i // 2, 0, i % 2)),
         ],
         out_specs=(
@@ -1055,7 +1076,7 @@
     )(normed, normed_other, ups, got)
 
 
-def input_grad_body(ups_ref, wm_ref, wo_ref, x_ref, grad_ref, gain_ref, out_ref, gain_out, total, turned_ups):
+def input_grad_body(um_ref, uo_ref, wm_ref, wo_ref, x_ref, grad_ref, gain_ref, out_ref, gain_out, total, turned_ups):
     n = pl.program_id(0)
     tokens, width = x_ref.shape
     half = width // 2
@@ -1063,9 +1084,9 @@
 
     @pl.when(n == 0)
     def _():
-        for w in range(2):
+        for w, ref in enumerate((um_ref, uo_ref)):
             for i in range(3):
-                turned_ups[w, i * half : (i + 1) * half, :] = ups_ref[w, i].T
+                turned_ups[w, i * half : (i + 1) * half, :] = ref[i].T
 
     acc = dot_nn(wm_ref[...], turned_ups[0]) + dot_nn(wo_ref[...], turned_ups[1])
     total[n] = acc.T
@@ -1095,7 +1116,8 @@
         out_shape=(jax.ShapeDtypeStruct((tokens, width), f32), jax.ShapeDtypeStruct((1, width), f32)),
         grid=(width // nb,),
         in_specs=[
-            whole(*ups.shape),
+            whole(*ups[0].shape),
+            whole(*ups[1].shape),
             pl.BlockSpec((nb, 3 * width // 2), lambda n: (n, 0)),
             pl.BlockSpec((nb, 3 * width // 2), lambda n: (n, 0)),
             whole(tokens, width),
@@ -1108,7 +1130,7 @@
             pltpu.VMEM((2, 3 * width // 2, tokens), jnp.bfloat16),
         ],
         compiler_params=kernel_params(),
-    )(ups, weights, weights_other, x, grad, gain[None])
+    )(*ups, weights, weights_other, x, grad, gain[None])
 
 
 def cut_body(x_ref, y_ref, low, high):
@@ -1542,7 +1564,7 @@
     mixed.move()
     more.append(send_more(1))
     got_branch = swap_core(branch_other)
-    ups, query_gain_grad, key_gain_grad = attend_back(
+    *ups, query_gain_grad, key_gain_grad = attend_back(
         query_heads,
         key_heads,
         value_heads,
@@ -1559,7 +1581,7 @@
     ups, mixed.value, got_branch, more = fence((ups, mixed.value, got_branch, more))
     got_ups = swap_core(ups[1])
     more.append(send_more(2))
-    first, second = qkv_grad(normed, normed_other, ups, got_ups)
+    first, second = qkv_grad(normed, normed_other, ups[0], got_ups)
     mixed.add()
     mixed.move()
     def several(v, picks):
@@ -1658,10 +1680,19 @@
     near_more, output_sum.value = fence((near_more, output_sum.value))
     output_sum.add()
     output_sum.move()
-    blocks = step_three(near, *near_got, *near_more)
+    weight_sum = Total(step_three(near, *near_got, *near_more))
+    weight_sum.value = weight_sum.value.astype(bf16)
     small_sum = fold(small_sum)
-    far_got, output_sum.value, blocks, small_sum = fence(
-        (far_got, output_sum.value, blocks, small_sum)
+    weight_sum.value, small_sum = fence((weight_sum.value, small_sum))
+    for _ in near[:-1]:
+        weight_sum.move()
+        if weight_sum.at < near[-1]:
+            weight_sum.add()
+    if not parts:
+        acts, rows, _ = fence((acts, rows, near_more))
+        parts = expert_grads(acts, rows, ff)
+    far_got, output_sum.value, parts, small_sum, got_x, got_y, more = fence(
+        (far_got, output_sum.value, parts, small_sum, got_x, got_y, more)
     )
     output_sum.add()
     output_sum = output_sum.rest()
@@ -1677,17 +1708,12 @@
         axis=1,
     )
     by_y, by_x = swap_y(to_y), swap_x(to_x)
-    weight_sum = Total(blocks)
-    for _ in near[:-1]:
-        weight_sum.move()
-        if weight_sum.at < near[-1]:
-            weight_sum.add()
+    if len(near) > 1:
+        weight_sum.add()
+    weight_sum.move()
     small_sum = fold(small_sum)
-    if not parts:
-        acts, rows, _ = fence((acts, rows, to_y))
-        parts = expert_grads(acts, rows, ff)
-    by_y, by_x, weight_sum.value, small_sum, parts, got_x, got_y, more = fence(
-        (by_y, by_x, weight_sum.value, small_sum, parts, got_x, got_y, more)
+    by_y, by_x, weight_sum.value, small_sum, parts = fence(
+        (by_y, by_x, weight_sum.value, small_sum, parts)
     )
     expert_grad = finish(*parts, got_x, got_y, more)
     far_more = (by_y[:, :side], by_x[:, :side])
@@ -1695,12 +1721,11 @@
     got_out_y = unpack(by_y[:, side:], 2 * unit)
     out_more_y = plus(out_low[2 * unit : 3 * unit], got_out_x[unit:]).astype(bf16)
     out_more_x = plus(out_high[unit : 2 * unit], got_out_y[unit:]).astype(bf16)
-    if len(near) > 1:
-        weight_sum.add()
-    weight_sum.move()
     out_more_y, out_more_x = swap_y(out_more_y), swap_x(out_more_x)
     small_sum = fold(small_sum)
     weight_sum.blocks.update(step_three(far, *far_got, *far_more))
+    weight_sum.add()
+    weight_sum.move()
     weight_sum.value, out_more_y, out_more_x, small_sum, expert_grad = fence(
         (weight_sum.value, out_more_y, out_more_x, small_sum, expert_grad)
     )

time: 864 us -> 858 us (level)
    ppermute x21, waiting for transfers between devices: 41.1 us -> 51.7 us  [ring(): lax.ppermute(v, 'expert', [(i, (i + 2) % owners) for i in range(owners)])]
  transfers between devices with their start and end apart: 102 -> 102, of which waited for: 40 -> 44; matrix products, arithmetic and copies ran while one was open for 20% -> 20% of each run, Pallas kernels for 36% -> 37%
where the time goes in v3:
time: 858 us; the launch traced here: 846 us
  Pallas kernels  313 us (36%)
  waiting for transfers between devices  246 us (29%)
  local copies, waits for them, and re-layouts  117 us (14%)
  other arithmetic  89.2 us (10%)
  starting transfers between devices  73.1 us (9%)
    ppermute x81, waiting for transfers between devices, swap(): return lax.ppermute(v, axis, [(i, i ^ bit) for i in range(size)])  194 us
    pallas_call x3, Pallas kernels, experts_spread(): pl.pallas_call(functools.partial(spread_body, cap, ff, nb, shape, kinds,...  76.1 us
    ppermute x81, starting transfers between devices, swap(): return lax.ppermute(v, axis, [(i, i ^ bit) for i in range(size)])  64.6 us
    pallas_call x1, Pallas kernels, experts_first(): pl.pallas_call(functools.partial(first_body, cap, ff, rb, nb, src, team,...  63.6 us
    ppermute x21, waiting for transfers between devices, ring(): lax.ppermute(v, 'expert', [(i, (i + 2) % owners) for i in range(owners)])  51.7 us
    dynamic_update_slice x20, local copies, waits for them, and re-layouts, put(): kept = lax.dynamic_update_slice(kept, v[:, :main], (row, 0))  40.8 us
    pallas_call x1, Pallas kernels, experts_last(): pl.pallas_call(functools.partial(last_body, ff, rb, nb, shape, pieces), o...  30.8 us
    convert_element_type x10, other arithmetic, move(): self.value = ring(self.value.astype(bf16))  29 us
  transfers between devices with their start and end apart: 102, of which 44 were waited for; matrix products, arithmetic and copies ran while one was open for 20% of the time, Pallas kernels for 37%

profile of v3, /device:TPU:0, one launch (start us, length us, event | category | flops | bytes accessed | tf_op | source)
XLA Modules:
  0.0 845.6 jit_solution(13421068047142503461)
XLA Ops:
  58.9 19.3 %collective-permute-done.7 = bf16[64,4224]{1,0:T(8,128)(2,1)} collective-permute-done((bf16[64,4224]{1,0:T(8,128)(2,1)}, bf16[64,4224]{1,0:T(8,128)(2,1)}, u32[]{:S(2)}, u32[]{:S(2)}) %collective-permute-start.7) | collective-permute-done | bytes 540704 | tf_op jit(solution)/shard_map/ppermute | solution.py:1247
  102.0 13.0 %collective-permute-done.12 = bf16[64,4224]{1,0:T(8,128)(2,1)} collective-permute-done((bf16[64,4224]{1,0:T(8,128)(2,1)}, bf16[64,4224]{1,0:T(8,128)(2,1)}, u32[]{:S(2)}, u32[]{:S(2)}) %collective-permute-start.12) | collective-permute-done | bytes 540704 | tf_op jit(solution)/shard_map/ppermute | solution.py:1247
  138.8 10.7 %collective-permute-done.16 = bf16[64,4224]{1,0:T(8,128)(2,1)} collective-permute-done((bf16[64,4224]{1,0:T(8,128)(2,1)}, bf16[64,4224]{1,0:T(8,128)(2,1)}, u32[]{:S(2)}, u32[]{:S(2)}) %collective-permute-start.16) | collective-permute-done | bytes 540704 | tf_op jit(solution)/shard_map/ppermute | solution.py:1247
  176.0 9.4 %shard_map.269 = (bf16[256,2048]{1,0:T(8,128)(2,1)}, f32[256,6144]{1,0:T(8,128)}, f32[256,1]{1,0:T(8,128)}, f32[256,1]{1,0:T(8,128)}) custom-call(bf16[256,2048]{1,0:T(8,128)(2,1)} %x_ref.1, f32[1,2048]{1,0:T(1,128)} %get-tuple-element.800.refs_1_.gain_ref, bf16[2048,4096]{1,0:T(8,128)(2,1)} %slice_dynamic-update-slice_fusion.12.refs_2_.wm_ref), custom_call_target="tpu_custom_call" | custom-call | tf_op jit(solution)/shard_map/pallas_call | solution.py:662
  187.0 11.0 %collective-permute-done.22.rest_20_.rest_4_ = bf16[2,256,1024]{2,1,0:T(8,128)(2,1)} collective-permute-done((bf16[2,256,1024]{2,1,0:T(8,128)(2,1)}, bf16[2,256,1024]{2,1,0:T(8,128)(2,1)}, u32[]{:S(2)}, u32[]{:S(2)}) %collective-permute-start.22) | collective-permute-done | bytes 1048608 | tf_op jit(solution)/shard_map/ppermute | solution.py:1247
  198.7 4.5 collective-permute-done.24.rest_12_
  206.9 9.0 %shard_map.270 = (f32[256,6144]{1,0:T(8,128)}, f32[256,1]{1,0:T(8,128)}, f32[256,1]{1,0:T(8,128)}) custom-call(bf16[256,2048]{1,0:T(8,128)(2,1)} %get-tuple-element.442.refs_0_.n_ref, bf16[2048,4096]{1,0:T(8,128)(2,1)} %collective-permute-done.21.refs_1_.wo_ref, f32[256,1]{1,0:T(8,128)} %get-tuple-element.419.refs_2_, ...), custom_call_target="tpu_custom_call", output_to_operand_aliasing={{0}: (4, {})} | custom-call | tf_op jit(solution)/shard_map/pallas_call | solution.py:686
  215.9 9.3 %shard_map.271 = (bf16[256,2048]{1,0:T(8,128)(2,1)}, bf16[256,2048]{1,0:T(8,128)(2,1)}, bf16[256,2048]{1,0:T(8,128)(2,1)}, bf16[256,2048]{1,0:T(8,128)(2,1)}) custom-call(f32[256,6144]{1,0:T(8,128)} %get-tuple-element.422.q_ref.k_ref.v_ref.q_raw.k_raw, f32[256,6144]{1,0:T(8,128)} %get-tuple-element.422.q_ref.k_ref.v_ref.q_raw.k_raw, ...), custom_call_target="tpu_custom_call" | custom-call | tf_op jit(solution)/shard_map/pallas_call | solution.py:744
  225.3 10.1 %shard_map.272 = (f32[256,2048]{1,0:T(8,128)}, bf16[272,2048]{1,0:T(8,128)(2,1)}, f32[16,256]{1,0:T(8,128)}) custom-call(s32[1]{0:T(128)} %bitcast.core_ref, bf16[256,2048]{1,0:T(8,128)(2,1)} %get-tuple-element.577.ctx_ref, bf16[2048,4096]{1,0:T(8,128)(2,1)} %slice_dynamic-update-slice_fusion.12.refs_2_.wm_ref, ...), custom_call_target="tpu_custom_call" | custom-call | tf_op jit(solution)/shard_map/pallas_call | solution.py:827
  235.4 14.6 %collective-permute-done.25.rest_21_.rest_5_ = bf16[2,512,1024]{2,1,0:T(8,128)(2,1)} collective-permute-done((bf16[2,512,1024]{2,1,0:T(8,128)(2,1)S(1)}, bf16[2,512,1024]{2,1,0:T(8,128)(2,1)}, u32[]{:S(2)}, u32[]{:S(2)}) %collective-permute-start.25) | collective-permute-done | bytes 2097184 | tf_op jit(solution)/shard_map/ppermute | solution.py:1247
  255.1 19.2 %collective-permute-done.35.rest_22_.rest_6_ = bf16[2,256,1024]{2,1,0:T(8,128)(2,1)S(1)} collective-permute-done((bf16[2,256,1024]{2,1,0:T(8,128)(2,1)S(1)}, bf16[2,256,1024]{2,1,0:T(8,128)(2,1)S(1)}, u32[]{:S(2)}, u32[]{:S(2)}) %collective-permute-start.35) | collective-permute-done | bytes 1048608 | tf_op jit(solution)/shard_map/ppermute | solution.py:1247
  277.9 19.7 %collective-permute-done.40.rest_23_.rest_7_ = bf16[2,256,1024]{2,1,0:T(8,128)(2,1)S(1)} collective-permute-done((bf16[2,256,1024]{2,1,0:T(8,128)(2,1)S(1)}, bf16[2,256,1024]{2,1,0:T(8,128)(2,1)S(1)}, u32[]{:S(2)}, u32[]{:S(2)}) %collective-permute-start.40) | collective-permute-done | bytes 1048608 | tf_op jit(solution)/shard_map/ppermute | solution.py:1247
  305.1 13.7 %collective-permute-done.45.rest_24_.rest_8_ = bf16[2,256,1024]{2,1,0:T(8,128)(2,1)S(1)} collective-permute-done((bf16[2,256,1024]{2,1,0:T(8,128)(2,1)S(1)}, bf16[2,256,1024]{2,1,0:T(8,128)(2,1)S(1)}, u32[]{:S(2)}, u32[]{:S(2)}) %collective-permute-start.45) | collective-permute-done | bytes 1048608 | tf_op jit(solution)/shard_map/ppermute | solution.py:1247
  318.9 8.6 %collective-permute-done.46.rest_27_.rest_11_ = bf16[2,256,1024]{2,1,0:T(8,128)(2,1)S(1)} collective-permute-done((bf16[2,256,1024]{2,1,0:T(8,128)(2,1)S(1)}, bf16[2,256,1024]{2,1,0:T(8,128)(2,1)S(1)}, u32[]{:S(2)}, u32[]{:S(2)}) %collective-permute-start.46) | collective-permute-done | bytes 1048608 | tf_op jit(solution)/shard_map/ppermute | solution.py:1247
  337.8 63.6 %shard_map.274 = (bf16[2,2,1280,2048]{3,2,1,0:T(8,128)(2,1)}, bf16[2,3,1280,768]{3,2,1,0:T(8,128)(2,1)}, f32[2,1280,1]{2,1,0:T(8,128)}, f32[2,1280,1]{2,1,0:T(8,...) custom-call(bf16[272,2048]{1,0:T(8,128)(2,1)} %get-tuple-element.481, ...), custom_call_target="tpu_custom_call" | custom-call | tf_op jit(solution)/shard_map/pallas_call | solution.py:231
  403.4 30.8 %shard_map.275 = (bf16[2,3,1280,256]{3,2,1,0:T(8,128)(2,1)}, f32[2,1280,1]{2,1,0:T(8,128)}, bf16[2,192,1024]{2,1,0:T(8,128)(2,1)}, bf16[2,320,1024]{2,1,0:T(8,12...) custom-call(bf16[2,2,1280,2048]{3,2,1,0:T(8,128)(2,1)} %get-tuple-el, ...), custom_call_target="tpu_custom_call" | custom-call | tf_op jit(solution)/shard_map/pallas_call | solution.py:398
  436.5 25.3 %shard_map.276 = (bf16[2,272,2048]{2,1,0:T(8,128)(2,1)}, bf16[2,272,2048]{2,1,0:T(8,128)(2,1)}) custom-call(s32[1]{0:T(128)} %bitcast.23.number_ref, bf16[2,3,1280,768]{3,2,1,0:T(8,128)(2,1)} %get-tuple-element.649.ha_ref.h_ref, bf16[2,3,1280,256]{3,2,1,0:T(8,128)(2,1)} %get-tuple-element.537.hd_ref, f32[2,1280,1]{2,1,0:T(8,128)} %get-tuple-element.538.dgr, ...), custom_call_target="tpu_custom_call" | custom-call | tf_op jit(solution)/shard_map/pallas_call | solution.py:553
  461.9 4.5 collective-permute-done.53
  474.6 25.3 %shard_map.277 = (bf16[2,272,2048]{2,1,0:T(8,128)(2,1)}, bf16[2,272,2048]{2,1,0:T(8,128)(2,1)}) custom-call(s32[1]{0:T(128)} %bitcast.23.number_ref, bf16[2,3,1280,768]{3,2,1,0:T(8,128)(2,1)} %get-tuple-element.649.ha_ref.h_ref, bf16[2,3,1280,256]{3,2,1,0:T(8,128)(2,1)} %get-tuple-element.537.hd_ref, f32[2,1280,1]{2,1,0:T(8,128)} %get-tuple-element.538.dgr, ...), custom_call_target="tpu_custom_call" | custom-call | tf_op jit(solution)/shard_map/pallas_call | solution.py:553
  500.0 5.9 collective-permute-done.55.rest_2_
  513.0 25.4 %shard_map.278 = (bf16[4,256,2048]{2,1,0:T(8,128)(2,1)}, bf16[4,256,2048]{2,1,0:T(8,128)(2,1)}) custom-call(s32[1]{0:T(128)} %bitcast.23.number_ref, bf16[2,3,1280,768]{3,2,1,0:T(8,128)(2,1)} %get-tuple-element.649.ha_ref.h_ref, bf16[2,3,1280,256]{3,2,1,0:T(8,128)(2,1)} %get-tuple-element.537.hd_ref, f32[2,1280,1]{2,1,0:T(8,128)} %get-tuple-element.538.dgr, ...), custom_call_target="tpu_custom_call" | custom-call | tf_op jit(solution)/shard_map/pallas_call | solution.py:553
  555.2 12.1 %collective-permute-done.64 = bf16[2,256,1024]{2,1,0:T(8,128)(2,1)S(1)} collective-permute-done((bf16[2,256,1024]{2,1,0:T(8,128)(2,1)S(1)}, bf16[2,256,1024]{2,1,0:T(8,128)(2,1)S(1)}, u32[]{:S(2)}, u32[]{:S(2)}) %collective-permute-start.64) | collective-permute-done | bytes 1048608 | tf_op jit(solution)/shard_map/ppermute | solution.py:1247
  568.1 6.6 collective-permute-done.63
  583.1 12.1 %shard_map.279 = (f32[256,2048]{1,0:T(8,128)}, bf16[256,1024]{1,0:T(8,128)(2,1)}, bf16[256,1024]{1,0:T(8,128)(2,1)}, bf16[256,2048]{1,0:T(8,128)(2,1)}, f32[1,20...) custom-call(s32[1]{0:T(128)} %bitcast.core_ref, f32[272,2048]{1,0:T(8,128)} %bitcast_add_fusion.sum_ref, ...), custom_call_target="tpu_custom_call" | custom-call | tf_op jit(solution)/shard_map/pallas_call | solution.py:896
  610.5 21.6 %shard_map.280 = (bf16[3,256,1024]{2,1,0:T(8,128)(2,1)}, bf16[3,256,1024]{2,1,0:T(8,128)(2,1)}, f32[1,2048]{1,0:T(1,128)}, f32[1,2048]{1,0:T(1,128)}) custom-call(bf16[256,2048]{1,0:T(8,128)(2,1)} %get-tuple-element.596.q_ref, bf16[256,2048]{1,0:T(8,128)(2,1)} %get-tuple-element.597.k_ref, bf16[256,2048]{1,0:T(8,128)(2,1)} %get-tuple-element.598.v_ref, ...), custom_call_target="tpu_custom_call" | custom-call | tf_op jit(solution)/shard_map/pallas_call | solution.py:1003
  646.6 13.7 %shard_map.281 = (bf16[2048,1536]{1,0:T(8,128)(2,1)}, bf16[2048,1536]{1,0:T(8,128)(2,1)}) custom-call(bf16[256,2048]{1,0:T(8,128)(2,1)} %get-tuple-element.442.refs_0_.n_ref, bf16[256,2048]{1,0:T(8,128)(2,1)} %collective-permute-done.68.no_ref, bf16[3,256,1024]{2,1,0:T(8,128)(2,1)} %get-tuple-element.625.u_ref.um_ref, bf16[3,256,1024]{2,1,0:T(8,128)(2,1)} %copy-done.44), custom_call_target="tpu_custom_call" | custom-call | tf_op jit(solution)/shard_map/pallas_call | solution.py:1060
  678.8 16.9 %shard_map.282 = (f32[256,2048]{1,0:T(8,128)}, f32[1,2048]{1,0:T(1,128)}) custom-call(bf16[3,256,1024]{2,1,0:T(8,128)(2,1)} %get-tuple-element.625.u_ref.um_ref, bf16[3,256,1024]{2,1,0:T(8,128)(2,1)} %get-tuple-element.626.uo_ref, bf16[2048,4096]{1,0:T(8,128)(2,1)} %slice_dynamic-update-slice_fusion.12.refs_2_.wm_ref, ...), custom_call_target="tpu_custom_call" | custom-call | tf_op jit(solution)/shard_map/pallas_call | solution.py:1114
  719.2 12.7 %collective-permute-done.85 = bf16[256,1536]{1,0:T(8,128)(2,1)} collective-permute-done((bf16[256,1536]{1,0:T(8,128)(2,1)S(1)}, bf16[256,1536]{1,0:T(8,128)(2,1)}, u32[]{:S(2)}, u32[]{:S(2)}) %collective-permute-start.85) | collective-permute-done | bytes 786464 | tf_op jit(solution)/shard_map/ppermute | solution.py:1247
  742.8 15.3 %shard_map.283 = (bf16[2,768,1024]{2,1,0:T(8,128)(2,1)}, bf16[2,768,1024]{2,1,0:T(8,128)(2,1)}) custom-call(bf16[2,3,1280,768]{3,2,1,0:T(8,128)(2,1)} %get-tuple-element.649.ha_ref.h_ref, bf16[2,2,1280,2048]{3,2,1,0:T(8,128)(2,1)} %get-tuple-element.650.rg_ref), custom_call_target="tpu_custom_call" | custom-call | tf_op jit(solution)/shard_map/pallas_call | solution.py:597
  763.5 19.5 %collective-permute-done.88 = bf16[512,1024]{1,0:T(8,128)(2,1)} collective-permute-done((bf16[512,1024]{1,0:T(8,128)(2,1)}, bf16[512,1024]{1,0:T(8,128)(2,1)}, u32[]{:S(2)}, u32[]{:S(2)}) %collective-permute-start.88) | collective-permute-done | bytes 1048608 | tf_op jit(solution)/shard_map/ppermute | solution.py:1259
  797.5 8.2 collective-permute-done.90
  818.4 14.0 %shard_map.284 = (f32[2,2048,256]{2,1,0:T(8,128)}, f32[2,2048,256]{2,1,0:T(8,128)}, f32[2,256,2048]{2,1,0:T(8,128)}) custom-call(bf16[2,768,1024]{2,1,0:T(8,128)(2,1)} %get-tuple-element.678.low, bf16[2,768,1024]{2,1,0:T(8,128)(2,1)} %get-tuple-element.679.high, bf16[2,320,1024]{2,1,0:T(8,128)(2,1)} %collective-permute-done.49.rest_0_, ...), custom_call_target="tpu_custom_call" | custom-call | tf_op jit(solution)/shard_map/pallas_call | solution.py:1188
  (531 shorter events, 337.0 us)
Async XLA Ops:
  41.5 36.7 %collective-permute-start.4 = (bf16[128,4224]{1,0:T(8,128)(2,1)}, bf16[128,4224]{1,0:T(8,128)(2,1)}, u32[]{:S(2)}, u32[]{:S(2)}) collective-permute-start(bf16[128,4224]{1,0:T(8,128)(2,1)} %collective-permute-done.3), channel_id=1, source_target_pairs={{0,8},{8,0},{16,24},{24,16},{1,9},{9,1},{17,25},{25,17},{2,10},{10... | collective-permute-start | bytes 3244040 | tf_op jit(solution)/shard_map/ppermute | solution.py:1247
  42.0 36.2 %collective-permute-start.5 = (bf16[128,4224]{1,0:T(8,128)(2,1)}, bf16[128,4224]{1,0:T(8,128)(2,1)}, u32[]{:S(2)}, u32[]{:S(2)}) collective-permute-start(bf16[128,4224]{1,0:T(8,128)(2,1)} %collective-permute-done.3), channel_id=1, source_target_pairs={{0,16},{8,24},{16,0},{24,8},{1,17},{9,25},{17,1},{25,9},{2,18},{10... | collective-permute-start | bytes 3244040 | tf_op jit(solution)/shard_map/ppermute | solution.py:1247
  42.5 35.7 %collective-permute-start.6 = (bf16[128,4224]{1,0:T(8,128)(2,1)}, bf16[128,4224]{1,0:T(8,128)(2,1)}, u32[]{:S(2)}, u32[]{:S(2)}) collective-permute-start(bf16[128,4224]{1,0:T(8,128)(2,1)} %collective-permute-done.3), channel_id=1, source_target_pairs={{0,2},{1,3},{2,4},{3,5},{4,6},{5,7},{6,0},{7,1},{8,10},{9,11},{10,... | collective-permute-start | bytes 3244040 | tf_op jit(solution)/shard_map/ppermute | solution.py:1259
  44.7 33.4 %collective-permute-start.7 = (bf16[64,4224]{1,0:T(8,128)(2,1)}, bf16[64,4224]{1,0:T(8,128)(2,1)}, u32[]{:S(2)}, u32[]{:S(2)}) collective-permute-start(bf16[64,4224]{1,0:T(8,128)(2,1)} %get-tuple-element.363), channel_id=1, source_target_pairs={{0,16},{8,24},{16,0},{24,8},{1,17},{9,25},{17,1},{25,9},{2,18},{10... | collective-permute-start | bytes 1622024 | tf_op jit(solution)/shard_map/ppermute | solution.py:1247
  46.3 31.9 %collective-permute-start.8 = (bf16[64,4224]{1,0:T(8,128)(2,1)}, bf16[64,4224]{1,0:T(8,128)(2,1)}, u32[]{:S(2)}, u32[]{:S(2)}) collective-permute-start(bf16[64,4224]{1,0:T(8,128)(2,1)} %get-tuple-element.364), channel_id=1, source_target_pairs={{0,8},{8,0},{16,24},{24,16},{1,9},{9,1},{17,25},{25,17},{2,10},{10... | collective-permute-start | bytes 1622024 | tf_op jit(solution)/shard_map/ppermute | solution.py:1247
  78.2 36.8 %collective-permute-start.9 = (bf16[128,4224]{1,0:T(8,128)(2,1)}, bf16[128,4224]{1,0:T(8,128)(2,1)}, u32[]{:S(2)}, u32[]{:S(2)}) collective-permute-start(bf16[128,4224]{1,0:T(8,128)(2,1)} %collective-permute-done.6), channel_id=1, source_target_pairs={{0,8},{8,0},{16,24},{24,16},{1,9},{9,1},{17,25},{25,17},{2,10},{10... | collective-permute-start | bytes 3244040 | tf_op jit(solution)/shard_map/ppermute | solution.py:1247
  79.8 35.3 %collective-permute-start.10 = (bf16[128,4224]{1,0:T(8,128)(2,1)}, bf16[128,4224]{1,0:T(8,128)(2,1)}, u32[]{:S(2)}, u32[]{:S(2)}) collective-permute-start(bf16[128,4224]{1,0:T(8,128)(2,1)} %collective-permute-done.6), channel_id=1, source_target_pairs={{0,16},{8,24},{16,0},{24,8},{1,17},{9,25},{17,1},{25,9},{2,18},{10... | collective-permute-start | bytes 3244040 | tf_op jit(solution)/shard_map/ppermute | solution.py:1247
  80.3 34.8 %collective-permute-start.11 = (bf16[128,4224]{1,0:T(8,128)(2,1)}, bf16[128,4224]{1,0:T(8,128)(2,1)}, u32[]{:S(2)}, u32[]{:S(2)}) collective-permute-start(bf16[128,4224]{1,0:T(8,128)(2,1)} %collective-permute-done.6), channel_id=1, source_target_pairs={{0,2},{1,3},{2,4},{3,5},{4,6},{5,7},{6,0},{7,1},{8,10},{9,11},{10,... | collective-permute-start | bytes 3244040 | tf_op jit(solution)/shard_map/ppermute | solution.py:1259
  82.5 32.5 %collective-permute-start.12 = (bf16[64,4224]{1,0:T(8,128)(2,1)}, bf16[64,4224]{1,0:T(8,128)(2,1)}, u32[]{:S(2)}, u32[]{:S(2)}) collective-permute-start(bf16[64,4224]{1,0:T(8,128)(2,1)} %get-tuple-element.371), channel_id=1, source_target_pairs={{0,16},{8,24},{16,0},{24,8},{1,17},{9,25},{17,1},{25,9},{2,18},{10... | collective-permute-start | bytes 1622024 | tf_op jit(solution)/shard_map/ppermute | solution.py:1247
  115.0 34.5 %collective-permute-start.14 = (bf16[128,4224]{1,0:T(8,128)(2,1)}, bf16[128,4224]{1,0:T(8,128)(2,1)}, u32[]{:S(2)}, u32[]{:S(2)}) collective-permute-start(bf16[128,4224]{1,0:T(8,128)(2,1)} %collective-permute-done.11), channel_id=1, source_target_pairs={{0,8},{8,0},{16,24},{24,16},{1,9},{9,1},{17,25},{25,17},{2,10},{10... | collective-permute-start | bytes 3244040 | tf_op jit(solution)/shard_map/ppermute | solution.py:1247
  115.4 34.1 %collective-permute-start.15 = (bf16[128,4224]{1,0:T(8,128)(2,1)}, bf16[128,4224]{1,0:T(8,128)(2,1)}, u32[]{:S(2)}, u32[]{:S(2)}) collective-permute-start(bf16[128,4224]{1,0:T(8,128)(2,1)} %collective-permute-done.11), channel_id=1, source_target_pairs={{0,16},{8,24},{16,0},{24,8},{1,17},{9,25},{17,1},{25,9},{2,18},{10... | collective-permute-start | bytes 3244040 | tf_op jit(solution)/shard_map/ppermute | solution.py:1247
  170.1 33.1 %collective-permute-start.21 = (bf16[2048,4096]{1,0:T(8,128)(2,1)}, bf16[2048,4096]{1,0:T(8,128)(2,1)}, u32[]{:S(2)}, u32[]{:S(2)}) collective-permute-start(bf16[2048,4096]{1,0:T(8,128)(2,1)} %slice_dynamic-update-slice_fusion.12.refs_2_.wm_ref), channel_id=1, source_target_pairs={{0,1},{1,0},{2,3},{3,2},{4,5},{5,4},{6,7},{7,6},{8,9},{9,8},{10,11... | collective-permute-start | bytes 50331656 | tf_op jit(solution)/shard_map/ppermute | solution.py:1247
  203.2 46.7 %collective-permute-start.25 = (bf16[2,512,1024]{2,1,0:T(8,128)(2,1)S(1)}, bf16[2,512,1024]{2,1,0:T(8,128)(2,1)}, u32[]{:S(2)}, u32[]{:S(2)}) collective-permute-start(bf16[2,512,1024]{2,1,0:T(8,128)(2,1)S(1)} %pad_maximum_fusion.rest_17_.rest_1_), channel_id=1, source_target_pairs={{0,8},{8,0},{16,24},{24,16},{1,9},{9,1},{17,25},{25,17},{2,10},{10... | collective-permute-start | bytes 6291464 | tf_op jit(solution)/shard_map/ppermute | solution.py:1247
  204.2 46.7 %collective-permute-start.26 = (bf16[2,512,1024]{2,1,0:T(8,128)(2,1)}, bf16[2,512,1024]{2,1,0:T(8,128)(2,1)}, u32[]{:S(2)}, u32[]{:S(2)}) collective-permute-start(bf16[2,512,1024]{2,1,0:T(8,128)(2,1)} %pad_maximum_fusion.1.rest_19_.rest_3_), channel_id=1, source_target_pairs={{0,16},{8,24},{16,0},{24,8},{1,17},{9,25},{17,1},{25,9},{2,18},{10... | collective-permute-start | bytes 6291464 | tf_op jit(solution)/shard_map/ppermute | solution.py:1247
  327.5 73.9 %collective-permute-start.29 = (bf16[2,512,1024]{2,1,0:T(8,128)(2,1)}, bf16[2,512,1024]{2,1,0:T(8,128)(2,1)S(1)}, u32[]{:S(2)}, u32[]{:S(2)}) collective-permute-start(bf16[2,512,1024]{2,1,0:T(8,128)(2,1)} %collective-permute-done.25.rest_21_.rest_5_), channel_id=1, source_target_pairs={{0,16},{8,24},{16,0},{24,8},{1,17},{9,25},{17,1},{25,9},{2,18},{10... | collective-permute-start | bytes 6291464 | tf_op jit(solution)/shard_map/ppermute | solution.py:1247
  328.2 73.3 %collective-permute-start.31 = (bf16[2,512,1024]{2,1,0:T(8,128)(2,1)}, bf16[2,512,1024]{2,1,0:T(8,128)(2,1)}, u32[]{:S(2)}, u32[]{:S(2)}) collective-permute-start(bf16[2,512,1024]{2,1,0:T(8,128)(2,1)} %collective-permute-done.26.rest_29_.rest_13_), channel_id=1, source_target_pairs={{0,8},{8,0},{16,24},{24,16},{1,9},{9,1},{17,25},{25,17},{2,10},{10... | collective-permute-start | bytes 6291464 | tf_op jit(solution)/shard_map/ppermute | solution.py:1247
  331.8 69.6 %collective-permute-start.28 = (bf16[2,256,1024]{2,1,0:T(8,128)(2,1)}, bf16[2,256,1024]{2,1,0:T(8,128)(2,1)S(1)}, u32[]{:S(2)}, u32[]{:S(2)}) collective-permute-start(bf16[2,256,1024]{2,1,0:T(8,128)(2,1)} %collective-permute-done.22.rest_20_.rest_4_), channel_id=1, source_target_pairs={{0,16},{8,24},{16,0},{24,8},{1,17},{9,25},{17,1},{25,9},{2,18},{10... | collective-permute-start | bytes 3145736 | tf_op jit(solution)/shard_map/ppermute | solution.py:1247
  334.3 67.1 %collective-permute-start.30 = (bf16[2,256,1024]{2,1,0:T(8,128)(2,1)}, bf16[2,256,1024]{2,1,0:T(8,128)(2,1)}, u32[]{:S(2)}, u32[]{:S(2)}) collective-permute-start(bf16[2,256,1024]{2,1,0:T(8,128)(2,1)} %collective-permute-done.23.rest_28_.rest_12_), channel_id=1, source_target_pairs={{0,8},{8,0},{16,24},{24,16},{1,9},{9,1},{17,25},{25,17},{2,10},{10... | collective-permute-start | bytes 3145736 | tf_op jit(solution)/shard_map/ppermute | solution.py:1247
  401.5 32.8 %collective-permute-start.49 = (bf16[2,320,1024]{2,1,0:T(8,128)(2,1)}, bf16[2,320,1024]{2,1,0:T(8,128)(2,1)}, u32[]{:S(2)}, u32[]{:S(2)}) collective-permute-start(bf16[2,320,1024]{2,1,0:T(8,128)(2,1)} %get-tuple-element.531), channel_id=1, source_target_pairs={{0,8},{8,0},{16,24},{24,16},{1,9},{9,1},{17,25},{25,17},{2,10},{10... | collective-permute-start | bytes 3932168 | tf_op jit(solution)/shard_map/ppermute | solution.py:1247
  470.5 36.1 %collective-permute-start.54 = (bf16[272,2048]{1,0:T(8,128)(2,1)}, bf16[272,2048]{1,0:T(8,128)(2,1)S(1)}, u32[]{:S(2)}, u32[]{:S(2)}) collective-permute-start(bf16[272,2048]{1,0:T(8,128)(2,1)} %fusion.17), channel_id=1, source_target_pairs={{0,2},{1,3},{2,4},{3,5},{4,6},{5,7},{6,0},{7,1},{8,10},{9,11},{10,... | collective-permute-start | bytes 3342344 | tf_op jit(solution)/shard_map/ppermute | solution.py:1259
  472.4 33.5 %collective-permute-start.55 = (bf16[2,176,1024]{2,1,0:T(8,128)(2,1)}, bf16[2,176,1024]{2,1,0:T(8,128)(2,1)}, u32[]{:S(2)}, u32[]{:S(2)}) collective-permute-start(bf16[2,176,1024]{2,1,0:T(8,128)(2,1)} %get-tuple-element.554), channel_id=1, source_target_pairs={{0,8},{8,0},{16,24},{24,16},{1,9},{9,1},{17,25},{25,17},{2,10},{10... | collective-permute-start | bytes 2162696 | tf_op jit(solution)/shard_map/ppermute | solution.py:1247
  473.4 33.2 %collective-permute-start.56 = (bf16[2,176,1024]{2,1,0:T(8,128)(2,1)}, bf16[2,176,1024]{2,1,0:T(8,128)(2,1)}, u32[]{:S(2)}, u32[]{:S(2)}) collective-permute-start(bf16[2,176,1024]{2,1,0:T(8,128)(2,1)} %get-tuple-element.557), channel_id=1, source_target_pairs={{0,16},{8,24},{16,0},{24,8},{1,17},{9,25},{17,1},{25,9},{2,18},{10... | collective-permute-start | bytes 2162696 | tf_op jit(solution)/shard_map/ppermute | solution.py:1247
  507.6 34.0 %collective-permute-start.60 = (bf16[2,272,2048]{2,1,0:T(8,128)(2,1)}, bf16[2,272,2048]{2,1,0:T(8,128)(2,1)}, u32[]{:S(2)}, u32[]{:S(2)}) collective-permute-start(bf16[2,272,2048]{2,1,0:T(8,128)(2,1)} %get-tuple-element.561), channel_id=1, source_target_pairs={{0,1},{1,0},{2,3},{3,2},{4,5},{5,4},{6,7},{7,6},{8,9},{9,8},{10,11... | collective-permute-start | bytes 6684680 | tf_op jit(solution)/shard_map/ppermute | solution.py:1247
  541.6 33.1 %collective-permute-start.66 = (bf16[4,256,2048]{2,1,0:T(8,128)(2,1)}, bf16[4,256,2048]{2,1,0:T(8,128)(2,1)S(1)}, u32[]{:S(2)}, u32[]{:S(2)}) collective-permute-start(bf16[4,256,2048]{2,1,0:T(8,128)(2,1)} %get-tuple-element.578), channel_id=1, source_target_pairs={{0,1},{1,0},{2,3},{3,2},{4,5},{5,4},{6,7},{7,6},{8,9},{9,8},{10,11... | collective-permute-start | bytes 12582920 | tf_op jit(solution)/shard_map/ppermute | solution.py:1247
  541.6 59.0 %collective-permute-start.68 = (bf16[256,2048]{1,0:T(8,128)(2,1)}, bf16[256,2048]{1,0:T(8,128)(2,1)}, u32[]{:S(2)}, u32[]{:S(2)}) collective-permute-start(bf16[256,2048]{1,0:T(8,128)(2,1)} %get-tuple-element.442.refs_0_.n_ref), channel_id=1, source_target_pairs={{0,1},{1,0},{2,3},{3,2},{4,5},{5,4},{6,7},{7,6},{8,9},{9,8},{10,11... | collective-permute-start | bytes 3145736 | tf_op jit(solution)/shard_map/ppermute | solution.py:1247
  645.4 58.9 %collective-permute-start.82 = (bf16[256,2048]{1,0:T(8,128)(2,1)}, bf16[256,2048]{1,0:T(8,128)(2,1)}, u32[]{:S(2)}, u32[]{:S(2)}) collective-permute-start(bf16[256,2048]{1,0:T(8,128)(2,1)} %fusion.7), channel_id=1, source_target_pairs={{0,2},{1,3},{2,4},{3,5},{4,6},{5,7},{6,0},{7,1},{8,10},{9,11},{10,... | collective-permute-start | bytes 3145736 | tf_op jit(solution)/shard_map/ppermute | solution.py:1259
  665.9 38.5 %collective-permute-start.79 = (bf16[512,1536]{1,0:T(8,128)(2,1)}, bf16[512,1536]{1,0:T(8,128)(2,1)}, u32[]{:S(2)}, u32[]{:S(2)}) collective-permute-start(bf16[512,1536]{1,0:T(8,128)(2,1)} %pad_maximum_fusion.5), channel_id=1, source_target_pairs={{0,8},{8,0},{16,24},{24,16},{1,9},{9,1},{17,25},{25,17},{2,10},{10... | collective-permute-start | bytes 4718600 | tf_op jit(solution)/shard_map/ppermute | solution.py:1247
  667.0 37.4 %collective-permute-start.80 = (bf16[512,1536]{1,0:T(8,128)(2,1)}, bf16[512,1536]{1,0:T(8,128)(2,1)}, u32[]{:S(2)}, u32[]{:S(2)}) collective-permute-start(bf16[512,1536]{1,0:T(8,128)(2,1)} %pad_maximum_fusion.6), channel_id=1, source_target_pairs={{0,16},{8,24},{16,0},{24,8},{1,17},{9,25},{17,1},{25,9},{2,18},{10... | collective-permute-start | bytes 4718600 | tf_op jit(solution)/shard_map/ppermute | solution.py:1247
  716.3 47.2 %collective-permute-start.83 = (bf16[512,1536]{1,0:T(8,128)(2,1)}, bf16[512,1536]{1,0:T(8,128)(2,1)}, u32[]{:S(2)}, u32[]{:S(2)}) collective-permute-start(bf16[512,1536]{1,0:T(8,128)(2,1)} %pad_maximum_fusion.7), channel_id=1, source_target_pairs={{0,8},{8,0},{16,24},{24,16},{1,9},{9,1},{17,25},{25,17},{2,10},{10... | collective-permute-start | bytes 4718600 | tf_op jit(solution)/shard_map/ppermute | solution.py:1247
  717.6 45.9 %collective-permute-start.84 = (bf16[512,1536]{1,0:T(8,128)(2,1)}, bf16[512,1536]{1,0:T(8,128)(2,1)}, u32[]{:S(2)}, u32[]{:S(2)}) collective-permute-start(bf16[512,1536]{1,0:T(8,128)(2,1)} %pad_maximum_fusion.8), channel_id=1, source_target_pairs={{0,16},{8,24},{16,0},{24,8},{1,17},{9,25},{17,1},{25,9},{2,18},{10... | collective-permute-start | bytes 4718600 | tf_op jit(solution)/shard_map/ppermute | solution.py:1247
  741.9 41.1 %collective-permute-start.88 = (bf16[512,1024]{1,0:T(8,128)(2,1)}, bf16[512,1024]{1,0:T(8,128)(2,1)}, u32[]{:S(2)}, u32[]{:S(2)}) collective-permute-start(bf16[512,1024]{1,0:T(8,128)(2,1)} %add_convert_fusion.2), channel_id=1, source_target_pairs={{0,2},{1,3},{2,4},{3,5},{4,6},{5,7},{6,0},{7,1},{8,10},{9,11},{10,... | collective-permute-start | bytes 3145736 | tf_op jit(solution)/shard_map/ppermute | solution.py:1259
  762.7 34.8 %collective-permute-start.93 = (bf16[128,3072]{1,0:T(8,128)(2,1)}, bf16[128,3072]{1,0:T(8,128)(2,1)}, u32[]{:S(2)}, u32[]{:S(2)}) collective-permute-start(bf16[128,3072]{1,0:T(8,128)(2,1)} %fusion.16), channel_id=1, source_target_pairs={{0,2},{1,3},{2,4},{3,5},{4,6},{5,7},{6,0},{7,1},{8,10},{9,11},{10,... | collective-permute-start | bytes 2359304 | tf_op jit(solution)/shard_map/ppermute | solution.py:1259
  (154 other events, 3073.7 us)
